TPU v7x, 768 devices: a whole 4x8x12 slice. The times are simulated.
768 devices in a mesh: inter: 128 (over z_hi, x, y), intra: 6 (over z_lo, core).
Axes of the slice: x: 4, y: 8, z: 12 (z_hi: 4, z_lo: 3; z = z_hi * 3 + z_lo), core: 2. Of those that a mesh axis runs over, the one named last changes fastest.
Arguments:
- grad_out: bfloat16 [393216, 1536], P(('inter', 'intra')), may hold values from -24 to 24
- context: bfloat16 [393216, 768], P(('inter', 'intra')), may hold values from -6 to 6
- codes: bfloat16 [6, 256, 768], P('intra'), may hold values from -127 to 127, as said below
- scales: bfloat16 [6, 768], P('intra'), may hold values from 9.9658966e-05 to 0.0009994507
Outputs:
- ctx_grad: bfloat16 [393216, 768], P(('inter', 'intra'))
- weight_grad: float32 [1536, 768], P(('inter', 'intra'))
- bias_grad: float32 [1536], P(('inter', 'intra'))
Inputs may be any that keep to these rules, and one draw needn't show every extreme that they name: codes are whole numbers.
All inputs are finite; a program needn't handle non-finite values.
Results may differ from a plain program's by a relative error of at most 0.0049.
Values may be sent and summed in bfloat16 or wider, within the bound.
No kernel may reach another device: no remote copies, remote signals or barrier semaphores. Data moves between devices by JAX's collectives and lax.ppermute only.
A program may use at most 64 MiB of HBM per device.

v0:
```python
import jax
import jax.numpy as jnp
from jax import lax
from jax.sharding import PartitionSpec as P


def dequantize(piece_codes, piece_scales):
    block_size = piece_codes.shape[1]
    values = piece_codes.astype(jnp.float32) * piece_scales[:, None, :].astype(jnp.float32)
    return values.astype(jnp.bfloat16).reshape(
        piece_codes.shape[0] * block_size, piece_codes.shape[2]
    )


def body(grad_out, context, codes, scales):
    model_width = grad_out.shape[1]
    all_codes, all_scales = (
        lax.all_gather(codes, "intra", axis=0, tiled=True),
        lax.all_gather(scales, "intra", axis=0, tiled=True),
    )
    weight = dequantize(all_codes, all_scales)
    ctx_wide = jnp.dot(grad_out, weight, preferred_element_type=jnp.float32)
    ctx_grad = ctx_wide.astype(jnp.bfloat16)
    node_size = lax.axis_size("intra")
    node_count = lax.axis_size("inter")
    average = 1.0 / (node_size * node_count)
    local_term = (
        jnp.einsum("td,th->dh", grad_out, context, preferred_element_type=jnp.float32) * average
    )
    local_bias = jnp.sum(grad_out, axis=0, dtype=jnp.float32) * average
    row_share = model_width // (node_size * node_count)
    term_split = local_term.reshape(node_count, node_size, row_share, local_term.shape[1])
    bias_split = local_bias.reshape(node_count, node_size, row_share)
    node_term, node_bias = (
        lax.psum_scatter(term_split, "intra", scatter_dimension=1, tiled=True),
        lax.psum_scatter(bias_split, "intra", scatter_dimension=1, tiled=True),
    )
    owned_term, owned_bias = (
        lax.psum_scatter(node_term, "inter", scatter_dimension=0, tiled=True),
        lax.psum_scatter(node_bias, "inter", scatter_dimension=0, tiled=True),
    )
    weight_grad = owned_term.reshape(row_share, local_term.shape[1])
    bias_grad = owned_bias.reshape(row_share)
    return (ctx_grad, weight_grad, bias_grad)


def solution(mesh):
    in_specs = (
        P(("inter", "intra"), None),
        P(("inter", "intra"), None),
        P("intra", None, None),
        P("intra", None),
    )
    out_specs = (P(("inter", "intra"), None), P(("inter", "intra"), None), P(("inter", "intra")))
    return jax.shard_map(body, mesh=mesh, in_specs=in_specs, out_specs=out_specs, check_vma=False)
```

profile of v0, /device:TPU:128, one launch (start us, length us, event | category | flops | bytes accessed | tf_op | source)
XLA Modules:
  0.0 2361.0 jit_solution(12804078252601446543)
XLA Ops:
  7.2 1.1 copy-done
  8.3 5.0 convolution_multiply_fusion
  13.3 6.8 reshape.25
  20.0 5.4 copy.9
  25.4 0.0 all-gather.3.cloned.1.call-start
  25.5 0.7 all-gather.3.cloned.1.call-update
  26.2 0.0 all-reduce.5.cloned.1.call-start
  26.2 1.3 dynamic-slice
  27.6 1.3 dynamic-slice.2
  28.8 0.3 convert_reduce_fusion
  29.1 0.2 mul.30
  29.3 0.2 copy.11
  29.5 14.4 all-reduce.1
  43.9 0.7 constant_dynamic-slice_fusion.1
  44.6 0.1 copy.12
  44.7 808.5 %all-reduce.2 = f32[128,1,2]{2,1,0:T(1,128)S(1)} all-reduce(f32[128,1,2]{2,1,0:T(1,128)S(1)} %copy.12), channel_id=5, replica_groups=mesh['inter'=128,'intra'=6] {'inter'}, use_global_device_ids=true, to_apply=%region_4.0.clone | all-reduce | flops 256 | bytes 2048
  853.2 2.6 copy.10
  855.8 1.1 fusion.1
  857.0 10.3 all-gather
  867.2 2.1 multiply_convert_fusion
  869.3 1.4 fusion
  870.8 1.2 copy.13
  871.9 1480.7 %all-reduce.5.cloned.1.call-done = f32[128,1,2,768]{3,2,1,0:T(2,128)} async-done(((f32[128,1,2,768]{3,2,1,0:T(2,128)}), f32[128,1,2,768]{3,2,1,0:T(2,128)}) %all-reduce.5.cloned.1.call-update) | async-done | bytes 786448
  2352.6 1.9 dynamic-slice_bitcast_fusion
  (12 shorter events, 0.1 us)
Async XLA Ops:
  7.2 1.1 copy-start
  7.2 846.0 %reduce-scatter.2.cloned.1.call-start = ((), (), s32[]{:S(2)}) async-start(), calls=%async_computation.2 | async-start | bytes 5505024 | tf_op jit(solution)/shard_map/reduce_scatter | solution.py:35
  25.4 3.4 copy-start.1
  25.4 841.8 %all-gather.3.cloned.1.call-start = ((), (), s32[]{:S(2)}) async-start(), calls=%async_computation.1 | async-start | bytes 2752512 | tf_op jit(solution)/shard_map/all_gather | solution.py:18
  26.2 2326.4 %all-reduce.5.cloned.1.call-start = ((), (), s32[]{:S(2)}) async-start(), calls=%async_computation.3 | async-start | bytes 1572864
  28.8 828.1 %copy-start.2 = (bf16[1,768]{1,0:T(2,128)(2,1)S(1)}, bf16[1,768]{1,0:T(2,128)(2,1)}, u32[]{:S(2)}) copy-start(bf16[1,768]{1,0:T(2,128)(2,1)} %param.7) | copy-start | bytes 4612
Sparse Core Ops, SparseCore 0:
  25.5 67.3 reduce-scatter.1
  95.3 41.7 all-gather.2
  855.9 1496.5 all-reduce.4
where the time goes:
time: 2360 us
  waiting for transfers between devices  1480 us (63%)
  blocking collectives  833 us (35%)
  local copies, waits for them, and re-layouts  23.8 us (1%)
    unnamed x4, waiting for transfers between devices  1480 us
    unnamed x2, blocking collectives  823 us
  transfers between devices with their start and end apart: 3, of which 1 were waited for; matrix products, arithmetic and copies ran while one was open for 1% of the time, Pallas kernels for 0%

commit v1 on v0

v1 whole, which is shorter than its diff:
```python
import functools
import jax
import jax.numpy as jnp
import numpy as np
from jax import lax
from jax.experimental import pallas as pl
from jax.experimental.pallas import tpu as pltpu
from jax.sharding import Mesh, PartitionSpec as P

SIZES = (4, 4, 4, 2, 3, 2)
NAMES = ("zh", "x", "yh", "yl", "zl", "c")
PAD = 128


def row_map(sizes):
    _, x, yh, yl, zl, _ = sizes
    index = np.arange(2 * x * yh * yl * zl * 4).reshape(2, x, yh, yl, zl, 2, 2)[..., :1, :]
    one = np.transpose(index, (5, 6, 1, 3, 0, 2, 4)).reshape(-1)
    return np.concatenate([one, one]).astype(np.int32)[:, None]


def split_pairs(values):
    lane = lax.broadcasted_iota(jnp.int32, (values[0].shape[0], PAD), 1)
    parts = jnp.zeros(lane.shape, jnp.float32)
    for s, value in enumerate(values):
        high = value.astype(jnp.bfloat16).astype(jnp.float32)
        parts = jnp.where(lane == 2 * s, high, parts)
        parts = jnp.where(lane == 2 * s + 1, value - high, parts)
    return parts


def join_pairs(parts):
    lane = lax.broadcasted_iota(jnp.int32, parts.shape, 1)
    return [
        jnp.sum(jnp.where((lane == 2 * s) | (lane == 2 * s + 1), parts, 0.0), axis=1, keepdims=True)
        for s in range(2)
    ]


def term_kernel(map_hbm, grad_hbm, ctx_hbm, codes_hbm, scales_hbm, send_ref, keep_ref, weight_ref, *scratch):
    map_ref, grad_ref, ctx_ref, codes_ref, scales_ref, acc, sems = scratch
    core = lax.axis_index("c")
    span = map_ref.shape[0]
    half = span // 2
    width = ctx_ref.shape[1]
    tokens = ctx_ref.shape[0]
    blocks = send_ref.shape[0]
    part = send_ref.shape[1] // 2

    def columns(step):
        return pl.ds(step * span, span)

    copies = [
        pltpu.make_async_copy(map_hbm, map_ref, sems.at[0]),
        pltpu.make_async_copy(grad_hbm.at[:, columns(0)], grad_ref.at[:, columns(0)], sems.at[1]),
        pltpu.make_async_copy(ctx_hbm, ctx_ref, sems.at[2]),
        pltpu.make_async_copy(grad_hbm.at[:, columns(1)], grad_ref.at[:, columns(1)], sems.at[3]),
        pltpu.make_async_copy(scales_hbm, scales_ref, sems.at[4]),
        pltpu.make_async_copy(codes_hbm, codes_ref, sems.at[5]),
    ]
    for copy in copies:
        copy.start()
    copies[0].wait()
    row = lax.broadcasted_iota(jnp.int32, (span, 1), 0)
    other = jnp.where(row < half, 1 - core, core)
    source = map_ref[...] + 2 * other
    column = lax.broadcasted_iota(jnp.int32, (span, span), 1)
    pick = jnp.where(source == column, 1.0, 0.0).astype(jnp.bfloat16)
    ones = jnp.ones((tokens, PAD), jnp.bfloat16)
    for step in range(2):
        copies[1 + 2 * step].wait()
        moved = lax.dot_general(
            pick,
            grad_ref[:, step * span : (step + 1) * span],
            (((1,), (1,)), ((), ())),
            preferred_element_type=jnp.float32,
        ).astype(jnp.bfloat16)
        if step == 0:
            copies[2].wait()
        acc[step, :, :width] = jnp.dot(moved, ctx_ref[...], preferred_element_type=jnp.float32)
        acc[step, :, width:] = jnp.dot(moved, ones, preferred_element_type=jnp.float32)
    copies[4].wait()
    copies[5].wait()
    scaled = codes_ref[0].astype(jnp.float32) * scales_ref[...].astype(jnp.float32)
    weight_ref[...] = scaled.astype(jnp.bfloat16)
    for side, out in enumerate((send_ref, keep_ref)):
        for block in range(blocks):
            sums = []
            for s in range(2):
                at = ((side * 2 + s) * blocks + block) * part
                rows = jnp.concatenate([acc[0, at : at + part, :], acc[1, at : at + part, :]], axis=0)
                out[block, :, s * width : (s + 1) * width] = rows[:, :width].astype(jnp.bfloat16)
                sums.append(rows[:, width:])
            out[block, :, 2 * width :] = split_pairs(sums).astype(jnp.bfloat16)


def local_terms(sizes, grad_out, context, codes, scales):
    zh, x, yh, yl, zl, _ = sizes
    width = context.shape[1]
    piece = jax.ShapeDtypeStruct((x * yl, zh * yh * zl, 2 * width + PAD), jnp.bfloat16)
    block = jax.ShapeDtypeStruct(codes.shape[1:], jnp.bfloat16)
    rows = row_map(sizes)
    operands = (jnp.asarray(rows), grad_out, context, codes, scales)
    return pl.pallas_call(
        term_kernel,
        out_shape=(piece, piece, block),
        in_specs=[pl.BlockSpec(memory_space=pltpu.HBM)] * 5,
        out_specs=(pl.BlockSpec(memory_space=pltpu.VMEM),) * 3,
        scratch_shapes=[pltpu.VMEM(a.shape, a.dtype) for a in operands]
        + [pltpu.VMEM((2, rows.shape[0], width + PAD), jnp.float32), pltpu.SemaphoreType.DMA((6,))],
        compiler_params=pltpu.CompilerParams(vmem_limit_bytes=60 * 1024 * 1024),
        cost_estimate=pl.CostEstimate(flops=4 * 10**9, bytes_accessed=5 * 10**6, transcendentals=0),
    )(*operands)


def chip_kernel(got_ref, keep_ref, out_ref):
    wide = out_ref.shape[2] - PAD
    for block in range(out_ref.shape[0]):
        total = got_ref[block].astype(jnp.float32) + keep_ref[block].astype(jnp.float32)
        out_ref[block, :, :wide] = total[:, :wide].astype(out_ref.dtype)
        out_ref[block, :, wide:] = split_pairs(join_pairs(total[:, wide:])).astype(out_ref.dtype)


def chip_sum(got, keep):
    whole = pl.BlockSpec(memory_space=pltpu.VMEM)
    return pl.pallas_call(
        chip_kernel,
        out_shape=jax.ShapeDtypeStruct(got.shape, got.dtype),
        in_specs=[whole] * 2,
        out_specs=whole,
        compiler_params=pltpu.CompilerParams(vmem_limit_bytes=16 * 1024 * 1024),
        cost_estimate=pl.CostEstimate(flops=10**6, bytes_accessed=4 * 10**6, transcendentals=0),
    )(got, keep)


def near_kernel(got_ref, *refs):
    held, (sum_ref, own_ref, wide) = refs[:-3], refs[-3:]
    rows = held[0].shape[0]
    for index, block in enumerate(held):
        own_ref[index * rows : (index + 1) * rows, :] = block[...]
    for chunk in range(sum_ref.shape[1]):
        lanes = slice(chunk * PAD, (chunk + 1) * PAD)
        total = got_ref[0, :, lanes].astype(jnp.float32)
        for index in range(1, got_ref.shape[0]):
            total = total + got_ref[index, :, lanes].astype(jnp.float32)
        if chunk == sum_ref.shape[1] - 1:
            total = split_pairs(join_pairs(total))
        wide[:, chunk, :] = total
    sum_ref[...] = wide[...].astype(sum_ref.dtype)


def near_sum(got, held):
    _, rows, lanes = got.shape
    shape = (rows, lanes // PAD, PAD)
    tall = (len(held) * held[0].shape[0], held[0].shape[1])
    whole = pl.BlockSpec(memory_space=pltpu.VMEM)
    return pl.pallas_call(
        near_kernel,
        out_shape=(jax.ShapeDtypeStruct(shape, jnp.bfloat16), jax.ShapeDtypeStruct(tall, jnp.bfloat16)),
        in_specs=[whole] * (1 + len(held)),
        out_specs=(whole, whole),
        scratch_shapes=[pltpu.VMEM(shape, jnp.float32)],
        compiler_params=pltpu.CompilerParams(vmem_limit_bytes=24 * 1024 * 1024),
        cost_estimate=pl.CostEstimate(flops=10**6, bytes_accessed=4 * 10**6, transcendentals=0),
    )(got, *held)


def last_kernel(scale, far_ref, weight_ref, bias_ref):
    total = far_ref[0].astype(jnp.float32)
    for index in range(1, far_ref.shape[0]):
        total = total + far_ref[index].astype(jnp.float32)
    total = total * scale
    chunks = (total.shape[0] - 1) // 2
    for s in range(2):
        for chunk in range(chunks):
            at = s * chunks + chunk
            weight_ref[s : s + 1, chunk * PAD : (chunk + 1) * PAD] = total[at : at + 1, :]
    tail = total[2 * chunks : 2 * chunks + 1, :]
    lane = lax.broadcasted_iota(jnp.int32, (1, PAD), 1)
    for s in range(2):
        bias_ref[s] = jnp.sum(jnp.where((lane == 2 * s) | (lane == 2 * s + 1), tail, 0.0))


def last_sum(far, scale):
    width = (far.shape[1] - 1) // 2 * PAD
    whole = pl.BlockSpec(memory_space=pltpu.VMEM)
    return pl.pallas_call(
        functools.partial(last_kernel, scale),
        out_shape=(jax.ShapeDtypeStruct((2, width), jnp.float32), jax.ShapeDtypeStruct((2,), jnp.float32)),
        in_specs=[whole],
        out_specs=(pl.BlockSpec((2, width), lambda: (0, 0)), pl.BlockSpec(memory_space=pltpu.SMEM)),
        compiler_params=pltpu.CompilerParams(vmem_limit_bytes=16 * 1024 * 1024),
        cost_estimate=pl.CostEstimate(flops=10**5, bytes_accessed=2 * 10**5, transcendentals=0),
    )(far)


def ctx_kernel(chips, grad_ref, own_ref, sibling_ref, out_ref):
    chip, core = lax.axis_index("zl"), lax.axis_index("c")
    rows = own_ref.shape[0] // chips
    total = None
    for back in range(chips):
        owner = lax.rem(chip + chips - back, chips)
        for held, side in ((own_ref, core), (sibling_ref, 1 - core)):
            at = pl.multiple_of((2 * owner + side) * rows, rows)
            product = jnp.dot(
                grad_ref[:, pl.ds(at, rows)],
                held[back * rows : (back + 1) * rows, :],
                preferred_element_type=jnp.float32,
            )
            total = product if total is None else total + product
    out_ref[...] = total.astype(out_ref.dtype)


def ctx_product(chips, grad_out, own, sibling):
    tokens, depth = grad_out.shape
    steps = 2
    whole = pl.BlockSpec(memory_space=pltpu.VMEM)
    return pl.pallas_call(
        functools.partial(ctx_kernel, chips),
        out_shape=jax.ShapeDtypeStruct((tokens, own.shape[1]), jnp.bfloat16),
        grid=(steps,),
        in_specs=[pl.BlockSpec((tokens // steps, depth), lambda i: (i, 0)), whole, whole],
        out_specs=pl.BlockSpec((tokens // steps, own.shape[1]), lambda i: (i, 0)),
        compiler_params=pltpu.CompilerParams(vmem_limit_bytes=24 * 1024 * 1024),
        cost_estimate=pl.CostEstimate(flops=12 * 10**8, bytes_accessed=5 * 10**6, transcendentals=0),
    )(grad_out, own, sibling)


def body(sizes, grad_out, context, codes, scales):
    count = int(np.prod(sizes))
    chips = sizes[4]
    swap = [(0, 1), (1, 0)]

    send, keep, block = local_terms(sizes, grad_out, context, codes, scales)
    got = lax.ppermute(send, "c", swap)
    held = [block]
    for shift in range(1, chips):
        held.append(lax.ppermute(block, "zl", [(i, (i + shift) % chips) for i in range(chips)]))

    chip = chip_sum(got, keep)
    near = lax.all_to_all(chip, ("x", "yl"), split_axis=0, concat_axis=0, tiled=True)
    near, own = near_sum(near, held)
    sibling = lax.ppermute(own, "c", swap)
    far = lax.all_to_all(near, ("zh", "yh", "zl"), split_axis=0, concat_axis=0, tiled=True)
    weight_grad, bias_grad = last_sum(far, 1.0 / count)

    ctx_grad = ctx_product(chips, grad_out, own, sibling)
    return ctx_grad, weight_grad, bias_grad


def solution(mesh, sizes=SIZES):
    fine = Mesh(mesh.devices.reshape(sizes), NAMES)
    in_specs = (P(NAMES, None), P(NAMES, None), P(("zl", "c"), None, None), P(("zl", "c"), None))
    out_specs = (P(NAMES, None), P(NAMES, None), P(NAMES))
    return jax.shard_map(
        functools.partial(body, sizes), mesh=fine, in_specs=in_specs, out_specs=out_specs, check_vma=False
    )
```

time: 2360 us -> 92.1 us (0.04)
  the two profiles are of different devices: /device:TPU:128 before, /device:TPU:2 now
where the time goes in v1:
time: 92.1 us; the launch traced here: 91.6 us
  blocking collectives  32.8 us (36%)
  starting transfers between devices  23.9 us (26%)
  waiting for transfers between devices  17.8 us (19%)
  Pallas kernels  11.7 us (13%)
  local copies, waits for them, and re-layouts  4.78 us (5%)
    all_to_all x1, blocking collectives, body(): lax.all_to_all(near, ('zh', 'yh', 'zl'), split_axis=0, concat_axis=0, til...  32.8 us
    ppermute x2, waiting for transfers between devices, body(): lax.ppermute(block, 'zl', [(i, (i + shift) % chips) for i in range(chips)])  14.6 us
    all_to_all x1, starting transfers between devices, body(): lax.all_to_all(chip, ('x', 'yl'), split_axis=0, concat_axis=0, tiled=True)  13.2 us
    ppermute x2, starting transfers between devices, body(): lax.ppermute(block, 'zl', [(i, (i + shift) % chips) for i in range(chips)])  6.87 us
    pallas_call x1, Pallas kernels, local_terms(): pl.pallas_call(term_kernel, out_shape=(piece, piece, block), in_specs=[pl...  6.56 us
    unnamed x14, local copies, waits for them, and re-layouts  4.78 us
    ppermute x1, waiting for transfers between devices, body(): got = lax.ppermute(send, 'c', swap)  3.16 us
    pallas_call x1, Pallas kernels, ctx_product(): pl.pallas_call(functools.partial(ctx_kernel, chips), out_shape=jax.ShapeD...  2.34 us
  transfers between devices with their start and end apart: 5, of which 3 were waited for; matrix products, arithmetic and copies ran while one was open for 0% of the time, Pallas kernels for 1%

profile of v1, /device:TPU:2, one launch (start us, length us, event | category | flops | bytes accessed | tf_op | source)
XLA Modules:
  0.0 91.6 jit_solution(11746706016810024619)
XLA Ops:
  0.6 6.6 %shard_map.76 = (bf16[8,48,1664]{2,1,0:T(8,128)(2,1)}, bf16[8,48,1664]{2,1,0:T(8,128)(2,1)}, bf16[256,768]{1,0:T(8,128)(2,1)}) custom-call(s32[768,1]{1,0:T(8,128)} %constant.2.clone.map_hbm, bf16[512,1536]{1,0:T(8,128)(2,1)} %grad_ref.1, bf16[512,768]{1,0:T(8,128)(2,1)} %ctx_hbm.1, bf16[1,256,768]{2,1,0:T(8,128)(2,1)} %codes_hbm.1, bf16[1,768]{1,0:T(2,128)(2,1)} %scales_hbm.1), custom_call_target="tpu_custom_call" | custom-call | flops 4000000000 | bytes 5000000 | tf_op jit(solution)/shard_map/pallas_call | solution.py:104
  7.2 1.9 %collective-permute-start = (bf16[8,48,1664]{2,1,0:T(8,128)(2,1)}, bf16[8,48,1664]{2,1,0:T(8,128)(2,1)S(1)}, u32[]{:S(2)}, u32[]{:S(2)}) collective-permute-start(bf16[8,48,1664]{2,1,0:T(8,128)(2,1)} %get-tuple-element.10), channel_id=1, source_target_pairs={{0,1},{1,0},{2,3},{3,2},{4,5},{5,4},{6,7},{7,6},{8,9},{9,8},{10,11... | collective-permute-start | bytes 3833864 | tf_op jit(solution)/shard_map/ppermute | solution.py:235
  9.1 3.2 %collective-permute-done.got_ref = bf16[8,48,1664]{2,1,0:T(8,128)(2,1)S(1)} collective-permute-done((bf16[8,48,1664]{2,1,0:T(8,128)(2,1)}, bf16[8,48,1664]{2,1,0:T(8,128)(2,1)S(1)}, u32[]{:S(2)}, u32[]{:S(2)}) %collective-permute-start) | collective-permute-done | bytes 1277984 | tf_op jit(solution)/shard_map/ppermute | solution.py:235
  12.3 0.0 copy-start.1
  12.3 1.3 %copy-done.1 = bf16[8,48,1664]{2,1,0:T(8,128)(2,1)S(1)} copy-done((bf16[8,48,1664]{2,1,0:T(8,128)(2,1)S(1)}, bf16[8,48,1664]{2,1,0:T(8,128)(2,1)}, u32[]{:S(2)}) %copy-start.1) | copy-done | bytes 1277976
  13.6 1.6 %shard_map.77 = bf16[8,48,1664]{2,1,0:T(8,128)(2,1)} custom-call(bf16[8,48,1664]{2,1,0:T(8,128)(2,1)S(1)} %collective-permute-done.got_ref, bf16[8,48,1664]{2,1,0:T(8,128)(2,1)S(1)} %copy-done.1), custom_call_target="tpu_custom_call" | custom-call | flops 1000000 | bytes 4000000 | tf_op jit(solution)/shard_map/pallas_call | solution.py:126
  15.2 13.2 %all-to-all-start = ((bf16[8,48,1664]{2,1,0:T(8,128)(2,1)}), bf16[8,48,1664]{2,1,0:T(8,128)(2,1)S(1)}, u32[]{:S(2)}, u32[]{:S(2)}) async-start(bf16[8,48,1664]{2,1,0:T(8,128)(2,1)} %shard_map.77), calls=%async_computation | async-start | bytes 2555904 | tf_op jit(solution)/shard_map/all_to_all | solution.py:241
  28.4 0.0 copy-done.2
  28.4 2.0 %collective-permute-start.1 = (bf16[256,768]{1,0:T(8,128)(2,1)S(1)}, bf16[256,768]{1,0:T(8,128)(2,1)S(1)}, u32[]{:S(2)}, u32[]{:S(2)}) collective-permute-start(bf16[256,768]{1,0:T(8,128)(2,1)S(1)} %copy-done.2), channel_id=1, source_target_pairs={{0,2},{2,4},{4,0},{1,3},{3,5},{5,1},{6,8},{8,10},{10,6},{7,9},{9,1... | collective-permute-start | bytes 1179656 | tf_op jit(solution)/shard_map/ppermute | solution.py:238
  30.5 4.8 %collective-permute-start.2 = (bf16[256,768]{1,0:T(8,128)(2,1)S(1)}, bf16[256,768]{1,0:T(8,128)(2,1)S(1)}, u32[]{:S(2)}, u32[]{:S(2)}) collective-permute-start(bf16[256,768]{1,0:T(8,128)(2,1)S(1)} %copy-done.2), channel_id=1, source_target_pairs={{0,4},{2,0},{4,2},{1,5},{3,1},{5,3},{6,10},{8,6},{10,8},{7,11},{9,... | collective-permute-start | bytes 1179656 | tf_op jit(solution)/shard_map/ppermute | solution.py:238
  35.3 8.1 %collective-permute-done.1.refs_1_ = bf16[256,768]{1,0:T(8,128)(2,1)S(1)} collective-permute-done((bf16[256,768]{1,0:T(8,128)(2,1)S(1)}, bf16[256,768]{1,0:T(8,128)(2,1)S(1)}, u32[]{:S(2)}, u32[]{:S(2)}) %collective-permute-start.1) | collective-permute-done | bytes 393248 | tf_op jit(solution)/shard_map/ppermute | solution.py:238
  43.4 0.7 copy-done.3
  44.2 6.5 %collective-permute-done.2.refs_2_ = bf16[256,768]{1,0:T(8,128)(2,1)S(1)} collective-permute-done((bf16[256,768]{1,0:T(8,128)(2,1)S(1)}, bf16[256,768]{1,0:T(8,128)(2,1)S(1)}, u32[]{:S(2)}, u32[]{:S(2)}) %collective-permute-start.2) | collective-permute-done | bytes 393248 | tf_op jit(solution)/shard_map/ppermute | solution.py:238
  50.7 0.7 copy-done.5
  51.4 0.0 all-to-all-done.got_ref
  51.4 1.0 %copy-done.4 = bf16[256,768]{1,0:T(8,128)(2,1)S(1)} copy-done((bf16[256,768]{1,0:T(8,128)(2,1)S(1)}, bf16[256,768]{1,0:T(8,128)(2,1)}, u32[]{:S(2)}) %copy-start.4) | copy-done | bytes 393240
  52.4 1.0 %copy-done.6 = bf16[256,768]{1,0:T(8,128)(2,1)S(1)} copy-done((bf16[256,768]{1,0:T(8,128)(2,1)S(1)}, bf16[256,768]{1,0:T(8,128)(2,1)}, u32[]{:S(2)}) %copy-start.6) | copy-done | bytes 393240
  53.4 0.5 shard_map.78
  53.9 1.9 %collective-permute-start.3 = (bf16[768,768]{1,0:T(8,128)(2,1)S(1)}, bf16[768,768]{1,0:T(8,128)(2,1)S(1)}, u32[]{:S(2)}, u32[]{:S(2)}) collective-permute-start(bf16[768,768]{1,0:T(8,128)(2,1)S(1)} %get-tuple-element.13.own_ref), channel_id=1, source_target_pairs={{0,1},{1,0},{2,3},{3,2},{4,5},{5,4},{6,7},{7,6},{8,9},{9,8},{10,11... | collective-permute-start | bytes 3538952 | tf_op jit(solution)/shard_map/ppermute | solution.py:243
  55.8 32.8 %all_to_all.10.far_ref = bf16[48,13,128]{2,1,0:T(8,128)(2,1)S(1)} all-to-all(bf16[48,13,128]{2,1,0:T(8,128)(2,1)S(1)} %get-tuple-element.14), channel_id=1, replica_groups=mesh['zh'=4,'x'=4,'yh'=4,'yl'=2,'zl'=3,'c'=2] {'zh','yh','zl'}, dimensions={0} | all-to-all | bytes 319488 | tf_op jit(solution)/shard_map/all_to_all | solution.py:244
  88.6 0.7 shard_map.80
  89.3 0.0 collective-permute-done.3.sibling_ref
  89.3 0.0 copy-done
  89.3 2.3 %shard_map.79 = bf16[512,768]{1,0:T(8,128)(2,1)} custom-call(bf16[512,1536]{1,0:T(8,128)(2,1)S(1)} %copy-done, bf16[768,768]{1,0:T(8,128)(2,1)S(1)} %get-tuple-element.13.own_ref, bf16[768,768]{1,0:T(8,128)(2,1)S(1)} %collective-permute-done.3.sibling_ref), custom_call_target="tpu_custom_call" | custom-call | flops 1200000000 | bytes 5000000 | tf_op jit(solution)/shard_map/pallas_call | solution.py:218
  (6 shorter events, 0.0 us)
Async XLA Ops:
  7.2 5.1 %collective-permute-start = (bf16[8,48,1664]{2,1,0:T(8,128)(2,1)}, bf16[8,48,1664]{2,1,0:T(8,128)(2,1)S(1)}, u32[]{:S(2)}, u32[]{:S(2)}) collective-permute-start(bf16[8,48,1664]{2,1,0:T(8,128)(2,1)} %get-tuple-element.10), channel_id=1, source_target_pairs={{0,1},{1,0},{2,3},{3,2},{4,5},{5,4},{6,7},{7,6},{8,9},{9,8},{10,11... | collective-permute-start | bytes 3833864 | tf_op jit(solution)/shard_map/ppermute | solution.py:235
  12.3 1.3 %copy-start.1 = (bf16[8,48,1664]{2,1,0:T(8,128)(2,1)S(1)}, bf16[8,48,1664]{2,1,0:T(8,128)(2,1)}, u32[]{:S(2)}) copy-start(bf16[8,48,1664]{2,1,0:T(8,128)(2,1)} %get-tuple-element.11.keep_ref) | copy-start | bytes 3833860
  15.2 13.2 %copy-start.2 = (bf16[256,768]{1,0:T(8,128)(2,1)S(1)}, bf16[256,768]{1,0:T(8,128)(2,1)}, u32[]{:S(2)}) copy-start(bf16[256,768]{1,0:T(8,128)(2,1)} %get-tuple-element.12.refs_0_) | copy-start | bytes 1179652
  15.2 36.2 %all-to-all-start = ((bf16[8,48,1664]{2,1,0:T(8,128)(2,1)}), bf16[8,48,1664]{2,1,0:T(8,128)(2,1)S(1)}, u32[]{:S(2)}, u32[]{:S(2)}) async-start(bf16[8,48,1664]{2,1,0:T(8,128)(2,1)} %shard_map.77), calls=%async_computation | async-start | bytes 2555904 | tf_op jit(solution)/shard_map/all_to_all | solution.py:241
  28.4 60.8 %copy-start = (bf16[512,1536]{1,0:T(8,128)(2,1)S(1)}, bf16[512,1536]{1,0:T(8,128)(2,1)}, u32[]{:S(2)}) copy-start(bf16[512,1536]{1,0:T(8,128)(2,1)} %grad_ref.1) | copy-start | bytes 4718596
  28.4 15.0 %collective-permute-start.1 = (bf16[256,768]{1,0:T(8,128)(2,1)S(1)}, bf16[256,768]{1,0:T(8,128)(2,1)S(1)}, u32[]{:S(2)}, u32[]{:S(2)}) collective-permute-start(bf16[256,768]{1,0:T(8,128)(2,1)S(1)} %copy-done.2), channel_id=1, source_target_pairs={{0,2},{2,4},{4,0},{1,3},{3,5},{5,1},{6,8},{8,10},{10,6},{7,9},{9,1... | collective-permute-start | bytes 1179656 | tf_op jit(solution)/shard_map/ppermute | solution.py:238
  30.5 20.2 %collective-permute-start.2 = (bf16[256,768]{1,0:T(8,128)(2,1)S(1)}, bf16[256,768]{1,0:T(8,128)(2,1)S(1)}, u32[]{:S(2)}, u32[]{:S(2)}) collective-permute-start(bf16[256,768]{1,0:T(8,128)(2,1)S(1)} %copy-done.2), channel_id=1, source_target_pairs={{0,4},{2,0},{4,2},{1,5},{3,1},{5,3},{6,10},{8,6},{10,8},{7,11},{9,... | collective-permute-start | bytes 1179656 | tf_op jit(solution)/shard_map/ppermute | solution.py:238
  43.4 0.7 copy-start.3
  50.7 0.7 copy-start.5
  51.4 1.0 %copy-start.4 = (bf16[256,768]{1,0:T(8,128)(2,1)S(1)}, bf16[256,768]{1,0:T(8,128)(2,1)}, u32[]{:S(2)}) copy-start(bf16[256,768]{1,0:T(8,128)(2,1)} %copy-done.3) | copy-start | bytes 1179652
  52.4 1.0 %copy-start.6 = (bf16[256,768]{1,0:T(8,128)(2,1)S(1)}, bf16[256,768]{1,0:T(8,128)(2,1)}, u32[]{:S(2)}) copy-start(bf16[256,768]{1,0:T(8,128)(2,1)} %copy-done.5) | copy-start | bytes 1179652
  53.9 35.4 %collective-permute-start.3 = (bf16[768,768]{1,0:T(8,128)(2,1)S(1)}, bf16[768,768]{1,0:T(8,128)(2,1)S(1)}, u32[]{:S(2)}, u32[]{:S(2)}) collective-permute-start(bf16[768,768]{1,0:T(8,128)(2,1)S(1)} %get-tuple-element.13.own_ref), channel_id=1, source_target_pairs={{0,1},{1,0},{2,3},{3,2},{4,5},{5,4},{6,7},{7,6},{8,9},{9,8},{10,11... | collective-permute-start | bytes 3538952 | tf_op jit(solution)/shard_map/ppermute | solution.py:243

commit v2 on v1

v2 whole, which is shorter than its diff:
```python
import functools
import jax
import jax.numpy as jnp
import numpy as np
from jax import lax
from jax.experimental import pallas as pl
from jax.experimental.pallas import tpu as pltpu
from jax.sharding import Mesh, PartitionSpec as P

SIZES = (4, 4, 4, 2, 3, 2)
NAMES = ("zh", "x", "yh", "yl", "zl", "c")
PAD = 128


ANY = pl.BlockSpec(memory_space=pl.ANY)
VMEM = pl.BlockSpec(memory_space=pltpu.VMEM)


def parameters():
    return pltpu.CompilerParams(vmem_limit_bytes=64 * 1024 * 1024)


def row_map(sizes):
    _, x, yh, yl, zl, _ = sizes
    index = np.arange(2 * x * yh * yl * zl * 4).reshape(2, x, yh, yl, zl, 2, 2)[..., :1, :]
    return np.transpose(index, (5, 6, 1, 3, 2, 0, 4)).reshape(-1, 1).astype(np.int32)


def split_pairs(values):
    lane = lax.broadcasted_iota(jnp.int32, (values[0].shape[0], PAD), 1)
    parts = jnp.zeros(lane.shape, jnp.float32)
    for s, value in enumerate(values):
        high = value.astype(jnp.bfloat16).astype(jnp.float32)
        parts = jnp.where(lane == 2 * s, high, parts)
        parts = jnp.where(lane == 2 * s + 1, value - high, parts)
    return parts


def join_pairs(parts):
    lane = lax.broadcasted_iota(jnp.int32, parts.shape, 1)
    return [
        jnp.sum(jnp.where((lane == 2 * s) | (lane == 2 * s + 1), parts, 0.0), axis=1, keepdims=True)
        for s in range(2)
    ]


def term_kernel(mine, *refs):
    count = 5 if mine else 3
    inputs, refs = refs[:count], refs[count:]
    outputs, refs = refs[: 1 + mine], refs[1 + mine :]
    held, (acc, done, in_sems, out_sems) = refs[:count], refs[count:]
    map_ref, grad_ref, ctx_ref = held[:3]
    core = lax.axis_index("c")
    rows = map_ref.shape[0]
    span = 2 * rows
    width = ctx_ref.shape[1]
    blocks, part = done.shape[0], done.shape[1] // 2

    def columns(step):
        return pl.ds(step * span, span)

    copies = [
        pltpu.make_async_copy(inputs[1].at[:, columns(0)], grad_ref.at[:, columns(0)], in_sems.at[0]),
        pltpu.make_async_copy(inputs[0], map_ref, in_sems.at[1]),
        pltpu.make_async_copy(inputs[2], ctx_ref, in_sems.at[2]),
        pltpu.make_async_copy(inputs[1].at[:, columns(1)], grad_ref.at[:, columns(1)], in_sems.at[3]),
    ]
    for extra in range(3, count):
        copies.append(pltpu.make_async_copy(inputs[extra], held[extra], in_sems.at[extra + 1]))
    for copy in copies:
        copy.start()
    copies[1].wait()
    source = map_ref[...] + 2 * (core if mine else 1 - core)
    column = lax.broadcasted_iota(jnp.int32, (rows, span), 1)
    pick = jnp.where(source == column, 1.0, 0.0).astype(jnp.bfloat16)
    ones = jnp.ones((ctx_ref.shape[0], PAD), jnp.bfloat16)
    for step in range(2):
        copies[3 * step].wait()
        moved = lax.dot_general(
            pick,
            grad_ref[:, step * span : (step + 1) * span],
            (((1,), (1,)), ((), ())),
            preferred_element_type=jnp.float32,
        ).astype(jnp.bfloat16)
        if step == 0:
            copies[2].wait()
        acc[step, :, :width] = jnp.dot(moved, ctx_ref[...], preferred_element_type=jnp.float32)
        acc[step, :, width:] = jnp.dot(moved, ones, preferred_element_type=jnp.float32)
    sent = []
    for block in range(blocks):
        sums = []
        for s in range(2):
            at = (s * blocks + block) * part
            both = jnp.concatenate([acc[0, at : at + part, :], acc[1, at : at + part, :]], axis=0)
            done[block, :, s * width : (s + 1) * width] = both[:, :width].astype(jnp.bfloat16)
            sums.append(both[:, width:])
        done[block, :, 2 * width :] = split_pairs(sums).astype(jnp.bfloat16)
        sent.append(pltpu.make_async_copy(done.at[block], outputs[0].at[block], out_sems.at[block]))
        sent[-1].start()
    if mine:
        copies[4].wait()
        copies[5].wait()
        scaled = held[3][0].astype(jnp.float32) * held[4][...].astype(jnp.float32)
        outputs[1][...] = scaled.astype(jnp.bfloat16)
    for copy in sent:
        copy.wait()


def local_terms(sizes, mine, grad_out, context, *weights):
    zh, x, yh, yl, zl, _ = sizes
    width = context.shape[1]
    piece = jax.ShapeDtypeStruct((x * yl, zh * yh * zl, 2 * width + PAD), jnp.bfloat16)
    rows = row_map(sizes)
    operands = (jnp.asarray(rows), grad_out, context, *weights)
    shapes, specs = (piece,), (ANY,)
    if mine:
        shapes += (jax.ShapeDtypeStruct(weights[0].shape[1:], jnp.bfloat16),)
        specs += (VMEM,)
    return pl.pallas_call(
        functools.partial(term_kernel, mine),
        out_shape=shapes,
        in_specs=[ANY] * len(operands),
        out_specs=specs,
        scratch_shapes=[pltpu.VMEM(a.shape, a.dtype) for a in operands]
        + [
            pltpu.VMEM((2, rows.shape[0], width + PAD), jnp.float32),
            pltpu.VMEM(piece.shape, piece.dtype),
            pltpu.SemaphoreType.DMA((6,)),
            pltpu.SemaphoreType.DMA((piece.shape[0],)),
        ],
        compiler_params=parameters(),
        cost_estimate=pl.CostEstimate(flops=2 * 10**9, bytes_accessed=5 * 10**6, transcendentals=0),
    )(*operands)


def ctx_kernel(chips, grad_hbm, own_hbm, sibling_hbm, out_hbm, grad_ref, weight_ref, out_ref, in_sems, out_sems):
    chip, core = lax.axis_index("zl"), lax.axis_index("c")
    rows = own_hbm.shape[0] // chips
    half = grad_hbm.shape[0] // 2

    def tokens(step):
        return pl.ds(step * half, half)

    grads = [
        pltpu.make_async_copy(grad_hbm.at[tokens(i)], grad_ref.at[tokens(i)], in_sems.at[i]) for i in range(2)
    ]
    blocks = []
    for side, held in enumerate((own_hbm, sibling_hbm)):
        for back in range(chips):
            slot = side * chips + back
            blocks.append(
                pltpu.make_async_copy(
                    held.at[pl.ds(back * rows, rows)],
                    weight_ref.at[pl.ds(slot * rows, rows)],
                    in_sems.at[2 + slot],
                )
            )
    grads[0].start()
    for copy in blocks:
        copy.start()
    grads[1].start()
    outs = []
    for step in range(2):
        grads[step].wait()
        total = None
        for slot in range(2 * chips):
            if step == 0:
                blocks[slot].wait()
            owner = lax.rem(chip + chips - slot % chips, chips)
            side = core if slot < chips else 1 - core
            at = pl.multiple_of((2 * owner + side) * rows, rows)
            product = jnp.dot(
                grad_ref[step * half : (step + 1) * half, pl.ds(at, rows)],
                weight_ref[slot * rows : (slot + 1) * rows, :],
                preferred_element_type=jnp.float32,
            )
            total = product if total is None else total + product
        out_ref[step * half : (step + 1) * half, :] = total.astype(out_ref.dtype)
        outs.append(pltpu.make_async_copy(out_ref.at[tokens(step)], out_hbm.at[tokens(step)], out_sems.at[step]))
        outs[-1].start()
    for copy in outs:
        copy.wait()


def ctx_product(chips, grad_out, own, sibling):
    out = jax.ShapeDtypeStruct((grad_out.shape[0], own.shape[1]), jnp.bfloat16)
    return pl.pallas_call(
        functools.partial(ctx_kernel, chips),
        out_shape=out,
        in_specs=[ANY] * 3,
        out_specs=ANY,
        scratch_shapes=[
            pltpu.VMEM(grad_out.shape, grad_out.dtype),
            pltpu.VMEM((2 * own.shape[0], own.shape[1]), own.dtype),
            pltpu.VMEM(out.shape, out.dtype),
            pltpu.SemaphoreType.DMA((2 + 2 * chips,)),
            pltpu.SemaphoreType.DMA((2,)),
        ],
        compiler_params=parameters(),
        cost_estimate=pl.CostEstimate(flops=12 * 10**8, bytes_accessed=5 * 10**6, transcendentals=0),
    )(grad_out, own, sibling)


def chip_kernel(got_hbm, keep_hbm, out_hbm, got_ref, keep_ref, out_ref, in_sems, out_sems):
    wide = out_ref.shape[2] - PAD
    blocks = range(out_ref.shape[0])
    pairs = []
    for b in blocks:
        pairs.append(
            (
                pltpu.make_async_copy(got_hbm.at[b], got_ref.at[b], in_sems.at[0, b]),
                pltpu.make_async_copy(keep_hbm.at[b], keep_ref.at[b], in_sems.at[1, b]),
            )
        )
        for copy in pairs[-1]:
            copy.start()
    outs = []
    for b in blocks:
        for copy in pairs[b]:
            copy.wait()
        total = got_ref[b].astype(jnp.float32) + keep_ref[b].astype(jnp.float32)
        out_ref[b, :, :wide] = total[:, :wide].astype(out_ref.dtype)
        out_ref[b, :, wide:] = split_pairs(join_pairs(total[:, wide:])).astype(out_ref.dtype)
        outs.append(pltpu.make_async_copy(out_ref.at[b], out_hbm.at[b], out_sems.at[b]))
        outs[-1].start()
    for copy in outs:
        copy.wait()


def chip_sum(got, keep):
    return pl.pallas_call(
        chip_kernel,
        out_shape=jax.ShapeDtypeStruct(got.shape, got.dtype),
        in_specs=[ANY] * 2,
        out_specs=ANY,
        scratch_shapes=[pltpu.VMEM(got.shape, got.dtype)] * 3
        + [pltpu.SemaphoreType.DMA((2, got.shape[0])), pltpu.SemaphoreType.DMA((got.shape[0],))],
        compiler_params=parameters(),
        cost_estimate=pl.CostEstimate(flops=10**6, bytes_accessed=4 * 10**6, transcendentals=0),
    )(got, keep)


def near_kernel(groups, got_hbm, sum_ref, got_ref, wide, sems):
    copies = [
        pltpu.make_async_copy(got_hbm.at[b], got_ref.at[b], sems.at[b]) for b in range(got_ref.shape[0])
    ]
    for copy in copies:
        copy.start()
    for copy in copies:
        copy.wait()
    for chunk in range(sum_ref.shape[1]):
        lanes = slice(chunk * PAD, (chunk + 1) * PAD)
        total = got_ref[0, :, lanes].astype(jnp.float32)
        for index in range(1, got_ref.shape[0]):
            total = total + got_ref[index, :, lanes].astype(jnp.float32)
        if chunk == sum_ref.shape[1] - 1:
            total = split_pairs(join_pairs(total))
        wide[:, chunk, :] = total
    rest = sum_ref.shape[0] // (2 * groups)
    for high in range(2):
        for group in range(groups):
            to, at = (2 * group + high) * rest, (high * groups + group) * rest
            sum_ref[to : to + rest] = wide[at : at + rest].astype(sum_ref.dtype)


def near_sum(groups, got):
    _, rows, lanes = got.shape
    shape = (rows, lanes // PAD, PAD)
    return pl.pallas_call(
        functools.partial(near_kernel, groups),
        out_shape=jax.ShapeDtypeStruct(shape, jnp.bfloat16),
        in_specs=[ANY],
        out_specs=VMEM,
        scratch_shapes=[
            pltpu.VMEM(got.shape, got.dtype),
            pltpu.VMEM(shape, jnp.float32),
            pltpu.SemaphoreType.DMA((got.shape[0],)),
        ],
        compiler_params=parameters(),
        cost_estimate=pl.CostEstimate(flops=10**6, bytes_accessed=15 * 10**5, transcendentals=0),
    )(got)


def middle_kernel(got_ref, *refs):
    held, (sum_ref, own_hbm, wide, sems) = refs[:-4], refs[-4:]
    rows = held[0].shape[0]
    copies = [
        pltpu.make_async_copy(block, own_hbm.at[pl.ds(i * rows, rows)], sems.at[i]) for i, block in enumerate(held)
    ]
    for copy in copies:
        copy.start()
    many = sum_ref.shape[0]
    total = got_ref[0:many].astype(jnp.float32)
    for index in range(1, got_ref.shape[0] // many):
        total = total + got_ref[index * many : (index + 1) * many].astype(jnp.float32)
    wide[...] = total
    last = wide.shape[1] - 1
    wide[:, last, :] = split_pairs(join_pairs(wide[:, last, :]))
    sum_ref[...] = wide[...].astype(sum_ref.dtype)
    for copy in copies:
        copy.wait()


def middle_sum(groups, got, held):
    shape = (got.shape[0] // groups, *got.shape[1:])
    tall = (len(held) * held[0].shape[0], held[0].shape[1])
    return pl.pallas_call(
        middle_kernel,
        out_shape=(jax.ShapeDtypeStruct(shape, jnp.bfloat16), jax.ShapeDtypeStruct(tall, jnp.bfloat16)),
        in_specs=[VMEM] + [ANY] * len(held),
        out_specs=(VMEM, ANY),
        scratch_shapes=[pltpu.VMEM(shape, jnp.float32), pltpu.SemaphoreType.DMA((len(held),))],
        compiler_params=parameters(),
        cost_estimate=pl.CostEstimate(flops=10**6, bytes_accessed=3 * 10**6, transcendentals=0),
    )(got, *held)


def last_kernel(scale, far_ref, weight_ref, bias_ref):
    total = far_ref[0].astype(jnp.float32)
    for index in range(1, far_ref.shape[0]):
        total = total + far_ref[index].astype(jnp.float32)
    total = total * scale
    chunks = (total.shape[0] - 1) // 2
    for s in range(2):
        for chunk in range(chunks):
            at = s * chunks + chunk
            weight_ref[s : s + 1, chunk * PAD : (chunk + 1) * PAD] = total[at : at + 1, :]
    tail = total[2 * chunks : 2 * chunks + 1, :]
    lane = lax.broadcasted_iota(jnp.int32, (1, PAD), 1)
    for s in range(2):
        bias_ref[s] = jnp.sum(jnp.where((lane == 2 * s) | (lane == 2 * s + 1), tail, 0.0))


def last_sum(far, scale):
    width = (far.shape[1] - 1) // 2 * PAD
    return pl.pallas_call(
        functools.partial(last_kernel, scale),
        out_shape=(jax.ShapeDtypeStruct((2, width), jnp.float32), jax.ShapeDtypeStruct((2,), jnp.float32)),
        in_specs=[VMEM],
        out_specs=(pl.BlockSpec((2, width), lambda: (0, 0)), pl.BlockSpec(memory_space=pltpu.SMEM)),
        compiler_params=parameters(),
        cost_estimate=pl.CostEstimate(flops=10**5, bytes_accessed=2 * 10**5, transcendentals=0),
    )(far)


def body(sizes, grad_out, context, codes, scales):
    count = int(np.prod(sizes))
    chips = sizes[4]
    swap = [(0, 1), (1, 0)]

    (send,) = local_terms(sizes, False, grad_out, context)
    got = lax.ppermute(send, "c", swap)
    keep, block = local_terms(sizes, True, grad_out, context, codes, scales)
    held = [block]
    for shift in range(1, chips):
        held.append(lax.ppermute(block, "zl", [(i, (i + shift) % chips) for i in range(chips)]))

    near = lax.all_to_all(chip_sum(got, keep), ("x", "yl"), split_axis=0, concat_axis=0, tiled=True)
    near = near_sum(sizes[2], near)
    middle = lax.all_to_all(near, "yh", split_axis=0, concat_axis=0, tiled=True)
    middle, own = middle_sum(sizes[2], middle, held)
    sibling = lax.ppermute(own, "c", swap)
    far = lax.all_to_all(middle, ("zh", "zl"), split_axis=0, concat_axis=0, tiled=True)
    weight_grad, bias_grad = last_sum(far, 1.0 / count)

    ctx_grad = ctx_product(chips, grad_out, own, sibling)
    return ctx_grad, weight_grad, bias_grad


def solution(mesh, sizes=SIZES):
    fine = Mesh(mesh.devices.reshape(sizes), NAMES)
    in_specs = (P(NAMES, None), P(NAMES, None), P(("zl", "c"), None, None), P(("zl", "c"), None))
    out_specs = (P(NAMES, None), P(NAMES, None), P(NAMES))
    return jax.shard_map(
        functools.partial(body, sizes), mesh=fine, in_specs=in_specs, out_specs=out_specs, check_vma=False
    )
```

time: 92.1 us -> 131 us (1.42)
  the two profiles are of different devices: /device:TPU:2 before, /device:TPU:1 now
where the time goes in v2:
time: 131 us; the launch traced here: 130 us
  Pallas kernels  60 us (46%)
  starting transfers between devices  30.5 us (23%)
  waiting for transfers between devices  20.9 us (16%)
  blocking collectives  18.1 us (14%)
    pallas_call x1, Pallas kernels, middle_sum(): pl.pallas_call(middle_kernel, out_shape=(jax.ShapeDtypeStruct(shape, jnp....  38.4 us
    all_to_all x1, blocking collectives, body(): lax.all_to_all(middle, ('zh', 'zl'), split_axis=0, concat_axis=0, tiled=T...  18.1 us
    all_to_all x1, waiting for transfers between devices, body(): lax.all_to_all(chip_sum(got, keep), ('x', 'yl'), split_axis=0, concat_axi...  13.1 us
    ppermute x1, starting transfers between devices, body(): got = lax.ppermute(send, 'c', swap)  12.4 us
    pallas_call x2, Pallas kernels, local_terms(): pl.pallas_call(functools.partial(term_kernel, mine), out_shape=shapes, in...  9.8 us
    all_to_all x1, waiting for transfers between devices, body(): middle = lax.all_to_all(near, 'yh', split_axis=0, concat_axis=0, tiled=True)  7.83 us
    ppermute x2, starting transfers between devices, body(): lax.ppermute(block, 'zl', [(i, (i + shift) % chips) for i in range(chips)])  5.29 us
    pallas_call x1, Pallas kernels, ctx_product(): pl.pallas_call(functools.partial(ctx_kernel, chips), out_shape=out, in_sp...  5.05 us
  transfers between devices with their start and end apart: 6, of which 2 were waited for; matrix products, arithmetic and copies ran while one was open for 0% of the time, Pallas kernels for 7%

profile of v2, /device:TPU:1, one launch (start us, length us, event | category | flops | bytes accessed | tf_op | source)
XLA Modules:
  0.0 130.2 jit_solution(10230386065094766822)
XLA Ops:
  0.6 4.5 %shard_map.85 = bf16[8,48,1664]{2,1,0:T(8,128)(2,1)} custom-call(s32[384,1]{1,0:T(8,128)} %constant.2.clone.refs_0_, bf16[512,1536]{1,0:T(8,128)(2,1)} %grad_hbm.1, bf16[512,768]{1,0:T(8,128)(2,1)} %refs_2_.3), custom_call_target="tpu_custom_call" | custom-call | flops 2000000000 | bytes 5000000 | tf_op jit(solution)/shard_map/pallas_call | solution.py:119
  5.2 12.4 %collective-permute-start = (bf16[8,48,1664]{2,1,0:T(8,128)(2,1)}, bf16[8,48,1664]{2,1,0:T(8,128)(2,1)}, u32[]{:S(2)}, u32[]{:S(2)}) collective-permute-start(bf16[8,48,1664]{2,1,0:T(8,128)(2,1)} %shard_map.85), channel_id=1, source_target_pairs={{0,1},{1,0},{2,3},{3,2},{4,5},{5,4},{6,7},{7,6},{8,9},{9,8},{10,11... | collective-permute-start | bytes 3833864 | tf_op jit(solution)/shard_map/ppermute | solution.py:352
  17.6 5.3 %shard_map.86 = (bf16[8,48,1664]{2,1,0:T(8,128)(2,1)}, bf16[256,768]{1,0:T(8,128)(2,1)}) custom-call(s32[384,1]{1,0:T(8,128)} %constant.2.clone.refs_0_, bf16[512,1536]{1,0:T(8,128)(2,1)} %grad_hbm.1, bf16[512,768]{1,0:T(8,128)(2,1)} %refs_2_.3, bf16[1,256,768]{2,1,0:T(8,128)(2,1)} %refs_3_.1, bf16[1,768]{1,0:T(2,128)(2,1)} %refs_4_.1), custom_call_target="tpu_custom_call" | custom-call | flops 2000000000 | bytes 5000000 | tf_op jit(solution)/shard_map/pallas_call | solution.py:119
  22.9 0.0 collective-permute-done.got_hbm
  22.9 2.7 %shard_map.87 = bf16[8,48,1664]{2,1,0:T(8,128)(2,1)} custom-call(bf16[8,48,1664]{2,1,0:T(8,128)(2,1)} %collective-permute-done.got_hbm, bf16[8,48,1664]{2,1,0:T(8,128)(2,1)} %get-tuple-element.9.keep_hbm), custom_call_target="tpu_custom_call" | custom-call | flops 1000000 | bytes 4000000 | tf_op jit(solution)/shard_map/pallas_call | solution.py:231
  25.6 4.3 %all-to-all-start = ((bf16[8,48,1664]{2,1,0:T(8,128)(2,1)}), bf16[8,48,1664]{2,1,0:T(8,128)(2,1)}, u32[]{:S(2)}, u32[]{:S(2)}) async-start(bf16[8,48,1664]{2,1,0:T(8,128)(2,1)} %shard_map.87), calls=%async_computation | async-start | bytes 2555904 | tf_op jit(solution)/shard_map/all_to_all | solution.py:358
  29.9 1.9 %collective-permute-start.2 = (bf16[256,768]{1,0:T(8,128)(2,1)}, bf16[256,768]{1,0:T(8,128)(2,1)}, u32[]{:S(2)}, u32[]{:S(2)}) collective-permute-start(bf16[256,768]{1,0:T(8,128)(2,1)} %get-tuple-element.10.refs_0_), channel_id=1, source_target_pairs={{0,4},{2,0},{4,2},{1,5},{3,1},{5,3},{6,10},{8,6},{10,8},{7,11},{9,... | collective-permute-start | bytes 1179656 | tf_op jit(solution)/shard_map/ppermute | solution.py:356
  31.8 3.4 %collective-permute-start.1 = (bf16[256,768]{1,0:T(8,128)(2,1)}, bf16[256,768]{1,0:T(8,128)(2,1)}, u32[]{:S(2)}, u32[]{:S(2)}) collective-permute-start(bf16[256,768]{1,0:T(8,128)(2,1)} %get-tuple-element.10.refs_0_), channel_id=1, source_target_pairs={{0,2},{2,4},{4,0},{1,3},{3,5},{5,1},{6,8},{8,10},{10,6},{7,9},{9,1... | collective-permute-start | bytes 1179656 | tf_op jit(solution)/shard_map/ppermute | solution.py:356
  35.2 13.1 %all-to-all-done.got_hbm = bf16[8,48,1664]{2,1,0:T(8,128)(2,1)} async-done(((bf16[8,48,1664]{2,1,0:T(8,128)(2,1)}), bf16[8,48,1664]{2,1,0:T(8,128)(2,1)}, u32[]{:S(2)}, u32[]{:S(2)}) %all-to-all-start) | async-done | bytes 1277984 | tf_op jit(solution)/shard_map/all_to_all | solution.py:358
  48.3 2.5 %shard_map.88 = bf16[48,13,128]{2,1,0:T(8,128)(2,1)} custom-call(bf16[8,48,1664]{2,1,0:T(8,128)(2,1)} %all-to-all-done.got_hbm), custom_call_target="tpu_custom_call" | custom-call | flops 1000000 | bytes 1500000 | tf_op jit(solution)/shard_map/pallas_call | solution.py:269
  50.8 4.0 %all-to-all-start.1 = ((bf16[48,13,128]{2,1,0:T(8,128)(2,1)}), bf16[48,13,128]{2,1,0:T(8,128)(2,1)}, u32[]{:S(2)}, u32[]{:S(2)}) async-start(bf16[48,13,128]{2,1,0:T(8,128)(2,1)} %shard_map.88), calls=%async_computation.1 | async-start | bytes 393216 | tf_op jit(solution)/shard_map/all_to_all | solution.py:360
  54.8 0.0 collective-permute-done.2.refs_2_
  54.8 0.0 collective-permute-done.1.refs_1_
  54.9 7.8 %all-to-all-done.1.got_ref = bf16[48,13,128]{2,1,0:T(8,128)(2,1)} async-done(((bf16[48,13,128]{2,1,0:T(8,128)(2,1)}), bf16[48,13,128]{2,1,0:T(8,128)(2,1)}, u32[]{:S(2)}, u32[]{:S(2)}) %all-to-all-start.1) | async-done | bytes 159776 | tf_op jit(solution)/shard_map/all_to_all | solution.py:360
  62.7 38.4 %shard_map.89 = (bf16[12,13,128]{2,1,0:T(8,128)(2,1)}, bf16[768,768]{1,0:T(8,128)(2,1)}) custom-call(bf16[48,13,128]{2,1,0:T(8,128)(2,1)} %all-to-all-done.1.got_ref, bf16[256,768]{1,0:T(8,128)(2,1)} %get-tuple-element.10.refs_0_, bf16[256,768]{1,0:T(8,128)(2,1)} %collective-permute-done.1.refs_1_, bf16[256,768]{1,0:T(8,128)(2,1)} %collective-permute-done.2.refs_2_), custom_call_target="tpu_custom_call" | custom-call | flops 1000000 | bytes 3000000 | tf_op jit(solution)/shard_map/pallas_call | solution.py:307
  101.1 4.5 %collective-permute-start.3 = (bf16[768,768]{1,0:T(8,128)(2,1)}, bf16[768,768]{1,0:T(8,128)(2,1)}, u32[]{:S(2)}, u32[]{:S(2)}) collective-permute-start(bf16[768,768]{1,0:T(8,128)(2,1)} %get-tuple-element.11.own_hbm), channel_id=1, source_target_pairs={{0,1},{1,0},{2,3},{3,2},{4,5},{5,4},{6,7},{7,6},{8,9},{9,8},{10,11... | collective-permute-start | bytes 3538952 | tf_op jit(solution)/shard_map/ppermute | solution.py:362
  105.6 18.1 %all_to_all.15.far_ref = bf16[12,13,128]{2,1,0:T(8,128)(2,1)} all-to-all(bf16[12,13,128]{2,1,0:T(8,128)(2,1)} %get-tuple-element.12), channel_id=1, replica_groups=mesh['zh'=4,'x'=4,'yh'=4,'yl'=2,'zl'=3,'c'=2] {'zh','zl'}, dimensions={0} | all-to-all | bytes 79872 | tf_op jit(solution)/shard_map/all_to_all | solution.py:363
  123.7 1.4 %shard_map.91 = (f32[2,768]{1,0:T(2,128)}, f32[2]{0:T(128)}) custom-call(bf16[12,13,128]{2,1,0:T(8,128)(2,1)} %all_to_all.15.far_ref), custom_call_target="tpu_custom_call" | custom-call | flops 100000 | bytes 200000 | tf_op jit(solution)/shard_map/pallas_call | solution.py:336
  125.2 0.0 collective-permute-done.3.sibling_hbm
  125.2 5.1 %shard_map.90 = bf16[512,768]{1,0:T(8,128)(2,1)} custom-call(bf16[512,1536]{1,0:T(8,128)(2,1)} %grad_hbm.1, bf16[768,768]{1,0:T(8,128)(2,1)} %get-tuple-element.11.own_hbm, bf16[768,768]{1,0:T(8,128)(2,1)} %collective-permute-done.3.sibling_hbm), custom_call_target="tpu_custom_call" | custom-call | flops 1200000000 | bytes 5000000 | tf_op jit(solution)/shard_map/pallas_call | solution.py:187
Async XLA Ops:
  5.2 17.7 %collective-permute-start = (bf16[8,48,1664]{2,1,0:T(8,128)(2,1)}, bf16[8,48,1664]{2,1,0:T(8,128)(2,1)}, u32[]{:S(2)}, u32[]{:S(2)}) collective-permute-start(bf16[8,48,1664]{2,1,0:T(8,128)(2,1)} %shard_map.85), channel_id=1, source_target_pairs={{0,1},{1,0},{2,3},{3,2},{4,5},{5,4},{6,7},{7,6},{8,9},{9,8},{10,11... | collective-permute-start | bytes 3833864 | tf_op jit(solution)/shard_map/ppermute | solution.py:352
  25.6 22.7 %all-to-all-start = ((bf16[8,48,1664]{2,1,0:T(8,128)(2,1)}), bf16[8,48,1664]{2,1,0:T(8,128)(2,1)}, u32[]{:S(2)}, u32[]{:S(2)}) async-start(bf16[8,48,1664]{2,1,0:T(8,128)(2,1)} %shard_map.87), calls=%async_computation | async-start | bytes 2555904 | tf_op jit(solution)/shard_map/all_to_all | solution.py:358
  29.9 24.9 %collective-permute-start.2 = (bf16[256,768]{1,0:T(8,128)(2,1)}, bf16[256,768]{1,0:T(8,128)(2,1)}, u32[]{:S(2)}, u32[]{:S(2)}) collective-permute-start(bf16[256,768]{1,0:T(8,128)(2,1)} %get-tuple-element.10.refs_0_), channel_id=1, source_target_pairs={{0,4},{2,0},{4,2},{1,5},{3,1},{5,3},{6,10},{8,6},{10,8},{7,11},{9,... | collective-permute-start | bytes 1179656 | tf_op jit(solution)/shard_map/ppermute | solution.py:356
  31.8 23.0 %collective-permute-start.1 = (bf16[256,768]{1,0:T(8,128)(2,1)}, bf16[256,768]{1,0:T(8,128)(2,1)}, u32[]{:S(2)}, u32[]{:S(2)}) collective-permute-start(bf16[256,768]{1,0:T(8,128)(2,1)} %get-tuple-element.10.refs_0_), channel_id=1, source_target_pairs={{0,2},{2,4},{4,0},{1,3},{3,5},{5,1},{6,8},{8,10},{10,6},{7,9},{9,1... | collective-permute-start | bytes 1179656 | tf_op jit(solution)/shard_map/ppermute | solution.py:356
  50.8 11.9 %all-to-all-start.1 = ((bf16[48,13,128]{2,1,0:T(8,128)(2,1)}), bf16[48,13,128]{2,1,0:T(8,128)(2,1)}, u32[]{:S(2)}, u32[]{:S(2)}) async-start(bf16[48,13,128]{2,1,0:T(8,128)(2,1)} %shard_map.88), calls=%async_computation.1 | async-start | bytes 393216 | tf_op jit(solution)/shard_map/all_to_all | solution.py:360
  101.1 24.1 %collective-permute-start.3 = (bf16[768,768]{1,0:T(8,128)(2,1)}, bf16[768,768]{1,0:T(8,128)(2,1)}, u32[]{:S(2)}, u32[]{:S(2)}) collective-permute-start(bf16[768,768]{1,0:T(8,128)(2,1)} %get-tuple-element.11.own_hbm), channel_id=1, source_target_pairs={{0,1},{1,0},{2,3},{3,2},{4,5},{5,4},{6,7},{7,6},{8,9},{9,8},{10,11... | collective-permute-start | bytes 3538952 | tf_op jit(solution)/shard_map/ppermute | solution.py:362

commit v3 on v1

v3 whole, which is shorter than its diff:
```python
import functools
import jax
import jax.numpy as jnp
import numpy as np
from jax import lax
from jax.experimental import pallas as pl
from jax.experimental.pallas import tpu as pltpu
from jax.sharding import Mesh, PartitionSpec as P

SIZES = (4, 4, 4, 2, 3, 2)
NAMES = ("zh", "x", "yh", "yl", "zl", "c")
PAD = 128


VMEM = pl.BlockSpec(memory_space=pltpu.VMEM)


def parameters(mib):
    return pltpu.CompilerParams(vmem_limit_bytes=mib * 1024 * 1024)


def quotient(values, divisor, bound):
    shift = 16
    factor = -(-(1 << shift) // divisor)
    assert all(v * factor >> shift == v // divisor for v in range(bound))
    return (values * factor) >> shift


def source_rows(sizes, core):
    _, x, yh, yl, zl, _ = sizes
    stride = {"s": 1, "zl": 4, "yl": 4 * zl, "yh": 4 * zl * yl, "x": 4 * zl * yl * yh, "zh": 4 * zl * yl * yh * x}
    bound = 8 * x * yh * yl * zl
    left = lax.broadcasted_iota(jnp.int32, (bound, 1), 0)
    source = jnp.zeros((bound, 1), jnp.int32)
    for name, size in (("yh", yh), ("zh", 2), ("zl", zl), ("yl", yl), ("x", x), ("s", 2)):
        over = quotient(left, size, bound)
        source = source + (left - over * size) * stride[name]
        left, bound = over, bound // size
    return source + 2 * jnp.where(left == 0, 1 - core, core)


def split_pairs(values):
    lane = lax.broadcasted_iota(jnp.int32, (values[0].shape[0], PAD), 1)
    parts = jnp.zeros(lane.shape, jnp.float32)
    for s, value in enumerate(values):
        high = value.astype(jnp.bfloat16).astype(jnp.float32)
        parts = jnp.where(lane == 2 * s, high, parts)
        parts = jnp.where(lane == 2 * s + 1, value - high, parts)
    return parts


def join_pairs(parts):
    lane = lax.broadcasted_iota(jnp.int32, parts.shape, 1)
    return [
        jnp.sum(jnp.where((lane == 2 * s) | (lane == 2 * s + 1), parts, 0.0), axis=1, keepdims=True)
        for s in range(2)
    ]


def term_kernel(sizes, grad_ref, ctx_ref, send_ref, keep_ref, acc):
    span = grad_ref.shape[1] // 2
    width = ctx_ref.shape[1]
    blocks, part = send_ref.shape[0], send_ref.shape[1] // 2
    column = lax.broadcasted_iota(jnp.int32, (span, span), 1)
    pick = jnp.where(source_rows(sizes, lax.axis_index("c")) == column, 1.0, 0.0).astype(jnp.bfloat16)
    ones = jnp.ones((ctx_ref.shape[0], PAD), jnp.bfloat16)
    for step in range(2):
        moved = lax.dot_general(
            pick,
            grad_ref[:, step * span : (step + 1) * span],
            (((1,), (1,)), ((), ())),
            preferred_element_type=jnp.float32,
        ).astype(jnp.bfloat16)
        acc[step, :, :width] = jnp.dot(moved, ctx_ref[...], preferred_element_type=jnp.float32)
        acc[step, :, width:] = jnp.dot(moved, ones, preferred_element_type=jnp.float32)
    for side, out in enumerate((send_ref, keep_ref)):
        for block in range(blocks):
            sums = []
            for s in range(2):
                at = ((side * 2 + s) * blocks + block) * part
                both = jnp.concatenate([acc[0, at : at + part, :], acc[1, at : at + part, :]], axis=0)
                out[block, :, s * width : (s + 1) * width] = both[:, :width].astype(jnp.bfloat16)
                sums.append(both[:, width:])
            out[block, :, 2 * width :] = split_pairs(sums).astype(jnp.bfloat16)


def local_terms(sizes, grad_out, context):
    zh, x, yh, yl, zl, _ = sizes
    width = context.shape[1]
    piece = jax.ShapeDtypeStruct((x * yl * zl, zh * yh, 2 * width + PAD), jnp.bfloat16)
    return pl.pallas_call(
        functools.partial(term_kernel, sizes),
        out_shape=(piece, piece),
        in_specs=[VMEM] * 2,
        out_specs=(VMEM, VMEM),
        scratch_shapes=[pltpu.VMEM((2, grad_out.shape[1] // 2, width + PAD), jnp.float32)],
        compiler_params=parameters(40),
        cost_estimate=pl.CostEstimate(flops=4 * 10**9, bytes_accessed=5 * 10**6, transcendentals=0),
    )(grad_out, context)


def chip_kernel(got_ref, keep_ref, out_ref):
    wide = out_ref.shape[2] - PAD
    for block in range(out_ref.shape[0]):
        total = got_ref[block].astype(jnp.float32) + keep_ref[block].astype(jnp.float32)
        out_ref[block, :, :wide] = total[:, :wide].astype(out_ref.dtype)
        out_ref[block, :, wide:] = split_pairs(join_pairs(total[:, wide:])).astype(out_ref.dtype)


def chip_sum(got, keep):
    return pl.pallas_call(
        chip_kernel,
        out_shape=jax.ShapeDtypeStruct(got.shape, got.dtype),
        in_specs=[VMEM] * 2,
        out_specs=VMEM,
        compiler_params=parameters(16),
        cost_estimate=pl.CostEstimate(flops=10**6, bytes_accessed=4 * 10**6, transcendentals=0),
    )(got, keep)


def near_kernel(got_ref, *refs):
    sum_ref, wide = refs[-2:]
    for chunk in range(sum_ref.shape[1]):
        lanes = slice(chunk * PAD, (chunk + 1) * PAD)
        total = got_ref[0, :, lanes].astype(jnp.float32)
        for index in range(1, got_ref.shape[0]):
            total = total + got_ref[index, :, lanes].astype(jnp.float32)
        if chunk == sum_ref.shape[1] - 1:
            total = split_pairs(join_pairs(total))
        wide[:, chunk, :] = total
    sum_ref[...] = wide[...].astype(sum_ref.dtype)


def near_sum(got, held):
    _, rows, lanes = got.shape
    shape = (rows, lanes // PAD, PAD)
    return pl.pallas_call(
        near_kernel,
        out_shape=jax.ShapeDtypeStruct(shape, jnp.bfloat16),
        in_specs=[VMEM] + [pl.BlockSpec(memory_space=pl.ANY)] * len(held),
        out_specs=VMEM,
        scratch_shapes=[pltpu.VMEM(shape, jnp.float32)],
        compiler_params=parameters(16),
        cost_estimate=pl.CostEstimate(flops=10**6, bytes_accessed=2 * 10**6, transcendentals=0),
    )(got, *held)


def last_kernel(scale, far_ref, weight_ref, bias_ref):
    total = far_ref[0].astype(jnp.float32)
    for index in range(1, far_ref.shape[0]):
        total = total + far_ref[index].astype(jnp.float32)
    total = total * scale
    chunks = (total.shape[0] - 1) // 2
    for s in range(2):
        for chunk in range(chunks):
            at = s * chunks + chunk
            weight_ref[s : s + 1, chunk * PAD : (chunk + 1) * PAD] = total[at : at + 1, :]
    tail = total[2 * chunks : 2 * chunks + 1, :]
    lane = lax.broadcasted_iota(jnp.int32, (1, PAD), 1)
    for s in range(2):
        bias_ref[s] = jnp.sum(jnp.where((lane == 2 * s) | (lane == 2 * s + 1), tail, 0.0))


def last_sum(far, scale):
    width = (far.shape[1] - 1) // 2 * PAD
    return pl.pallas_call(
        functools.partial(last_kernel, scale),
        out_shape=(jax.ShapeDtypeStruct((2, width), jnp.float32), jax.ShapeDtypeStruct((2,), jnp.float32)),
        in_specs=[VMEM],
        out_specs=(pl.BlockSpec((2, width), lambda: (0, 0)), pl.BlockSpec(memory_space=pltpu.SMEM)),
        compiler_params=parameters(16),
        cost_estimate=pl.CostEstimate(flops=10**5, bytes_accessed=2 * 10**5, transcendentals=0),
    )(far)


def ctx_kernel(chips, grad_ref, *refs):
    held, out_ref = refs[:-1], refs[-1]
    chip, core = lax.axis_index("zl"), lax.axis_index("c")
    rows = held[0].shape[0]
    total = None
    for slot, block in enumerate(held):
        owner = lax.rem(chip + chips - slot % chips, chips)
        side = core if slot < chips else 1 - core
        at = pl.multiple_of((2 * owner + side) * rows, rows)
        product = jnp.dot(grad_ref[:, pl.ds(at, rows)], block[...], preferred_element_type=jnp.float32)
        total = product if total is None else total + product
    out_ref[...] = total.astype(out_ref.dtype)


def ctx_product(chips, grad_out, held):
    tokens, depth = grad_out.shape
    width = held[0].shape[1]
    steps = 2
    return pl.pallas_call(
        functools.partial(ctx_kernel, chips),
        out_shape=jax.ShapeDtypeStruct((tokens, width), jnp.bfloat16),
        grid=(steps,),
        in_specs=[pl.BlockSpec((tokens // steps, depth), lambda i: (i, 0))] + [VMEM] * len(held),
        out_specs=pl.BlockSpec((tokens // steps, width), lambda i: (i, 0)),
        compiler_params=parameters(24),
        cost_estimate=pl.CostEstimate(flops=12 * 10**8, bytes_accessed=5 * 10**6, transcendentals=0),
    )(grad_out, *held)


def body(sizes, grad_out, context, codes, scales):
    count = int(np.prod(sizes))
    chips = sizes[4]
    ring = sizes[0] * chips
    swap = [(0, 1), (1, 0)]

    send, keep = local_terms(sizes, grad_out, context)
    got = lax.ppermute(send, "c", swap)
    block = (codes[0].astype(jnp.float32) * scales.astype(jnp.float32)).astype(jnp.bfloat16)
    held = [block]
    for back in range(1, chips):
        hop = back if back <= chips // 2 else back - chips
        held.append(lax.ppermute(block, ("zh", "zl"), [(i, (i + hop) % ring) for i in range(ring)]))
    held += [lax.ppermute(piece, "c", swap) for piece in held]

    near = lax.all_to_all(chip_sum(got, keep), ("x", "yl", "zl"), split_axis=0, concat_axis=0, tiled=True)
    near = near_sum(near, held[1:])
    far = lax.all_to_all(near, ("zh", "yh"), split_axis=0, concat_axis=0, tiled=True)
    weight_grad, bias_grad = last_sum(far, 1.0 / count)

    ctx_grad = ctx_product(chips, grad_out, held)
    return ctx_grad, weight_grad, bias_grad


def solution(mesh, sizes=SIZES):
    fine = Mesh(mesh.devices.reshape(sizes), NAMES)
    in_specs = (P(NAMES, None), P(NAMES, None), P(("zl", "c"), None, None), P(("zl", "c"), None))
    out_specs = (P(NAMES, None), P(NAMES, None), P(NAMES))
    return jax.shard_map(
        functools.partial(body, sizes), mesh=fine, in_specs=in_specs, out_specs=out_specs, check_vma=False
    )
```

time: 92.1 us -> 90 us (0.977)
  blocking collectives: 32.8 us -> 0 us
  starting transfers between devices: 23.9 us -> 46.3 us
  waiting for transfers between devices: 17.8 us -> 27.8 us
  Pallas kernels: 11.7 us -> 8.73 us
    all_to_all x1 -> x0, blocking collectives: 32.8 us -> none  [body(): lax.all_to_all(near, ('zh', 'yh', 'zl'), split_axis=0, concat_axis=0, til...]
    all_to_all x1 -> x2, starting transfers between devices: 13.2 us -> 27.2 us  [the longest x1 13.8 us: body(): lax.all_to_all(near, ('zh', 'yh'), split_axis=0, concat_axis=0, tiled=True)]
    all_to_all x1 -> x2, waiting for transfers between devices: 0.01 us -> 10.1 us  [the longest x1 10.1 us: body(): lax.all_to_all(near, ('zh', 'yh'), split_axis=0, concat_axis=0, tiled=True)]
    ppermute x3 -> x5, starting transfers between devices: 8.79 us -> 17.2 us  [the longest x2 11 us: body(): lax.ppermute(block, ('zh', 'zl'), [(i, (i + hop) % ring) for i in range(r...]
    pallas_call x2, Pallas kernels: 7.02 us -> 4.24 us  [the longest x1 3.37 us: local_terms(): pl.pallas_call(functools.partial(term_kernel, sizes), out_shape=(piece, p...]
    ppermute x3 -> x5, waiting for transfers between devices: 14.6 us -> 14.7 us  [the longest x2 13.4 us: body(): lax.ppermute(block, ('zh', 'zl'), [(i, (i + hop) % ring) for i in range(r...]
  transfers between devices with their start and end apart: 5 -> 8, of which waited for: 3 -> 4; matrix products, arithmetic and copies ran while one was open for 0% -> 0% of each run, Pallas kernels for 1% -> 3%
where the time goes in v3:
time: 90 us; the launch traced here: 89.4 us
  starting transfers between devices  46.3 us (51%)
  waiting for transfers between devices  27.8 us (31%)
  Pallas kernels  8.73 us (10%)
  local copies, waits for them, and re-layouts  5.68 us (6%)
    all_to_all x1, starting transfers between devices, body(): lax.all_to_all(near, ('zh', 'yh'), split_axis=0, concat_axis=0, tiled=True)  13.8 us
    ppermute x2, waiting for transfers between devices, body(): lax.ppermute(block, ('zh', 'zl'), [(i, (i + hop) % ring) for i in range(r...  13.4 us
    all_to_all x1, starting transfers between devices, body(): lax.all_to_all(chip_sum(got, keep), ('x', 'yl', 'zl'), split_axis=0, conc...  13.4 us
    ppermute x2, starting transfers between devices, body(): lax.ppermute(block, ('zh', 'zl'), [(i, (i + hop) % ring) for i in range(r...  11 us
    all_to_all x1, waiting for transfers between devices, body(): lax.all_to_all(near, ('zh', 'yh'), split_axis=0, concat_axis=0, tiled=True)  10.1 us
    ppermute x3, starting transfers between devices, body(): held += [lax.ppermute(piece, 'c', swap) for piece in held]  6.24 us
    unnamed x14, local copies, waits for them, and re-layouts  5.68 us
    pallas_call x1, Pallas kernels, local_terms(): pl.pallas_call(functools.partial(term_kernel, sizes), out_shape=(piece, p...  3.37 us
  transfers between devices with their start and end apart: 8, of which 4 were waited for; matrix products, arithmetic and copies ran while one was open for 0% of the time, Pallas kernels for 3%

profile of v3, /device:TPU:2, one launch (start us, length us, event | category | flops | bytes accessed | tf_op | source)
XLA Modules:
  0.0 89.4 jit_solution(3982210075462499635)
XLA Ops:
  0.6 1.4 %copy-done.2 = bf16[512,1536]{1,0:T(8,128)(2,1)S(1)} copy-done((bf16[512,1536]{1,0:T(8,128)(2,1)S(1)}, bf16[512,1536]{1,0:T(8,128)(2,1)}, u32[]{:S(2)}) %copy-start.2) | copy-done | bytes 1572888
  2.0 1.1 %copy-done.4 = bf16[512,768]{1,0:T(8,128)(2,1)S(1)} copy-done((bf16[512,768]{1,0:T(8,128)(2,1)S(1)}, bf16[512,768]{1,0:T(8,128)(2,1)}, u32[]{:S(2)}) %copy-start.4) | copy-done | bytes 786456
  3.2 3.4 %shard_map.68 = (bf16[24,16,1664]{2,1,0:T(8,128)(2,1)S(1)}, bf16[24,16,1664]{2,1,0:T(8,128)(2,1)S(1)}) custom-call(bf16[512,1536]{1,0:T(8,128)(2,1)S(1)} %copy-done.2, bf16[512,768]{1,0:T(8,128)(2,1)S(1)} %copy-done.4), custom_call_target="tpu_custom_call" | custom-call | flops 4000000000 | bytes 5000000 | tf_op jit(solution)/shard_map/pallas_call | solution.py:91
  6.5 1.9 %collective-permute-start.5 = (bf16[24,16,1664]{2,1,0:T(8,128)(2,1)S(1)}, bf16[24,16,1664]{2,1,0:T(8,128)(2,1)S(1)}, u32[]{:S(2)}, u32[]{:S(2)}) collective-permute-start(bf16[24,16,1664]{2,1,0:T(8,128)(2,1)S(1)} %get-tuple-element.7), channel_id=1, source_target_pairs={{0,1},{1,0},{2,3},{3,2},{4,5},{5,4},{6,7},{7,6},{8,9},{9,8},{10,11... | collective-permute-start | bytes 3833864 | tf_op jit(solution)/shard_map/ppermute | solution.py:212
  8.5 3.0 %collective-permute-done.5.got_ref = bf16[24,16,1664]{2,1,0:T(8,128)(2,1)S(1)} collective-permute-done((bf16[24,16,1664]{2,1,0:T(8,128)(2,1)S(1)}, bf16[24,16,1664]{2,1,0:T(8,128)(2,1)S(1)}, u32[]{:S(2)}, u32[]{:S(2)}) %collective-permute-start.5) | collective-permute-done | bytes 1277984 | tf_op jit(solution)/shard_map/ppermute | solution.py:212
  11.4 1.5 %shard_map.69 = bf16[24,16,1664]{2,1,0:T(8,128)(2,1)} custom-call(bf16[24,16,1664]{2,1,0:T(8,128)(2,1)S(1)} %collective-permute-done.5.got_ref, bf16[24,16,1664]{2,1,0:T(8,128)(2,1)S(1)} %get-tuple-element.8.keep_ref), custom_call_target="tpu_custom_call" | custom-call | flops 1000000 | bytes 4000000 | tf_op jit(solution)/shard_map/pallas_call | solution.py:111
  12.9 13.4 %all-to-all-start = ((bf16[24,16,1664]{2,1,0:T(8,128)(2,1)}), bf16[24,16,1664]{2,1,0:T(8,128)(2,1)S(1)}, u32[]{:S(2)}, u32[]{:S(2)}) async-start(bf16[24,16,1664]{2,1,0:T(8,128)(2,1)} %shard_map.69), calls=%async_computation | async-start | bytes 2555904 | tf_op jit(solution)/shard_map/all_to_all | solution.py:220
  26.3 0.1 fusion.refs_0_
  26.4 3.4 %collective-permute-start = (bf16[256,768]{1,0:T(8,128)(2,1)S(1)}, bf16[256,768]{1,0:T(8,128)(2,1)S(1)}, u32[]{:S(2)}, u32[]{:S(2)}) collective-permute-start(bf16[256,768]{1,0:T(8,128)(2,1)S(1)} %fusion.refs_0_), channel_id=1, source_target_pairs={{0,2},{2,4},{4,192},{192,194},{194,196},{196,384},{384,386},{386,3... | collective-permute-start | bytes 1179656 | tf_op jit(solution)/shard_map/ppermute | solution.py:217
  29.8 7.6 %collective-permute-start.1 = (bf16[256,768]{1,0:T(8,128)(2,1)S(1)}, bf16[256,768]{1,0:T(8,128)(2,1)S(1)}, u32[]{:S(2)}, u32[]{:S(2)}) collective-permute-start(bf16[256,768]{1,0:T(8,128)(2,1)S(1)} %fusion.refs_0_), channel_id=1, source_target_pairs={{0,580},{2,0},{4,2},{192,4},{194,192},{196,194},{384,196},{386,384... | collective-permute-start | bytes 1179656 | tf_op jit(solution)/shard_map/ppermute | solution.py:217
  37.4 1.9 %collective-permute-start.2 = (bf16[256,768]{1,0:T(8,128)(2,1)S(1)}, bf16[256,768]{1,0:T(8,128)(2,1)S(1)}, u32[]{:S(2)}, u32[]{:S(2)}) collective-permute-start(bf16[256,768]{1,0:T(8,128)(2,1)S(1)} %fusion.refs_0_), channel_id=1, source_target_pairs={{0,1},{1,0},{2,3},{3,2},{4,5},{5,4},{6,7},{7,6},{8,9},{9,8},{10,11... | collective-permute-start | bytes 1179656 | tf_op jit(solution)/shard_map/ppermute | solution.py:218
  39.4 0.0 copy-start
  39.4 0.7 copy-done
  40.1 13.4 %collective-permute-done.refs_1_.refs_0_ = bf16[256,768]{1,0:T(8,128)(2,1)S(1)} collective-permute-done((bf16[256,768]{1,0:T(8,128)(2,1)S(1)}, bf16[256,768]{1,0:T(8,128)(2,1)S(1)}, u32[]{:S(2)}, u32[]{:S(2)}) %collective-permute-start) | collective-permute-done | bytes 393248 | tf_op jit(solution)/shard_map/ppermute | solution.py:217
  53.5 1.9 %collective-permute-start.3 = (bf16[256,768]{1,0:T(8,128)(2,1)S(1)}, bf16[256,768]{1,0:T(8,128)(2,1)S(1)}, u32[]{:S(2)}, u32[]{:S(2)}) collective-permute-start(bf16[256,768]{1,0:T(8,128)(2,1)S(1)} %collective-permute-done.refs_1_.refs_0_), channel_id=1, source_target_pairs={{0,1},{1,0},{2,3},{3,2},{4,5},{5,4},{6,7},{7,6},{8,9},{9,8},{10,11... | collective-permute-start | bytes 1179656 | tf_op jit(solution)/shard_map/ppermute | solution.py:218
  55.4 2.4 %collective-permute-start.4 = (bf16[256,768]{1,0:T(8,128)(2,1)S(1)}, bf16[256,768]{1,0:T(8,128)(2,1)S(1)}, u32[]{:S(2)}, u32[]{:S(2)}) collective-permute-start(bf16[256,768]{1,0:T(8,128)(2,1)S(1)} %collective-permute-done.1.refs_2_.refs_1_), channel_id=1, source_target_pairs={{0,1},{1,0},{2,3},{3,2},{4,5},{5,4},{6,7},{7,6},{8,9},{9,8},{10,11... | collective-permute-start | bytes 1179656 | tf_op jit(solution)/shard_map/ppermute | solution.py:218
  57.8 1.3 %collective-permute-done.4.refs_5_.refs_4_ = bf16[256,768]{1,0:T(8,128)(2,1)S(1)} collective-permute-done((bf16[256,768]{1,0:T(8,128)(2,1)S(1)}, bf16[256,768]{1,0:T(8,128)(2,1)S(1)}, u32[]{:S(2)}, u32[]{:S(2)}) %collective-permute-start.4) | collective-permute-done | bytes 393248 | tf_op jit(solution)/shard_map/ppermute | solution.py:218
  59.2 0.9 shard_map.70
  60.0 13.8 %all-to-all-start.1 = ((bf16[16,13,128]{2,1,0:T(8,128)(2,1)}), bf16[16,13,128]{2,1,0:T(8,128)(2,1)S(1)}, u32[]{:S(2)}, u32[]{:S(2)}) async-start(bf16[16,13,128]{2,1,0:T(8,128)(2,1)} %shard_map.70), calls=%async_computation.1 | async-start | bytes 131072 | tf_op jit(solution)/shard_map/all_to_all | solution.py:222
  73.9 1.0 %copy-done.1 = bf16[256,768]{1,0:T(8,128)(2,1)S(1)} copy-done((bf16[256,768]{1,0:T(8,128)(2,1)S(1)}, bf16[256,768]{1,0:T(8,128)(2,1)}, u32[]{:S(2)}) %copy-start.1) | copy-done | bytes 393240
  74.9 1.4 %copy-done.3 = bf16[512,1536]{1,0:T(8,128)(2,1)S(1)} copy-done((bf16[512,1536]{1,0:T(8,128)(2,1)S(1)}, bf16[512,1536]{1,0:T(8,128)(2,1)}, u32[]{:S(2)}) %copy-start.3) | copy-done | bytes 1572888
  76.3 2.3 %shard_map.67 = bf16[512,768]{1,0:T(8,128)(2,1)} custom-call(bf16[512,1536]{1,0:T(8,128)(2,1)S(1)} %copy-done.3, bf16[256,768]{1,0:T(8,128)(2,1)S(1)} %copy-done.1, bf16[256,768]{1,0:T(8,128)(2,1)S(1)} %collective-permute-done.refs_1_.refs_0_, bf16[256,768]{1,0:T(8,128)(2,1)S(1)} %collective-permute-done.1.refs_2_.refs_1_, ...), custom_call_target="tpu_custom_call" | custom-call | flops 1200000000 | bytes 5000000 | tf_op jit(solution)/shard_map/pallas_call | solution.py:194
  78.6 10.1 %all-to-all-done.1.far_ref = bf16[16,13,128]{2,1,0:T(8,128)(2,1)S(1)} async-done(((bf16[16,13,128]{2,1,0:T(8,128)(2,1)}), bf16[16,13,128]{2,1,0:T(8,128)(2,1)S(1)}, u32[]{:S(2)}, u32[]{:S(2)}) %all-to-all-start.1) | async-done | bytes 53280 | tf_op jit(solution)/shard_map/all_to_all | solution.py:222
  88.7 0.7 shard_map.71
  (13 shorter events, 0.0 us)
Async XLA Ops:
  0.6 1.4 %copy-start.2 = (bf16[512,1536]{1,0:T(8,128)(2,1)S(1)}, bf16[512,1536]{1,0:T(8,128)(2,1)}, u32[]{:S(2)}) copy-start(bf16[512,1536]{1,0:T(8,128)(2,1)} %grad_ref.3) | copy-start | bytes 4718596
  2.0 1.1 %copy-start.4 = (bf16[512,768]{1,0:T(8,128)(2,1)S(1)}, bf16[512,768]{1,0:T(8,128)(2,1)}, u32[]{:S(2)}) copy-start(bf16[512,768]{1,0:T(8,128)(2,1)} %ctx_ref.1) | copy-start | bytes 2359300
  6.5 4.9 %collective-permute-start.5 = (bf16[24,16,1664]{2,1,0:T(8,128)(2,1)S(1)}, bf16[24,16,1664]{2,1,0:T(8,128)(2,1)S(1)}, u32[]{:S(2)}, u32[]{:S(2)}) collective-permute-start(bf16[24,16,1664]{2,1,0:T(8,128)(2,1)S(1)} %get-tuple-element.7), channel_id=1, source_target_pairs={{0,1},{1,0},{2,3},{3,2},{4,5},{5,4},{6,7},{7,6},{8,9},{9,8},{10,11... | collective-permute-start | bytes 3833864 | tf_op jit(solution)/shard_map/ppermute | solution.py:212
  12.9 13.4 %copy-start.6 = (bf16[1,768]{1,0:T(2,128)(2,1)S(1)}, bf16[1,768]{1,0:T(2,128)(2,1)}, u32[]{:S(2)}) copy-start(bf16[1,768]{1,0:T(2,128)(2,1)} %param.7) | copy-start | bytes 4612
  12.9 13.4 %copy-start.5 = (bf16[1,256,768]{2,1,0:T(8,128)(2,1)S(1)}, bf16[1,256,768]{2,1,0:T(8,128)(2,1)}, u32[]{:S(2)}) copy-start(bf16[1,256,768]{2,1,0:T(8,128)(2,1)} %param.6) | copy-start | bytes 1179652
  12.9 46.2 %all-to-all-start = ((bf16[24,16,1664]{2,1,0:T(8,128)(2,1)}), bf16[24,16,1664]{2,1,0:T(8,128)(2,1)S(1)}, u32[]{:S(2)}, u32[]{:S(2)}) async-start(bf16[24,16,1664]{2,1,0:T(8,128)(2,1)} %shard_map.69), calls=%async_computation | async-start | bytes 2555904 | tf_op jit(solution)/shard_map/all_to_all | solution.py:220
  26.4 27.1 %collective-permute-start = (bf16[256,768]{1,0:T(8,128)(2,1)S(1)}, bf16[256,768]{1,0:T(8,128)(2,1)S(1)}, u32[]{:S(2)}, u32[]{:S(2)}) collective-permute-start(bf16[256,768]{1,0:T(8,128)(2,1)S(1)} %fusion.refs_0_), channel_id=1, source_target_pairs={{0,2},{2,4},{4,192},{192,194},{194,196},{196,384},{384,386},{386,3... | collective-permute-start | bytes 1179656 | tf_op jit(solution)/shard_map/ppermute | solution.py:217
  29.8 25.6 %collective-permute-start.1 = (bf16[256,768]{1,0:T(8,128)(2,1)S(1)}, bf16[256,768]{1,0:T(8,128)(2,1)S(1)}, u32[]{:S(2)}, u32[]{:S(2)}) collective-permute-start(bf16[256,768]{1,0:T(8,128)(2,1)S(1)} %fusion.refs_0_), channel_id=1, source_target_pairs={{0,580},{2,0},{4,2},{192,4},{194,192},{196,194},{384,196},{386,384... | collective-permute-start | bytes 1179656 | tf_op jit(solution)/shard_map/ppermute | solution.py:217
  37.4 20.4 %collective-permute-start.2 = (bf16[256,768]{1,0:T(8,128)(2,1)S(1)}, bf16[256,768]{1,0:T(8,128)(2,1)S(1)}, u32[]{:S(2)}, u32[]{:S(2)}) collective-permute-start(bf16[256,768]{1,0:T(8,128)(2,1)S(1)} %fusion.refs_0_), channel_id=1, source_target_pairs={{0,1},{1,0},{2,3},{3,2},{4,5},{5,4},{6,7},{7,6},{8,9},{9,8},{10,11... | collective-permute-start | bytes 1179656 | tf_op jit(solution)/shard_map/ppermute | solution.py:218
  39.4 0.7 copy-start
  53.5 4.4 %collective-permute-start.3 = (bf16[256,768]{1,0:T(8,128)(2,1)S(1)}, bf16[256,768]{1,0:T(8,128)(2,1)S(1)}, u32[]{:S(2)}, u32[]{:S(2)}) collective-permute-start(bf16[256,768]{1,0:T(8,128)(2,1)S(1)} %collective-permute-done.refs_1_.refs_0_), channel_id=1, source_target_pairs={{0,1},{1,0},{2,3},{3,2},{4,5},{5,4},{6,7},{7,6},{8,9},{9,8},{10,11... | collective-permute-start | bytes 1179656 | tf_op jit(solution)/shard_map/ppermute | solution.py:218
  55.4 3.7 %collective-permute-start.4 = (bf16[256,768]{1,0:T(8,128)(2,1)S(1)}, bf16[256,768]{1,0:T(8,128)(2,1)S(1)}, u32[]{:S(2)}, u32[]{:S(2)}) collective-permute-start(bf16[256,768]{1,0:T(8,128)(2,1)S(1)} %collective-permute-done.1.refs_2_.refs_1_), channel_id=1, source_target_pairs={{0,1},{1,0},{2,3},{3,2},{4,5},{5,4},{6,7},{7,6},{8,9},{9,8},{10,11... | collective-permute-start | bytes 1179656 | tf_op jit(solution)/shard_map/ppermute | solution.py:218
  60.0 28.7 %all-to-all-start.1 = ((bf16[16,13,128]{2,1,0:T(8,128)(2,1)}), bf16[16,13,128]{2,1,0:T(8,128)(2,1)S(1)}, u32[]{:S(2)}, u32[]{:S(2)}) async-start(bf16[16,13,128]{2,1,0:T(8,128)(2,1)} %shard_map.70), calls=%async_computation.1 | async-start | bytes 131072 | tf_op jit(solution)/shard_map/all_to_all | solution.py:222
  73.9 1.0 %copy-start.1 = (bf16[256,768]{1,0:T(8,128)(2,1)S(1)}, bf16[256,768]{1,0:T(8,128)(2,1)}, u32[]{:S(2)}) copy-start(bf16[256,768]{1,0:T(8,128)(2,1)} %copy-done) | copy-start | bytes 1179652
  74.8 1.4 %copy-start.3 = (bf16[512,1536]{1,0:T(8,128)(2,1)S(1)}, bf16[512,1536]{1,0:T(8,128)(2,1)}, u32[]{:S(2)}) copy-start(bf16[512,1536]{1,0:T(8,128)(2,1)} %grad_ref.3) | copy-start | bytes 4718596

commit v4 on v3

--- a/solution.py
+++ b/solution.py
@@ -32,7 +32,7 @@
     bound = 8 * x * yh * yl * zl
     left = lax.broadcasted_iota(jnp.int32, (bound, 1), 0)
     source = jnp.zeros((bound, 1), jnp.int32)
-    for name, size in (("yh", yh), ("zh", 2), ("zl", zl), ("yl", yl), ("x", x), ("s", 2)):
+    for name, size in (("zl", zl), ("yh", yh), ("zh", 2), ("yl", yl), ("x", x), ("s", 2)):
         over = quotient(left, size, bound)
         source = source + (left - over * size) * stride[name]
         left, bound = over, bound // size
@@ -87,7 +87,7 @@
 def local_terms(sizes, grad_out, context):
     zh, x, yh, yl, zl, _ = sizes
     width = context.shape[1]
-    piece = jax.ShapeDtypeStruct((x * yl * zl, zh * yh, 2 * width + PAD), jnp.bfloat16)
+    piece = jax.ShapeDtypeStruct((x * yl, zh * yh * zl, 2 * width + PAD), jnp.bfloat16)
     return pl.pallas_call(
         functools.partial(term_kernel, sizes),
         out_shape=(piece, piece),
@@ -217,9 +217,9 @@
         held.append(lax.ppermute(block, ("zh", "zl"), [(i, (i + hop) % ring) for i in range(ring)]))
     held += [lax.ppermute(piece, "c", swap) for piece in held]
 
-    near = lax.all_to_all(chip_sum(got, keep), ("x", "yl", "zl"), split_axis=0, concat_axis=0, tiled=True)
+    near = lax.all_to_all(chip_sum(got, keep), ("x", "yl"), split_axis=0, concat_axis=0, tiled=True)
     near = near_sum(near, held[1:])
-    far = lax.all_to_all(near, ("zh", "yh"), split_axis=0, concat_axis=0, tiled=True)
+    far = lax.all_to_all(near, ("zh", "yh", "zl"), split_axis=0, concat_axis=0, tiled=True)
     weight_grad, bias_grad = last_sum(far, 1.0 / count)
 
     ctx_grad = ctx_product(chips, grad_out, held)

time: 90 us -> 88.5 us (0.983)
  local copies, waits for them, and re-layouts: 5.68 us -> 16.2 us
  waiting for transfers between devices: 27.8 us -> 20.3 us
  starting transfers between devices: 46.3 us -> 41.2 us
    unnamed x14 -> x40, local copies, waits for them, and re-layouts: 5.68 us -> 16.2 us
    ppermute x2, waiting for transfers between devices: 13.4 us -> 4.99 us  [body(): lax.ppermute(block, ('zh', 'zl'), [(i, (i + hop) % ring) for i in range(r...]
    all_to_all x2, starting transfers between devices: 27.2 us -> 23.6 us  [the longest x1 13.2 us: body(): lax.all_to_all(chip_sum(got, keep), ('x', 'yl'), split_axis=0, concat_axi...]
    all_to_all x2, waiting for transfers between devices: 10.1 us -> 12.3 us  [the longest x1 12.3 us: body(): lax.all_to_all(near, ('zh', 'yh', 'zl'), split_axis=0, concat_axis=0, til...]
    ppermute x2, starting transfers between devices: 11 us -> 9.46 us  [body(): lax.ppermute(block, ('zh', 'zl'), [(i, (i + hop) % ring) for i in range(r...]
    ppermute x3, waiting for transfers between devices: 1.31 us -> 0.01 us  [body(): held += [lax.ppermute(piece, 'c', swap) for piece in held]]
  transfers between devices with their start and end apart: 8 -> 8, of which waited for: 4 -> 3; matrix products, arithmetic and copies ran while one was open for 0% -> 0% of each run, Pallas kernels for 3% -> 3%
where the time goes in v4:
time: 88.5 us; the launch traced here: 87.6 us
  starting transfers between devices  41.2 us (47%)
  waiting for transfers between devices  20.3 us (23%)
  local copies, waits for them, and re-layouts  16.2 us (18%)
  Pallas kernels  9.09 us (10%)
    unnamed x40, local copies, waits for them, and re-layouts  16.2 us
    all_to_all x1, starting transfers between devices, body(): lax.all_to_all(chip_sum(got, keep), ('x', 'yl'), split_axis=0, concat_axi...  13.2 us
    all_to_all x1, waiting for transfers between devices, body(): lax.all_to_all(near, ('zh', 'yh', 'zl'), split_axis=0, concat_axis=0, til...  12.3 us
    all_to_all x1, starting transfers between devices, body(): lax.all_to_all(near, ('zh', 'yh', 'zl'), split_axis=0, concat_axis=0, til...  10.4 us
    ppermute x2, starting transfers between devices, body(): lax.ppermute(block, ('zh', 'zl'), [(i, (i + hop) % ring) for i in range(r...  9.46 us
    ppermute x3, starting transfers between devices, body(): held += [lax.ppermute(piece, 'c', swap) for piece in held]  6.22 us
    ppermute x2, waiting for transfers between devices, body(): lax.ppermute(block, ('zh', 'zl'), [(i, (i + hop) % ring) for i in range(r...  4.99 us
    pallas_call x1, Pallas kernels, local_terms(): pl.pallas_call(functools.partial(term_kernel, sizes), out_shape=(piece, p...  3.37 us
  transfers between devices with their start and end apart: 8, of which 3 were waited for; matrix products, arithmetic and copies ran while one was open for 0% of the time, Pallas kernels for 3%

profile of v4, /device:TPU:2, one launch (start us, length us, event | category | flops | bytes accessed | tf_op | source)
XLA Modules:
  0.0 87.6 jit_solution(15961435149236274709)
XLA Ops:
  0.6 1.4 %copy-done = bf16[512,1536]{1,0:T(8,128)(2,1)S(1)} copy-done((bf16[512,1536]{1,0:T(8,128)(2,1)S(1)}, bf16[512,1536]{1,0:T(8,128)(2,1)}, u32[]{:S(2)}) %copy-start) | copy-done | bytes 1572888
  2.0 1.1 %copy-done.17 = bf16[512,768]{1,0:T(8,128)(2,1)S(1)} copy-done((bf16[512,768]{1,0:T(8,128)(2,1)S(1)}, bf16[512,768]{1,0:T(8,128)(2,1)}, u32[]{:S(2)}) %copy-start.17) | copy-done | bytes 786456
  3.2 3.4 %shard_map.68 = (bf16[8,48,1664]{2,1,0:T(8,128)(2,1)S(1)}, bf16[8,48,1664]{2,1,0:T(8,128)(2,1)S(1)}) custom-call(bf16[512,1536]{1,0:T(8,128)(2,1)S(1)} %copy-done, bf16[512,768]{1,0:T(8,128)(2,1)S(1)} %copy-done.17), custom_call_target="tpu_custom_call" | custom-call | flops 4000000000 | bytes 5000000 | tf_op jit(solution)/shard_map/pallas_call | solution.py:91
  6.5 1.9 %collective-permute-start.5 = (bf16[8,48,1664]{2,1,0:T(8,128)(2,1)S(1)}, bf16[8,48,1664]{2,1,0:T(8,128)(2,1)S(1)}, u32[]{:S(2)}, u32[]{:S(2)}) collective-permute-start(bf16[8,48,1664]{2,1,0:T(8,128)(2,1)S(1)} %get-tuple-element.7), channel_id=1, source_target_pairs={{0,1},{1,0},{2,3},{3,2},{4,5},{5,4},{6,7},{7,6},{8,9},{9,8},{10,11... | collective-permute-start | bytes 3833864 | tf_op jit(solution)/shard_map/ppermute | solution.py:212
  8.5 3.0 %collective-permute-done.5.got_ref = bf16[8,48,1664]{2,1,0:T(8,128)(2,1)S(1)} collective-permute-done((bf16[8,48,1664]{2,1,0:T(8,128)(2,1)S(1)}, bf16[8,48,1664]{2,1,0:T(8,128)(2,1)S(1)}, u32[]{:S(2)}, u32[]{:S(2)}) %collective-permute-start.5) | collective-permute-done | bytes 1277984 | tf_op jit(solution)/shard_map/ppermute | solution.py:212
  11.4 1.6 %shard_map.69 = bf16[8,48,1664]{2,1,0:T(8,128)(2,1)} custom-call(bf16[8,48,1664]{2,1,0:T(8,128)(2,1)S(1)} %collective-permute-done.5.got_ref, bf16[8,48,1664]{2,1,0:T(8,128)(2,1)S(1)} %get-tuple-element.8.keep_ref), custom_call_target="tpu_custom_call" | custom-call | flops 1000000 | bytes 4000000 | tf_op jit(solution)/shard_map/pallas_call | solution.py:111
  13.0 13.2 %all-to-all-start = ((bf16[8,48,1664]{2,1,0:T(8,128)(2,1)}), bf16[8,48,1664]{2,1,0:T(8,128)(2,1)S(1)}, u32[]{:S(2)}, u32[]{:S(2)}) async-start(bf16[8,48,1664]{2,1,0:T(8,128)(2,1)} %shard_map.69), calls=%async_computation | async-start | bytes 2555904 | tf_op jit(solution)/shard_map/all_to_all | solution.py:220
  26.3 2.1 %collective-permute-start = (bf16[256,768]{1,0:T(8,128)(2,1)S(1)}, bf16[256,768]{1,0:T(8,128)(2,1)S(1)}, u32[]{:S(2)}, u32[]{:S(2)}) collective-permute-start(bf16[256,768]{1,0:T(8,128)(2,1)S(1)} %fusion.refs_0_), channel_id=1, source_target_pairs={{0,2},{2,4},{4,192},{192,194},{194,196},{196,384},{384,386},{386,3... | collective-permute-start | bytes 1179656 | tf_op jit(solution)/shard_map/ppermute | solution.py:217
  28.4 7.4 %collective-permute-start.1 = (bf16[256,768]{1,0:T(8,128)(2,1)S(1)}, bf16[256,768]{1,0:T(8,128)(2,1)S(1)}, u32[]{:S(2)}, u32[]{:S(2)}) collective-permute-start(bf16[256,768]{1,0:T(8,128)(2,1)S(1)} %fusion.refs_0_), channel_id=1, source_target_pairs={{0,580},{2,0},{4,2},{192,4},{194,192},{196,194},{384,196},{386,384... | collective-permute-start | bytes 1179656 | tf_op jit(solution)/shard_map/ppermute | solution.py:217
  35.8 1.9 %collective-permute-start.2 = (bf16[256,768]{1,0:T(8,128)(2,1)S(1)}, bf16[256,768]{1,0:T(8,128)(2,1)S(1)}, u32[]{:S(2)}, u32[]{:S(2)}) collective-permute-start(bf16[256,768]{1,0:T(8,128)(2,1)S(1)} %fusion.refs_0_), channel_id=1, source_target_pairs={{0,1},{1,0},{2,3},{3,2},{4,5},{5,4},{6,7},{7,6},{8,9},{9,8},{10,11... | collective-permute-start | bytes 1179656 | tf_op jit(solution)/shard_map/ppermute | solution.py:218
  37.7 5.0 %collective-permute-done.refs_1_.refs_0_ = bf16[256,768]{1,0:T(8,128)(2,1)S(1)} collective-permute-done((bf16[256,768]{1,0:T(8,128)(2,1)S(1)}, bf16[256,768]{1,0:T(8,128)(2,1)S(1)}, u32[]{:S(2)}, u32[]{:S(2)}) %collective-permute-start) | collective-permute-done | bytes 393248 | tf_op jit(solution)/shard_map/ppermute | solution.py:217
  42.7 1.9 %collective-permute-start.3 = (bf16[256,768]{1,0:T(8,128)(2,1)S(1)}, bf16[256,768]{1,0:T(8,128)(2,1)S(1)}, u32[]{:S(2)}, u32[]{:S(2)}) collective-permute-start(bf16[256,768]{1,0:T(8,128)(2,1)S(1)} %collective-permute-done.refs_1_.refs_0_), channel_id=1, source_target_pairs={{0,1},{1,0},{2,3},{3,2},{4,5},{5,4},{6,7},{7,6},{8,9},{9,8},{10,11... | collective-permute-start | bytes 1179656 | tf_op jit(solution)/shard_map/ppermute | solution.py:218
  45.4 2.4 %collective-permute-start.4 = (bf16[256,768]{1,0:T(8,128)(2,1)S(1)}, bf16[256,768]{1,0:T(8,128)(2,1)S(1)}, u32[]{:S(2)}, u32[]{:S(2)}) collective-permute-start(bf16[256,768]{1,0:T(8,128)(2,1)S(1)} %collective-permute-done.1.refs_2_.refs_1_), channel_id=1, source_target_pairs={{0,1},{1,0},{2,3},{3,2},{4,5},{5,4},{6,7},{7,6},{8,9},{9,8},{10,11... | collective-permute-start | bytes 1179656 | tf_op jit(solution)/shard_map/ppermute | solution.py:218
  50.8 1.0 %copy-done.3 = bf16[256,768]{1,0:T(8,128)(2,1)S(1)} copy-done((bf16[256,768]{1,0:T(8,128)(2,1)S(1)}, bf16[256,768]{1,0:T(8,128)(2,1)}, u32[]{:S(2)}) %copy-start.3) | copy-done | bytes 393240
  51.8 1.0 %copy-done.6 = bf16[256,768]{1,0:T(8,128)(2,1)S(1)} copy-done((bf16[256,768]{1,0:T(8,128)(2,1)S(1)}, bf16[256,768]{1,0:T(8,128)(2,1)}, u32[]{:S(2)}) %copy-start.6) | copy-done | bytes 393240
  52.8 1.0 %copy-done.9 = bf16[256,768]{1,0:T(8,128)(2,1)S(1)} copy-done((bf16[256,768]{1,0:T(8,128)(2,1)S(1)}, bf16[256,768]{1,0:T(8,128)(2,1)}, u32[]{:S(2)}) %copy-start.9) | copy-done | bytes 393240
  53.8 1.0 %copy-done.12 = bf16[256,768]{1,0:T(8,128)(2,1)S(1)} copy-done((bf16[256,768]{1,0:T(8,128)(2,1)S(1)}, bf16[256,768]{1,0:T(8,128)(2,1)}, u32[]{:S(2)}) %copy-start.12) | copy-done | bytes 393240
  54.8 1.0 %copy-done.15 = bf16[256,768]{1,0:T(8,128)(2,1)S(1)} copy-done((bf16[256,768]{1,0:T(8,128)(2,1)S(1)}, bf16[256,768]{1,0:T(8,128)(2,1)}, u32[]{:S(2)}) %copy-start.15) | copy-done | bytes 393240
  55.8 1.1 %shard_map.70 = bf16[48,13,128]{2,1,0:T(8,128)(2,1)} custom-call(bf16[8,48,1664]{2,1,0:T(8,128)(2,1)S(1)} %all-to-all-done.got_ref, bf16[256,768]{1,0:T(8,128)(2,1)S(1)} %copy-done.3, bf16[256,768]{1,0:T(8,128)(2,1)S(1)} %copy-done.6, bf16[256,768]{1,0:T(8,128)(2,1)S(1)} %copy-done.9, bf16[256,768]{1,0:T(8,128)(2,1)S(1)} %copy-done.12, ...), custom_call_target="tpu_custom_call" | custom-call | flops 1000000 | bytes 2000000 | tf_op jit(solution)/shard_map/pallas_call | solution.py:137
  56.9 10.4 %all-to-all-start.1 = ((bf16[48,13,128]{2,1,0:T(8,128)(2,1)}), bf16[48,13,128]{2,1,0:T(8,128)(2,1)S(1)}, u32[]{:S(2)}, u32[]{:S(2)}) async-start(bf16[48,13,128]{2,1,0:T(8,128)(2,1)} %shard_map.70), calls=%async_computation.1 | async-start | bytes 393216 | tf_op jit(solution)/shard_map/all_to_all | solution.py:222
  68.3 1.0 %copy-done.7 = bf16[256,768]{1,0:T(8,128)(2,1)S(1)} copy-done((bf16[256,768]{1,0:T(8,128)(2,1)S(1)}, bf16[256,768]{1,0:T(8,128)(2,1)}, u32[]{:S(2)}) %copy-start.7) | copy-done | bytes 393240
  69.3 1.0 %copy-done.10 = bf16[256,768]{1,0:T(8,128)(2,1)S(1)} copy-done((bf16[256,768]{1,0:T(8,128)(2,1)S(1)}, bf16[256,768]{1,0:T(8,128)(2,1)}, u32[]{:S(2)}) %copy-start.10) | copy-done | bytes 393240
  72.3 2.3 %shard_map.67 = bf16[512,768]{1,0:T(8,128)(2,1)} custom-call(bf16[512,1536]{1,0:T(8,128)(2,1)S(1)} %copy-done.1, bf16[256,768]{1,0:T(8,128)(2,1)S(1)} %fusion.refs_0_, bf16[256,768]{1,0:T(8,128)(2,1)S(1)} %copy-done.4, bf16[256,768]{1,0:T(8,128)(2,1)S(1)} %copy-done.7, bf16[256,768]{1,0:T(8,128)(2,1)S(1)} %copy-done.10, bf16[256,768]{1,0:T(8,128)(2,1)S(1)} %copy-done.13, ...), custom_call_target="tpu_custom_call" | custom-call | flops 1200000000 | bytes 5000000 | tf_op jit(solution)/shard_map/pallas_call | solution.py:194
  74.6 12.3 %all-to-all-done.1.far_ref = bf16[48,13,128]{2,1,0:T(8,128)(2,1)S(1)} async-done(((bf16[48,13,128]{2,1,0:T(8,128)(2,1)}), bf16[48,13,128]{2,1,0:T(8,128)(2,1)S(1)}, u32[]{:S(2)}, u32[]{:S(2)}) %all-to-all-start.1) | async-done | bytes 159776 | tf_op jit(solution)/shard_map/all_to_all | solution.py:222
  (39 shorter events, 7.5 us)
Async XLA Ops:
  0.6 1.4 %copy-start = (bf16[512,1536]{1,0:T(8,128)(2,1)S(1)}, bf16[512,1536]{1,0:T(8,128)(2,1)}, u32[]{:S(2)}) copy-start(bf16[512,1536]{1,0:T(8,128)(2,1)} %grad_ref.3) | copy-start | bytes 4718596
  2.0 1.1 %copy-start.17 = (bf16[512,768]{1,0:T(8,128)(2,1)S(1)}, bf16[512,768]{1,0:T(8,128)(2,1)}, u32[]{:S(2)}) copy-start(bf16[512,768]{1,0:T(8,128)(2,1)} %ctx_ref.1) | copy-start | bytes 2359300
  6.5 4.9 %collective-permute-start.5 = (bf16[8,48,1664]{2,1,0:T(8,128)(2,1)S(1)}, bf16[8,48,1664]{2,1,0:T(8,128)(2,1)S(1)}, u32[]{:S(2)}, u32[]{:S(2)}) collective-permute-start(bf16[8,48,1664]{2,1,0:T(8,128)(2,1)S(1)} %get-tuple-element.7), channel_id=1, source_target_pairs={{0,1},{1,0},{2,3},{3,2},{4,5},{5,4},{6,7},{7,6},{8,9},{9,8},{10,11... | collective-permute-start | bytes 3833864 | tf_op jit(solution)/shard_map/ppermute | solution.py:212
  13.0 13.2 %copy-start.19 = (bf16[1,768]{1,0:T(2,128)(2,1)S(1)}, bf16[1,768]{1,0:T(2,128)(2,1)}, u32[]{:S(2)}) copy-start(bf16[1,768]{1,0:T(2,128)(2,1)} %param.7) | copy-start | bytes 4612
  13.0 13.2 %copy-start.18 = (bf16[1,256,768]{2,1,0:T(8,128)(2,1)S(1)}, bf16[1,256,768]{2,1,0:T(8,128)(2,1)}, u32[]{:S(2)}) copy-start(bf16[1,256,768]{2,1,0:T(8,128)(2,1)} %param.6) | copy-start | bytes 1179652
  13.0 37.7 %all-to-all-start = ((bf16[8,48,1664]{2,1,0:T(8,128)(2,1)}), bf16[8,48,1664]{2,1,0:T(8,128)(2,1)S(1)}, u32[]{:S(2)}, u32[]{:S(2)}) async-start(bf16[8,48,1664]{2,1,0:T(8,128)(2,1)} %shard_map.69), calls=%async_computation | async-start | bytes 2555904 | tf_op jit(solution)/shard_map/all_to_all | solution.py:220
  26.3 41.0 %copy-start.1 = (bf16[512,1536]{1,0:T(8,128)(2,1)S(1)}, bf16[512,1536]{1,0:T(8,128)(2,1)}, u32[]{:S(2)}) copy-start(bf16[512,1536]{1,0:T(8,128)(2,1)} %grad_ref.3) | copy-start | bytes 4718596
  26.3 16.4 %collective-permute-start = (bf16[256,768]{1,0:T(8,128)(2,1)S(1)}, bf16[256,768]{1,0:T(8,128)(2,1)S(1)}, u32[]{:S(2)}, u32[]{:S(2)}) collective-permute-start(bf16[256,768]{1,0:T(8,128)(2,1)S(1)} %fusion.refs_0_), channel_id=1, source_target_pairs={{0,2},{2,4},{4,192},{192,194},{194,196},{196,384},{384,386},{386,3... | collective-permute-start | bytes 1179656 | tf_op jit(solution)/shard_map/ppermute | solution.py:217
  28.4 17.0 %collective-permute-start.1 = (bf16[256,768]{1,0:T(8,128)(2,1)S(1)}, bf16[256,768]{1,0:T(8,128)(2,1)S(1)}, u32[]{:S(2)}, u32[]{:S(2)}) collective-permute-start(bf16[256,768]{1,0:T(8,128)(2,1)S(1)} %fusion.refs_0_), channel_id=1, source_target_pairs={{0,580},{2,0},{4,2},{192,4},{194,192},{196,194},{384,196},{386,384... | collective-permute-start | bytes 1179656 | tf_op jit(solution)/shard_map/ppermute | solution.py:217
  35.8 12.7 %collective-permute-start.2 = (bf16[256,768]{1,0:T(8,128)(2,1)S(1)}, bf16[256,768]{1,0:T(8,128)(2,1)S(1)}, u32[]{:S(2)}, u32[]{:S(2)}) collective-permute-start(bf16[256,768]{1,0:T(8,128)(2,1)S(1)} %fusion.refs_0_), channel_id=1, source_target_pairs={{0,1},{1,0},{2,3},{3,2},{4,5},{5,4},{6,7},{7,6},{8,9},{9,8},{10,11... | collective-permute-start | bytes 1179656 | tf_op jit(solution)/shard_map/ppermute | solution.py:218
  42.7 6.6 %collective-permute-start.3 = (bf16[256,768]{1,0:T(8,128)(2,1)S(1)}, bf16[256,768]{1,0:T(8,128)(2,1)S(1)}, u32[]{:S(2)}, u32[]{:S(2)}) collective-permute-start(bf16[256,768]{1,0:T(8,128)(2,1)S(1)} %collective-permute-done.refs_1_.refs_0_), channel_id=1, source_target_pairs={{0,1},{1,0},{2,3},{3,2},{4,5},{5,4},{6,7},{7,6},{8,9},{9,8},{10,11... | collective-permute-start | bytes 1179656 | tf_op jit(solution)/shard_map/ppermute | solution.py:218
  45.4 4.6 %collective-permute-start.4 = (bf16[256,768]{1,0:T(8,128)(2,1)S(1)}, bf16[256,768]{1,0:T(8,128)(2,1)S(1)}, u32[]{:S(2)}, u32[]{:S(2)}) collective-permute-start(bf16[256,768]{1,0:T(8,128)(2,1)S(1)} %collective-permute-done.1.refs_2_.refs_1_), channel_id=1, source_target_pairs={{0,1},{1,0},{2,3},{3,2},{4,5},{5,4},{6,7},{7,6},{8,9},{9,8},{10,11... | collective-permute-start | bytes 1179656 | tf_op jit(solution)/shard_map/ppermute | solution.py:218
  50.0 0.8 copy-start.14
  50.8 1.0 %copy-start.3 = (bf16[256,768]{1,0:T(8,128)(2,1)S(1)}, bf16[256,768]{1,0:T(8,128)(2,1)}, u32[]{:S(2)}) copy-start(bf16[256,768]{1,0:T(8,128)(2,1)} %copy-done.2) | copy-start | bytes 1179652
  51.8 1.0 %copy-start.6 = (bf16[256,768]{1,0:T(8,128)(2,1)S(1)}, bf16[256,768]{1,0:T(8,128)(2,1)}, u32[]{:S(2)}) copy-start(bf16[256,768]{1,0:T(8,128)(2,1)} %copy-done.5) | copy-start | bytes 1179652
  52.8 1.0 %copy-start.9 = (bf16[256,768]{1,0:T(8,128)(2,1)S(1)}, bf16[256,768]{1,0:T(8,128)(2,1)}, u32[]{:S(2)}) copy-start(bf16[256,768]{1,0:T(8,128)(2,1)} %copy-done.8) | copy-start | bytes 1179652
  53.8 1.0 %copy-start.12 = (bf16[256,768]{1,0:T(8,128)(2,1)S(1)}, bf16[256,768]{1,0:T(8,128)(2,1)}, u32[]{:S(2)}) copy-start(bf16[256,768]{1,0:T(8,128)(2,1)} %copy-done.11) | copy-start | bytes 1179652
  54.8 1.0 %copy-start.15 = (bf16[256,768]{1,0:T(8,128)(2,1)S(1)}, bf16[256,768]{1,0:T(8,128)(2,1)}, u32[]{:S(2)}) copy-start(bf16[256,768]{1,0:T(8,128)(2,1)} %copy-done.14) | copy-start | bytes 1179652
  56.9 30.1 %all-to-all-start.1 = ((bf16[48,13,128]{2,1,0:T(8,128)(2,1)}), bf16[48,13,128]{2,1,0:T(8,128)(2,1)S(1)}, u32[]{:S(2)}, u32[]{:S(2)}) async-start(bf16[48,13,128]{2,1,0:T(8,128)(2,1)} %shard_map.70), calls=%async_computation.1 | async-start | bytes 393216 | tf_op jit(solution)/shard_map/all_to_all | solution.py:222
  67.3 1.0 %copy-start.4 = (bf16[256,768]{1,0:T(8,128)(2,1)S(1)}, bf16[256,768]{1,0:T(8,128)(2,1)}, u32[]{:S(2)}) copy-start(bf16[256,768]{1,0:T(8,128)(2,1)} %copy-done.2) | copy-start | bytes 1179652
  68.3 1.0 %copy-start.7 = (bf16[256,768]{1,0:T(8,128)(2,1)S(1)}, bf16[256,768]{1,0:T(8,128)(2,1)}, u32[]{:S(2)}) copy-start(bf16[256,768]{1,0:T(8,128)(2,1)} %copy-done.5) | copy-start | bytes 1179652
  69.3 1.0 %copy-start.10 = (bf16[256,768]{1,0:T(8,128)(2,1)S(1)}, bf16[256,768]{1,0:T(8,128)(2,1)}, u32[]{:S(2)}) copy-start(bf16[256,768]{1,0:T(8,128)(2,1)} %copy-done.8) | copy-start | bytes 1179652
  70.3 1.0 %copy-start.13 = (bf16[256,768]{1,0:T(8,128)(2,1)S(1)}, bf16[256,768]{1,0:T(8,128)(2,1)}, u32[]{:S(2)}) copy-start(bf16[256,768]{1,0:T(8,128)(2,1)} %copy-done.11) | copy-start | bytes 1179652
  71.3 1.0 %copy-start.16 = (bf16[256,768]{1,0:T(8,128)(2,1)S(1)}, bf16[256,768]{1,0:T(8,128)(2,1)}, u32[]{:S(2)}) copy-start(bf16[256,768]{1,0:T(8,128)(2,1)} %copy-done.14) | copy-start | bytes 1179652
  (4 other events, 3.0 us)

commit v5 on v4

--- a/solution.py
+++ b/solution.py
@@ -118,8 +118,7 @@
     )(got, keep)
 
 
-def near_kernel(got_ref, *refs):
-    sum_ref, wide = refs[-2:]
+def near_kernel(got_ref, sum_ref, wide):
     for chunk in range(sum_ref.shape[1]):
         lanes = slice(chunk * PAD, (chunk + 1) * PAD)
         total = got_ref[0, :, lanes].astype(jnp.float32)
@@ -131,18 +130,18 @@
     sum_ref[...] = wide[...].astype(sum_ref.dtype)
 
 
-def near_sum(got, held):
+def near_sum(got):
     _, rows, lanes = got.shape
     shape = (rows, lanes // PAD, PAD)
     return pl.pallas_call(
         near_kernel,
         out_shape=jax.ShapeDtypeStruct(shape, jnp.bfloat16),
-        in_specs=[VMEM] + [pl.BlockSpec(memory_space=pl.ANY)] * len(held),
+        in_specs=[VMEM],
         out_specs=VMEM,
         scratch_shapes=[pltpu.VMEM(shape, jnp.float32)],
         compiler_params=parameters(16),
         cost_estimate=pl.CostEstimate(flops=10**6, bytes_accessed=2 * 10**6, transcendentals=0),
-    )(got, *held)
+    )(got)
 
 
 def last_kernel(scale, far_ref, weight_ref, bias_ref):
@@ -218,7 +217,7 @@
     held += [lax.ppermute(piece, "c", swap) for piece in held]
 
     near = lax.all_to_all(chip_sum(got, keep), ("x", "yl"), split_axis=0, concat_axis=0, tiled=True)
-    near = near_sum(near, held[1:])
+    near = near_sum(near)
     far = lax.all_to_all(near, ("zh", "yh", "zl"), split_axis=0, concat_axis=0, tiled=True)
     weight_grad, bias_grad = last_sum(far, 1.0 / count)
 

time: 88.5 us -> 80.3 us (0.907)
  local copies, waits for them, and re-layouts: 16.2 us -> 2.55 us
  waiting for transfers between devices: 20.3 us -> 26.2 us
  starting transfers between devices: 41.2 us -> 38.4 us
  Pallas kernels: 9.09 us -> 10.6 us
  other arithmetic: 0.08 us -> 1.2 us
    unnamed x40 -> x8, local copies, waits for them, and re-layouts: 16.2 us -> 2.55 us
    all_to_all x1, waiting for transfers between devices: 12.3 us -> 15.5 us  [body(): lax.all_to_all(near, ('zh', 'yh', 'zl'), split_axis=0, concat_axis=0, til...]
    ppermute x2, waiting for transfers between devices: 4.99 us -> 7.75 us  [body(): lax.ppermute(block, ('zh', 'zl'), [(i, (i + hop) % ring) for i in range(r...]
    all_to_all x1, starting transfers between devices: 10.4 us -> 8.3 us  [body(): lax.all_to_all(near, ('zh', 'yh', 'zl'), split_axis=0, concat_axis=0, til...]
    pallas_call x1, Pallas kernels: 2.34 us -> 3.84 us  [ctx_product(): pl.pallas_call(functools.partial(ctx_kernel, chips), out_shape=jax.ShapeD...]
    convert_element_type x1, other arithmetic: 0.07 us -> 1.18 us  [body(): (codes[0].astype(jnp.float32) * scales.astype(jnp.float32)).astype(jnp.bf...]
  transfers between devices with their start and end apart: 8 -> 8, of which waited for: 3 -> 4; matrix products, arithmetic and copies ran while one was open for 0% -> 1% of each run, Pallas kernels for 3% -> 6%
where the time goes in v5:
time: 80.3 us; the launch traced here: 79.8 us
  starting transfers between devices  38.4 us (48%)
  waiting for transfers between devices  26.2 us (33%)
  Pallas kernels  10.6 us (13%)
  local copies, waits for them, and re-layouts  2.55 us (3%)
  other arithmetic  1.2 us (1%)
    all_to_all x1, waiting for transfers between devices, body(): lax.all_to_all(near, ('zh', 'yh', 'zl'), split_axis=0, concat_axis=0, til...  15.5 us
    all_to_all x1, starting transfers between devices, body(): lax.all_to_all(chip_sum(got, keep), ('x', 'yl'), split_axis=0, concat_axi...  13.2 us
    ppermute x2, starting transfers between devices, body(): lax.ppermute(block, ('zh', 'zl'), [(i, (i + hop) % ring) for i in range(r...  9.33 us
    all_to_all x1, starting transfers between devices, body(): lax.all_to_all(near, ('zh', 'yh', 'zl'), split_axis=0, concat_axis=0, til...  8.3 us
    ppermute x2, waiting for transfers between devices, body(): lax.ppermute(block, ('zh', 'zl'), [(i, (i + hop) % ring) for i in range(r...  7.75 us
    ppermute x3, starting transfers between devices, body(): held += [lax.ppermute(piece, 'c', swap) for piece in held]  5.74 us
    pallas_call x1, Pallas kernels, ctx_product(): pl.pallas_call(functools.partial(ctx_kernel, chips), out_shape=jax.ShapeD...  3.84 us
    pallas_call x1, Pallas kernels, local_terms(): pl.pallas_call(functools.partial(term_kernel, sizes), out_shape=(piece, p...  3.37 us
  transfers between devices with their start and end apart: 8, of which 4 were waited for; matrix products, arithmetic and copies ran while one was open for 1% of the time, Pallas kernels for 6%

profile of v5, /device:TPU:2, one launch (start us, length us, event | category | flops | bytes accessed | tf_op | source)
XLA Modules:
  0.0 79.8 jit_solution(8010068755524101076)
XLA Ops:
  0.6 0.0 copy-start
  0.6 1.4 %copy-done = bf16[512,1536]{1,0:T(8,128)(2,1)S(1)} copy-done((bf16[512,1536]{1,0:T(8,128)(2,1)S(1)}, bf16[512,1536]{1,0:T(8,128)(2,1)}, u32[]{:S(2)}) %copy-start) | copy-done | bytes 1572888
  2.0 1.1 %copy-done.2 = bf16[512,768]{1,0:T(8,128)(2,1)S(1)} copy-done((bf16[512,768]{1,0:T(8,128)(2,1)S(1)}, bf16[512,768]{1,0:T(8,128)(2,1)}, u32[]{:S(2)}) %copy-start.2) | copy-done | bytes 786456
  3.2 3.4 %shard_map.68 = (bf16[8,48,1664]{2,1,0:T(8,128)(2,1)S(1)}, bf16[8,48,1664]{2,1,0:T(8,128)(2,1)S(1)}) custom-call(bf16[512,1536]{1,0:T(8,128)(2,1)S(1)} %copy-done, bf16[512,768]{1,0:T(8,128)(2,1)S(1)} %copy-done.2), custom_call_target="tpu_custom_call" | custom-call | flops 4000000000 | bytes 5000000 | tf_op jit(solution)/shard_map/pallas_call | solution.py:91
  6.5 1.9 %collective-permute-start.5 = (bf16[8,48,1664]{2,1,0:T(8,128)(2,1)S(1)}, bf16[8,48,1664]{2,1,0:T(8,128)(2,1)S(1)}, u32[]{:S(2)}, u32[]{:S(2)}) collective-permute-start(bf16[8,48,1664]{2,1,0:T(8,128)(2,1)S(1)} %get-tuple-element.7), channel_id=1, source_target_pairs={{0,1},{1,0},{2,3},{3,2},{4,5},{5,4},{6,7},{7,6},{8,9},{9,8},{10,11... | collective-permute-start | bytes 3833864 | tf_op jit(solution)/shard_map/ppermute | solution.py:211
  8.5 3.0 %collective-permute-done.5.got_ref = bf16[8,48,1664]{2,1,0:T(8,128)(2,1)S(1)} collective-permute-done((bf16[8,48,1664]{2,1,0:T(8,128)(2,1)S(1)}, bf16[8,48,1664]{2,1,0:T(8,128)(2,1)S(1)}, u32[]{:S(2)}, u32[]{:S(2)}) %collective-permute-start.5) | collective-permute-done | bytes 1277984 | tf_op jit(solution)/shard_map/ppermute | solution.py:211
  11.4 1.6 %shard_map.69 = bf16[8,48,1664]{2,1,0:T(8,128)(2,1)} custom-call(bf16[8,48,1664]{2,1,0:T(8,128)(2,1)S(1)} %collective-permute-done.5.got_ref, bf16[8,48,1664]{2,1,0:T(8,128)(2,1)S(1)} %get-tuple-element.8.keep_ref), custom_call_target="tpu_custom_call" | custom-call | flops 1000000 | bytes 4000000 | tf_op jit(solution)/shard_map/pallas_call | solution.py:111
  13.1 13.2 %all-to-all-start = ((bf16[8,48,1664]{2,1,0:T(8,128)(2,1)}), bf16[8,48,1664]{2,1,0:T(8,128)(2,1)S(1)}, u32[]{:S(2)}, u32[]{:S(2)}) async-start(bf16[8,48,1664]{2,1,0:T(8,128)(2,1)} %shard_map.69), calls=%async_computation | async-start | bytes 2555904 | tf_op jit(solution)/shard_map/all_to_all | solution.py:219
  26.2 0.0 copy-start.1
  26.3 1.2 %fusion.refs_0_ = bf16[256,768]{1,0:T(8,128)(2,1)S(1)} fusion(bf16[1,256,768]{2,1,0:T(8,128)(2,1)} %param.6, f32[768]{0:T(1024)S(1)} %convert_reduce_fusion), kind=kLoop, calls=%fused_computation.1 | loop fusion | flops 589824 | bytes 789504 | tf_op jit(solution)/shard_map/convert_element_type | solution.py:212
  27.4 7.4 %collective-permute-start.1 = (bf16[256,768]{1,0:T(8,128)(2,1)S(1)}, bf16[256,768]{1,0:T(8,128)(2,1)}, u32[]{:S(2)}, u32[]{:S(2)}) collective-permute-start(bf16[256,768]{1,0:T(8,128)(2,1)S(1)} %fusion.refs_0_), channel_id=1, source_target_pairs={{0,580},{2,0},{4,2},{192,4},{194,192},{196,194},{384,196},{386,384... | collective-permute-start | bytes 1179656 | tf_op jit(solution)/shard_map/ppermute | solution.py:216
  34.9 1.9 %collective-permute-start = (bf16[256,768]{1,0:T(8,128)(2,1)S(1)}, bf16[256,768]{1,0:T(8,128)(2,1)}, u32[]{:S(2)}, u32[]{:S(2)}) collective-permute-start(bf16[256,768]{1,0:T(8,128)(2,1)S(1)} %fusion.refs_0_), channel_id=1, source_target_pairs={{0,2},{2,4},{4,192},{192,194},{194,196},{196,384},{384,386},{386,3... | collective-permute-start | bytes 1179656 | tf_op jit(solution)/shard_map/ppermute | solution.py:216
  36.8 1.9 %collective-permute-start.2 = (bf16[256,768]{1,0:T(8,128)(2,1)S(1)}, bf16[256,768]{1,0:T(8,128)(2,1)}, u32[]{:S(2)}, u32[]{:S(2)}) collective-permute-start(bf16[256,768]{1,0:T(8,128)(2,1)S(1)} %fusion.refs_0_), channel_id=1, source_target_pairs={{0,1},{1,0},{2,3},{3,2},{4,5},{5,4},{6,7},{7,6},{8,9},{9,8},{10,11... | collective-permute-start | bytes 1179656 | tf_op jit(solution)/shard_map/ppermute | solution.py:217
  38.7 4.2 %collective-permute-done.1.refs_2_ = bf16[256,768]{1,0:T(8,128)(2,1)} collective-permute-done((bf16[256,768]{1,0:T(8,128)(2,1)S(1)}, bf16[256,768]{1,0:T(8,128)(2,1)}, u32[]{:S(2)}, u32[]{:S(2)}) %collective-permute-start.1) | collective-permute-done | bytes 393248 | tf_op jit(solution)/shard_map/ppermute | solution.py:216
  43.0 1.9 %collective-permute-start.4 = (bf16[256,768]{1,0:T(8,128)(2,1)}, bf16[256,768]{1,0:T(8,128)(2,1)}, u32[]{:S(2)}, u32[]{:S(2)}) collective-permute-start(bf16[256,768]{1,0:T(8,128)(2,1)} %collective-permute-done.1.refs_2_), channel_id=1, source_target_pairs={{0,1},{1,0},{2,3},{3,2},{4,5},{5,4},{6,7},{7,6},{8,9},{9,8},{10,11... | collective-permute-start | bytes 1179656 | tf_op jit(solution)/shard_map/ppermute | solution.py:217
  44.9 3.5 %collective-permute-done.refs_1_ = bf16[256,768]{1,0:T(8,128)(2,1)} collective-permute-done((bf16[256,768]{1,0:T(8,128)(2,1)S(1)}, bf16[256,768]{1,0:T(8,128)(2,1)}, u32[]{:S(2)}, u32[]{:S(2)}) %collective-permute-start) | collective-permute-done | bytes 393248 | tf_op jit(solution)/shard_map/ppermute | solution.py:216
  48.4 1.9 %collective-permute-start.3 = (bf16[256,768]{1,0:T(8,128)(2,1)}, bf16[256,768]{1,0:T(8,128)(2,1)}, u32[]{:S(2)}, u32[]{:S(2)}) collective-permute-start(bf16[256,768]{1,0:T(8,128)(2,1)} %collective-permute-done.refs_1_), channel_id=1, source_target_pairs={{0,1},{1,0},{2,3},{3,2},{4,5},{5,4},{6,7},{7,6},{8,9},{9,8},{10,11... | collective-permute-start | bytes 1179656 | tf_op jit(solution)/shard_map/ppermute | solution.py:217
  50.3 0.0 all-to-all-done.got_ref
  50.3 1.1 %shard_map.70 = bf16[48,13,128]{2,1,0:T(8,128)(2,1)} custom-call(bf16[8,48,1664]{2,1,0:T(8,128)(2,1)S(1)} %all-to-all-done.got_ref), custom_call_target="tpu_custom_call" | custom-call | flops 1000000 | bytes 2000000 | tf_op jit(solution)/shard_map/pallas_call | solution.py:136
  51.4 8.3 %all-to-all-start.1 = ((bf16[48,13,128]{2,1,0:T(8,128)(2,1)}), bf16[48,13,128]{2,1,0:T(8,128)(2,1)S(1)}, u32[]{:S(2)}, u32[]{:S(2)}) async-start(bf16[48,13,128]{2,1,0:T(8,128)(2,1)} %shard_map.70), calls=%async_computation.1 | async-start | bytes 393216 | tf_op jit(solution)/shard_map/all_to_all | solution.py:221
  59.7 0.0 collective-permute-done.2.refs_3_
  59.7 3.8 %shard_map.67 = bf16[512,768]{1,0:T(8,128)(2,1)} custom-call(bf16[512,1536]{1,0:T(8,128)(2,1)S(1)} %copy-done.1, bf16[256,768]{1,0:T(8,128)(2,1)S(1)} %fusion.refs_0_, bf16[256,768]{1,0:T(8,128)(2,1)} %collective-permute-done.refs_1_, bf16[256,768]{1,0:T(8,128)(2,1)} %collective-permute-done.1.refs_2_, bf16[256,768]{1,0:T(8,128)(2,1)} %collective-permute-done.2.refs_3_, ...), custom_call_target="tpu_custom_call" | custom-call | flops 1200000000 | bytes 5000000 | tf_op jit(solution)/shard_map/pallas_call | solution.py:193
  63.6 15.5 %all-to-all-done.1.far_ref = bf16[48,13,128]{2,1,0:T(8,128)(2,1)S(1)} async-done(((bf16[48,13,128]{2,1,0:T(8,128)(2,1)}), bf16[48,13,128]{2,1,0:T(8,128)(2,1)S(1)}, u32[]{:S(2)}, u32[]{:S(2)}) %all-to-all-start.1) | async-done | bytes 159776 | tf_op jit(solution)/shard_map/all_to_all | solution.py:221
  79.1 0.7 shard_map.71
  (7 shorter events, 0.0 us)
Async XLA Ops:
  0.6 1.4 %copy-start = (bf16[512,1536]{1,0:T(8,128)(2,1)S(1)}, bf16[512,1536]{1,0:T(8,128)(2,1)}, u32[]{:S(2)}) copy-start(bf16[512,1536]{1,0:T(8,128)(2,1)} %grad_ref.3) | copy-start | bytes 4718596
  2.0 1.1 %copy-start.2 = (bf16[512,768]{1,0:T(8,128)(2,1)S(1)}, bf16[512,768]{1,0:T(8,128)(2,1)}, u32[]{:S(2)}) copy-start(bf16[512,768]{1,0:T(8,128)(2,1)} %ctx_ref.1) | copy-start | bytes 2359300
  6.5 4.9 %collective-permute-start.5 = (bf16[8,48,1664]{2,1,0:T(8,128)(2,1)S(1)}, bf16[8,48,1664]{2,1,0:T(8,128)(2,1)S(1)}, u32[]{:S(2)}, u32[]{:S(2)}) collective-permute-start(bf16[8,48,1664]{2,1,0:T(8,128)(2,1)S(1)} %get-tuple-element.7), channel_id=1, source_target_pairs={{0,1},{1,0},{2,3},{3,2},{4,5},{5,4},{6,7},{7,6},{8,9},{9,8},{10,11... | collective-permute-start | bytes 3833864 | tf_op jit(solution)/shard_map/ppermute | solution.py:211
  13.1 13.2 %copy-start.3 = (bf16[1,768]{1,0:T(2,128)(2,1)S(1)}, bf16[1,768]{1,0:T(2,128)(2,1)}, u32[]{:S(2)}) copy-start(bf16[1,768]{1,0:T(2,128)(2,1)} %param.7) | copy-start | bytes 4612
  13.1 37.2 %all-to-all-start = ((bf16[8,48,1664]{2,1,0:T(8,128)(2,1)}), bf16[8,48,1664]{2,1,0:T(8,128)(2,1)S(1)}, u32[]{:S(2)}, u32[]{:S(2)}) async-start(bf16[8,48,1664]{2,1,0:T(8,128)(2,1)} %shard_map.69), calls=%async_computation | async-start | bytes 2555904 | tf_op jit(solution)/shard_map/all_to_all | solution.py:219
  26.2 33.5 %copy-start.1 = (bf16[512,1536]{1,0:T(8,128)(2,1)S(1)}, bf16[512,1536]{1,0:T(8,128)(2,1)}, u32[]{:S(2)}) copy-start(bf16[512,1536]{1,0:T(8,128)(2,1)} %grad_ref.3) | copy-start | bytes 4718596
  27.4 15.5 %collective-permute-start.1 = (bf16[256,768]{1,0:T(8,128)(2,1)S(1)}, bf16[256,768]{1,0:T(8,128)(2,1)}, u32[]{:S(2)}, u32[]{:S(2)}) collective-permute-start(bf16[256,768]{1,0:T(8,128)(2,1)S(1)} %fusion.refs_0_), channel_id=1, source_target_pairs={{0,580},{2,0},{4,2},{192,4},{194,192},{196,194},{384,196},{386,384... | collective-permute-start | bytes 1179656 | tf_op jit(solution)/shard_map/ppermute | solution.py:216
  34.9 13.5 %collective-permute-start = (bf16[256,768]{1,0:T(8,128)(2,1)S(1)}, bf16[256,768]{1,0:T(8,128)(2,1)}, u32[]{:S(2)}, u32[]{:S(2)}) collective-permute-start(bf16[256,768]{1,0:T(8,128)(2,1)S(1)} %fusion.refs_0_), channel_id=1, source_target_pairs={{0,2},{2,4},{4,192},{192,194},{194,196},{196,384},{384,386},{386,3... | collective-permute-start | bytes 1179656 | tf_op jit(solution)/shard_map/ppermute | solution.py:216
  36.8 22.9 %collective-permute-start.2 = (bf16[256,768]{1,0:T(8,128)(2,1)S(1)}, bf16[256,768]{1,0:T(8,128)(2,1)}, u32[]{:S(2)}, u32[]{:S(2)}) collective-permute-start(bf16[256,768]{1,0:T(8,128)(2,1)S(1)} %fusion.refs_0_), channel_id=1, source_target_pairs={{0,1},{1,0},{2,3},{3,2},{4,5},{5,4},{6,7},{7,6},{8,9},{9,8},{10,11... | collective-permute-start | bytes 1179656 | tf_op jit(solution)/shard_map/ppermute | solution.py:217
  43.0 16.8 %collective-permute-start.4 = (bf16[256,768]{1,0:T(8,128)(2,1)}, bf16[256,768]{1,0:T(8,128)(2,1)}, u32[]{:S(2)}, u32[]{:S(2)}) collective-permute-start(bf16[256,768]{1,0:T(8,128)(2,1)} %collective-permute-done.1.refs_2_), channel_id=1, source_target_pairs={{0,1},{1,0},{2,3},{3,2},{4,5},{5,4},{6,7},{7,6},{8,9},{9,8},{10,11... | collective-permute-start | bytes 1179656 | tf_op jit(solution)/shard_map/ppermute | solution.py:217
  48.4 11.3 %collective-permute-start.3 = (bf16[256,768]{1,0:T(8,128)(2,1)}, bf16[256,768]{1,0:T(8,128)(2,1)}, u32[]{:S(2)}, u32[]{:S(2)}) collective-permute-start(bf16[256,768]{1,0:T(8,128)(2,1)} %collective-permute-done.refs_1_), channel_id=1, source_target_pairs={{0,1},{1,0},{2,3},{3,2},{4,5},{5,4},{6,7},{7,6},{8,9},{9,8},{10,11... | collective-permute-start | bytes 1179656 | tf_op jit(solution)/shard_map/ppermute | solution.py:217
  51.4 27.7 %all-to-all-start.1 = ((bf16[48,13,128]{2,1,0:T(8,128)(2,1)}), bf16[48,13,128]{2,1,0:T(8,128)(2,1)S(1)}, u32[]{:S(2)}, u32[]{:S(2)}) async-start(bf16[48,13,128]{2,1,0:T(8,128)(2,1)} %shard_map.70), calls=%async_computation.1 | async-start | bytes 393216 | tf_op jit(solution)/shard_map/all_to_all | solution.py:221

commit v6 on v5

--- a/solution.py
+++ b/solution.py
@@ -210,11 +210,12 @@
     send, keep = local_terms(sizes, grad_out, context)
     got = lax.ppermute(send, "c", swap)
     block = (codes[0].astype(jnp.float32) * scales.astype(jnp.float32)).astype(jnp.bfloat16)
-    held = [block]
-    for back in range(1, chips):
-        hop = back if back <= chips // 2 else back - chips
-        held.append(lax.ppermute(block, ("zh", "zl"), [(i, (i + hop) % ring) for i in range(ring)]))
-    held += [lax.ppermute(piece, "c", swap) for piece in held]
+    held = []
+    for side in range(2):
+        for back in range(chips):
+            hop = back if back <= chips // 2 else back - chips
+            moves = [(2 * i + c, 2 * ((i + hop) % ring) + (c ^ side)) for i in range(ring) for c in range(2)]
+            held.append(lax.ppermute(block, ("zh", "zl", "c"), moves) if side + back else block)
 
     near = lax.all_to_all(chip_sum(got, keep), ("x", "yl"), split_axis=0, concat_axis=0, tiled=True)
     near = near_sum(near)

time: 80.3 us -> 77.6 us (0.966)
  waiting for transfers between devices: 26.2 us -> 18.2 us
  starting transfers between devices: 38.4 us -> 43.8 us
    ppermute x5, waiting for transfers between devices: 7.76 us -> 0.65 us  [body(): lax.ppermute(block, ('zh', 'zl', 'c'), moves)]
    ppermute x5, starting transfers between devices: 15.1 us -> 18 us  [body(): lax.ppermute(block, ('zh', 'zl', 'c'), moves)]
    all_to_all x1, starting transfers between devices: 8.3 us -> 10.7 us  [body(): lax.all_to_all(near, ('zh', 'yh', 'zl'), split_axis=0, concat_axis=0, til...]
    all_to_all x1, waiting for transfers between devices: 15.5 us -> 14.6 us  [body(): lax.all_to_all(near, ('zh', 'yh', 'zl'), split_axis=0, concat_axis=0, til...]
  transfers between devices with their start and end apart: 8 -> 8, of which waited for: 4 -> 3; matrix products, arithmetic and copies ran while one was open for 1% -> 2% of each run, Pallas kernels for 6% -> 6%
where the time goes in v6:
time: 77.6 us; the launch traced here: 77.1 us
  starting transfers between devices  43.8 us (56%)
  waiting for transfers between devices  18.2 us (23%)
  Pallas kernels  10.6 us (14%)
  local copies, waits for them, and re-layouts  2.55 us (3%)
  other arithmetic  1.2 us (2%)
    ppermute x5, starting transfers between devices, body(): lax.ppermute(block, ('zh', 'zl', 'c'), moves)  18 us
    all_to_all x1, waiting for transfers between devices, body(): lax.all_to_all(near, ('zh', 'yh', 'zl'), split_axis=0, concat_axis=0, til...  14.6 us
    all_to_all x1, starting transfers between devices, body(): lax.all_to_all(chip_sum(got, keep), ('x', 'yl'), split_axis=0, concat_axi...  13.2 us
    all_to_all x1, starting transfers between devices, body(): lax.all_to_all(near, ('zh', 'yh', 'zl'), split_axis=0, concat_axis=0, til...  10.7 us
    pallas_call x1, Pallas kernels, ctx_product(): pl.pallas_call(functools.partial(ctx_kernel, chips), out_shape=jax.ShapeD...  3.8 us
    pallas_call x1, Pallas kernels, local_terms(): pl.pallas_call(functools.partial(term_kernel, sizes), out_shape=(piece, p...  3.37 us
    ppermute x1, waiting for transfers between devices, body(): got = lax.ppermute(send, 'c', swap)  2.95 us
    unnamed x8, local copies, waits for them, and re-layouts  2.55 us
  transfers between devices with their start and end apart: 8, of which 3 were waited for; matrix products, arithmetic and copies ran while one was open for 2% of the time, Pallas kernels for 6%

profile of v6, /device:TPU:2, one launch (start us, length us, event | category | flops | bytes accessed | tf_op | source)
XLA Modules:
  0.0 77.1 jit_solution(9722608493224341102)
XLA Ops:
  0.6 0.0 copy-start
  0.6 1.4 %copy-done = bf16[512,1536]{1,0:T(8,128)(2,1)S(1)} copy-done((bf16[512,1536]{1,0:T(8,128)(2,1)S(1)}, bf16[512,1536]{1,0:T(8,128)(2,1)}, u32[]{:S(2)}) %copy-start) | copy-done | bytes 1572888
  2.0 1.1 %copy-done.2 = bf16[512,768]{1,0:T(8,128)(2,1)S(1)} copy-done((bf16[512,768]{1,0:T(8,128)(2,1)S(1)}, bf16[512,768]{1,0:T(8,128)(2,1)}, u32[]{:S(2)}) %copy-start.2) | copy-done | bytes 786456
  3.2 3.4 %shard_map.68 = (bf16[8,48,1664]{2,1,0:T(8,128)(2,1)S(1)}, bf16[8,48,1664]{2,1,0:T(8,128)(2,1)S(1)}) custom-call(bf16[512,1536]{1,0:T(8,128)(2,1)S(1)} %copy-done, bf16[512,768]{1,0:T(8,128)(2,1)S(1)} %copy-done.2), custom_call_target="tpu_custom_call" | custom-call | flops 4000000000 | bytes 5000000 | tf_op jit(solution)/shard_map/pallas_call | solution.py:91
  6.5 1.9 %collective-permute-start.5 = (bf16[8,48,1664]{2,1,0:T(8,128)(2,1)S(1)}, bf16[8,48,1664]{2,1,0:T(8,128)(2,1)S(1)}, u32[]{:S(2)}, u32[]{:S(2)}) collective-permute-start(bf16[8,48,1664]{2,1,0:T(8,128)(2,1)S(1)} %get-tuple-element.7), channel_id=1, source_target_pairs={{0,1},{1,0},{2,3},{3,2},{4,5},{5,4},{6,7},{7,6},{8,9},{9,8},{10,11... | collective-permute-start | bytes 3833864 | tf_op jit(solution)/shard_map/ppermute | solution.py:211
  8.5 3.0 %collective-permute-done.5.got_ref = bf16[8,48,1664]{2,1,0:T(8,128)(2,1)S(1)} collective-permute-done((bf16[8,48,1664]{2,1,0:T(8,128)(2,1)S(1)}, bf16[8,48,1664]{2,1,0:T(8,128)(2,1)S(1)}, u32[]{:S(2)}, u32[]{:S(2)}) %collective-permute-start.5) | collective-permute-done | bytes 1277984 | tf_op jit(solution)/shard_map/ppermute | solution.py:211
  11.4 1.6 %shard_map.69 = bf16[8,48,1664]{2,1,0:T(8,128)(2,1)} custom-call(bf16[8,48,1664]{2,1,0:T(8,128)(2,1)S(1)} %collective-permute-done.5.got_ref, bf16[8,48,1664]{2,1,0:T(8,128)(2,1)S(1)} %get-tuple-element.8.keep_ref), custom_call_target="tpu_custom_call" | custom-call | flops 1000000 | bytes 4000000 | tf_op jit(solution)/shard_map/pallas_call | solution.py:111
  13.1 13.2 %all-to-all-start = ((bf16[8,48,1664]{2,1,0:T(8,128)(2,1)}), bf16[8,48,1664]{2,1,0:T(8,128)(2,1)S(1)}, u32[]{:S(2)}, u32[]{:S(2)}) async-start(bf16[8,48,1664]{2,1,0:T(8,128)(2,1)} %shard_map.69), calls=%async_computation | async-start | bytes 2555904 | tf_op jit(solution)/shard_map/all_to_all | solution.py:220
  26.2 0.0 copy-start.1
  26.3 1.2 %fusion.refs_0_ = bf16[256,768]{1,0:T(8,128)(2,1)S(1)} fusion(bf16[1,256,768]{2,1,0:T(8,128)(2,1)} %param.6, f32[768]{0:T(1024)S(1)} %convert_reduce_fusion), kind=kLoop, calls=%fused_computation.1 | loop fusion | flops 589824 | bytes 789504 | tf_op jit(solution)/shard_map/convert_element_type | solution.py:212
  27.4 6.6 %collective-permute-start.4 = (bf16[256,768]{1,0:T(8,128)(2,1)S(1)}, bf16[256,768]{1,0:T(8,128)(2,1)}, u32[]{:S(2)}, u32[]{:S(2)}) collective-permute-start(bf16[256,768]{1,0:T(8,128)(2,1)S(1)} %fusion.refs_0_), channel_id=1, source_target_pairs={{0,581},{1,580},{2,1},{3,0},{4,3},{5,2},{192,5},{193,4},{194,193},... | collective-permute-start | bytes 1179656 | tf_op jit(solution)/shard_map/ppermute | solution.py:218
  34.0 1.9 %collective-permute-start.3 = (bf16[256,768]{1,0:T(8,128)(2,1)S(1)}, bf16[256,768]{1,0:T(8,128)(2,1)}, u32[]{:S(2)}, u32[]{:S(2)}) collective-permute-start(bf16[256,768]{1,0:T(8,128)(2,1)S(1)} %fusion.refs_0_), channel_id=1, source_target_pairs={{0,3},{1,2},{2,5},{3,4},{4,193},{5,192},{192,195},{193,194},{194,1... | collective-permute-start | bytes 1179656 | tf_op jit(solution)/shard_map/ppermute | solution.py:218
  36.0 2.8 %collective-permute-start.2 = (bf16[256,768]{1,0:T(8,128)(2,1)S(1)}, bf16[256,768]{1,0:T(8,128)(2,1)}, u32[]{:S(2)}, u32[]{:S(2)}) collective-permute-start(bf16[256,768]{1,0:T(8,128)(2,1)S(1)} %fusion.refs_0_), channel_id=1, source_target_pairs={{0,1},{1,0},{2,3},{3,2},{4,5},{5,4},{192,193},{193,192},{194,195},... | collective-permute-start | bytes 1179656 | tf_op jit(solution)/shard_map/ppermute | solution.py:218
  38.8 4.8 %collective-permute-start.1 = (bf16[256,768]{1,0:T(8,128)(2,1)S(1)}, bf16[256,768]{1,0:T(8,128)(2,1)}, u32[]{:S(2)}, u32[]{:S(2)}) collective-permute-start(bf16[256,768]{1,0:T(8,128)(2,1)S(1)} %fusion.refs_0_), channel_id=1, source_target_pairs={{0,580},{1,581},{2,0},{3,1},{4,2},{5,3},{192,4},{193,5},{194,192},... | collective-permute-start | bytes 1179656 | tf_op jit(solution)/shard_map/ppermute | solution.py:218
  43.6 1.9 %collective-permute-start = (bf16[256,768]{1,0:T(8,128)(2,1)S(1)}, bf16[256,768]{1,0:T(8,128)(2,1)}, u32[]{:S(2)}, u32[]{:S(2)}) collective-permute-start(bf16[256,768]{1,0:T(8,128)(2,1)S(1)} %fusion.refs_0_), channel_id=1, source_target_pairs={{0,2},{1,3},{2,4},{3,5},{4,192},{5,193},{192,194},{193,195},{194,1... | collective-permute-start | bytes 1179656 | tf_op jit(solution)/shard_map/ppermute | solution.py:218
  45.5 0.0 all-to-all-done.got_ref
  45.5 1.1 %shard_map.70 = bf16[48,13,128]{2,1,0:T(8,128)(2,1)} custom-call(bf16[8,48,1664]{2,1,0:T(8,128)(2,1)S(1)} %all-to-all-done.got_ref), custom_call_target="tpu_custom_call" | custom-call | flops 1000000 | bytes 2000000 | tf_op jit(solution)/shard_map/pallas_call | solution.py:136
  46.6 10.7 %all-to-all-start.1 = ((bf16[48,13,128]{2,1,0:T(8,128)(2,1)}), bf16[48,13,128]{2,1,0:T(8,128)(2,1)S(1)}, u32[]{:S(2)}, u32[]{:S(2)}) async-start(bf16[48,13,128]{2,1,0:T(8,128)(2,1)} %shard_map.70), calls=%async_computation.1 | async-start | bytes 393216 | tf_op jit(solution)/shard_map/all_to_all | solution.py:222
  57.3 0.0 collective-permute-done.4.refs_5_
  57.4 0.0 collective-permute-done.2.refs_3_
  57.4 0.6 collective-permute-done.refs_1_
  58.0 3.8 %shard_map.67 = bf16[512,768]{1,0:T(8,128)(2,1)} custom-call(bf16[512,1536]{1,0:T(8,128)(2,1)S(1)} %copy-done.1, bf16[256,768]{1,0:T(8,128)(2,1)S(1)} %fusion.refs_0_, bf16[256,768]{1,0:T(8,128)(2,1)} %collective-permute-done.refs_1_, bf16[256,768]{1,0:T(8,128)(2,1)} %collective-permute-done.1.refs_2_, bf16[256,768]{1,0:T(8,128)(2,1)} %collective-permute-done.2.refs_3_, ...), custom_call_target="tpu_custom_call" | custom-call | flops 1200000000 | bytes 5000000 | tf_op jit(solution)/shard_map/pallas_call | solution.py:193
  61.8 14.6 %all-to-all-done.1.far_ref = bf16[48,13,128]{2,1,0:T(8,128)(2,1)S(1)} async-done(((bf16[48,13,128]{2,1,0:T(8,128)(2,1)}), bf16[48,13,128]{2,1,0:T(8,128)(2,1)S(1)}, u32[]{:S(2)}, u32[]{:S(2)}) %all-to-all-start.1) | async-done | bytes 159776 | tf_op jit(solution)/shard_map/all_to_all | solution.py:222
  76.4 0.7 shard_map.71
  (7 shorter events, 0.0 us)
Async XLA Ops:
  0.6 1.4 %copy-start = (bf16[512,1536]{1,0:T(8,128)(2,1)S(1)}, bf16[512,1536]{1,0:T(8,128)(2,1)}, u32[]{:S(2)}) copy-start(bf16[512,1536]{1,0:T(8,128)(2,1)} %grad_ref.3) | copy-start | bytes 4718596
  2.0 1.1 %copy-start.2 = (bf16[512,768]{1,0:T(8,128)(2,1)S(1)}, bf16[512,768]{1,0:T(8,128)(2,1)}, u32[]{:S(2)}) copy-start(bf16[512,768]{1,0:T(8,128)(2,1)} %ctx_ref.1) | copy-start | bytes 2359300
  6.5 4.9 %collective-permute-start.5 = (bf16[8,48,1664]{2,1,0:T(8,128)(2,1)S(1)}, bf16[8,48,1664]{2,1,0:T(8,128)(2,1)S(1)}, u32[]{:S(2)}, u32[]{:S(2)}) collective-permute-start(bf16[8,48,1664]{2,1,0:T(8,128)(2,1)S(1)} %get-tuple-element.7), channel_id=1, source_target_pairs={{0,1},{1,0},{2,3},{3,2},{4,5},{5,4},{6,7},{7,6},{8,9},{9,8},{10,11... | collective-permute-start | bytes 3833864 | tf_op jit(solution)/shard_map/ppermute | solution.py:211
  13.1 13.2 %copy-start.3 = (bf16[1,768]{1,0:T(2,128)(2,1)S(1)}, bf16[1,768]{1,0:T(2,128)(2,1)}, u32[]{:S(2)}) copy-start(bf16[1,768]{1,0:T(2,128)(2,1)} %param.7) | copy-start | bytes 4612
  13.1 32.4 %all-to-all-start = ((bf16[8,48,1664]{2,1,0:T(8,128)(2,1)}), bf16[8,48,1664]{2,1,0:T(8,128)(2,1)S(1)}, u32[]{:S(2)}, u32[]{:S(2)}) async-start(bf16[8,48,1664]{2,1,0:T(8,128)(2,1)} %shard_map.69), calls=%async_computation | async-start | bytes 2555904 | tf_op jit(solution)/shard_map/all_to_all | solution.py:220
  26.2 31.8 %copy-start.1 = (bf16[512,1536]{1,0:T(8,128)(2,1)S(1)}, bf16[512,1536]{1,0:T(8,128)(2,1)}, u32[]{:S(2)}) copy-start(bf16[512,1536]{1,0:T(8,128)(2,1)} %grad_ref.3) | copy-start | bytes 4718596
  27.4 29.9 %collective-permute-start.4 = (bf16[256,768]{1,0:T(8,128)(2,1)S(1)}, bf16[256,768]{1,0:T(8,128)(2,1)}, u32[]{:S(2)}, u32[]{:S(2)}) collective-permute-start(bf16[256,768]{1,0:T(8,128)(2,1)S(1)} %fusion.refs_0_), channel_id=1, source_target_pairs={{0,581},{1,580},{2,1},{3,0},{4,3},{5,2},{192,5},{193,4},{194,193},... | collective-permute-start | bytes 1179656 | tf_op jit(solution)/shard_map/ppermute | solution.py:218
  34.0 23.3 %collective-permute-start.3 = (bf16[256,768]{1,0:T(8,128)(2,1)S(1)}, bf16[256,768]{1,0:T(8,128)(2,1)}, u32[]{:S(2)}, u32[]{:S(2)}) collective-permute-start(bf16[256,768]{1,0:T(8,128)(2,1)S(1)} %fusion.refs_0_), channel_id=1, source_target_pairs={{0,3},{1,2},{2,5},{3,4},{4,193},{5,192},{192,195},{193,194},{194,1... | collective-permute-start | bytes 1179656 | tf_op jit(solution)/shard_map/ppermute | solution.py:218
  36.0 21.4 %collective-permute-start.2 = (bf16[256,768]{1,0:T(8,128)(2,1)S(1)}, bf16[256,768]{1,0:T(8,128)(2,1)}, u32[]{:S(2)}, u32[]{:S(2)}) collective-permute-start(bf16[256,768]{1,0:T(8,128)(2,1)S(1)} %fusion.refs_0_), channel_id=1, source_target_pairs={{0,1},{1,0},{2,3},{3,2},{4,5},{5,4},{192,193},{193,192},{194,195},... | collective-permute-start | bytes 1179656 | tf_op jit(solution)/shard_map/ppermute | solution.py:218
  38.8 18.6 %collective-permute-start.1 = (bf16[256,768]{1,0:T(8,128)(2,1)S(1)}, bf16[256,768]{1,0:T(8,128)(2,1)}, u32[]{:S(2)}, u32[]{:S(2)}) collective-permute-start(bf16[256,768]{1,0:T(8,128)(2,1)S(1)} %fusion.refs_0_), channel_id=1, source_target_pairs={{0,580},{1,581},{2,0},{3,1},{4,2},{5,3},{192,4},{193,5},{194,192},... | collective-permute-start | bytes 1179656 | tf_op jit(solution)/shard_map/ppermute | solution.py:218
  43.6 14.4 %collective-permute-start = (bf16[256,768]{1,0:T(8,128)(2,1)S(1)}, bf16[256,768]{1,0:T(8,128)(2,1)}, u32[]{:S(2)}, u32[]{:S(2)}) collective-permute-start(bf16[256,768]{1,0:T(8,128)(2,1)S(1)} %fusion.refs_0_), channel_id=1, source_target_pairs={{0,2},{1,3},{2,4},{3,5},{4,192},{5,193},{192,194},{193,195},{194,1... | collective-permute-start | bytes 1179656 | tf_op jit(solution)/shard_map/ppermute | solution.py:218
  46.6 29.8 %all-to-all-start.1 = ((bf16[48,13,128]{2,1,0:T(8,128)(2,1)}), bf16[48,13,128]{2,1,0:T(8,128)(2,1)S(1)}, u32[]{:S(2)}, u32[]{:S(2)}) async-start(bf16[48,13,128]{2,1,0:T(8,128)(2,1)} %shard_map.70), calls=%async_computation.1 | async-start | bytes 393216 | tf_op jit(solution)/shard_map/all_to_all | solution.py:222

commit v7 on v5

--- a/solution.py
+++ b/solution.py
@@ -172,33 +172,38 @@
     )(far)
 
 
-def ctx_kernel(chips, grad_ref, *refs):
-    held, out_ref = refs[:-1], refs[-1]
+def ctx_kernel(chips, slots, grad_ref, *refs):
+    held, (*before, out_ref) = refs[: len(slots)], refs[len(slots) :]
     chip, core = lax.axis_index("zl"), lax.axis_index("c")
     rows = held[0].shape[0]
-    total = None
-    for slot, block in enumerate(held):
-        owner = lax.rem(chip + chips - slot % chips, chips)
-        side = core if slot < chips else 1 - core
+    total = before[0][...] if before else None
+    for (back, other), block in zip(slots, held):
+        owner = lax.rem(chip + chips - back, chips)
+        side = 1 - core if other else core
         at = pl.multiple_of((2 * owner + side) * rows, rows)
         product = jnp.dot(grad_ref[:, pl.ds(at, rows)], block[...], preferred_element_type=jnp.float32)
         total = product if total is None else total + product
     out_ref[...] = total.astype(out_ref.dtype)
 
 
-def ctx_product(chips, grad_out, held):
+def ctx_product(chips, kind, grad_out, held, *before):
     tokens, depth = grad_out.shape
-    width = held[0].shape[1]
     steps = 2
-    return pl.pallas_call(
-        functools.partial(ctx_kernel, chips),
-        out_shape=jax.ShapeDtypeStruct((tokens, width), jnp.bfloat16),
+
+    def rows(width):
+        return pl.BlockSpec((tokens // steps, width), lambda i: (i, 0))
+
+    blocks = list(held.values())
+    width = blocks[0].shape[1]
+    return pl.pallas_call(
+        functools.partial(ctx_kernel, chips, tuple(held)),
+        out_shape=jax.ShapeDtypeStruct((tokens, width), kind),
         grid=(steps,),
-        in_specs=[pl.BlockSpec((tokens // steps, depth), lambda i: (i, 0))] + [VMEM] * len(held),
-        out_specs=pl.BlockSpec((tokens // steps, width), lambda i: (i, 0)),
+        in_specs=[rows(depth)] + [VMEM] * len(blocks) + [rows(width)] * len(before),
+        out_specs=rows(width),
         compiler_params=parameters(24),
-        cost_estimate=pl.CostEstimate(flops=12 * 10**8, bytes_accessed=5 * 10**6, transcendentals=0),
-    )(grad_out, *held)
+        cost_estimate=pl.CostEstimate(flops=len(blocks) * 2 * 10**8, bytes_accessed=4 * 10**6, transcendentals=0),
+    )(grad_out, *blocks, *before)
 
 
 def body(sizes, grad_out, context, codes, scales):
@@ -210,18 +215,22 @@
     send, keep = local_terms(sizes, grad_out, context)
     got = lax.ppermute(send, "c", swap)
     block = (codes[0].astype(jnp.float32) * scales.astype(jnp.float32)).astype(jnp.bfloat16)
-    held = [block]
+    held = {(0, False): block, (0, True): lax.ppermute(block, "c", swap)}
     for back in range(1, chips):
         hop = back if back <= chips // 2 else back - chips
-        held.append(lax.ppermute(block, ("zh", "zl"), [(i, (i + hop) % ring) for i in range(ring)]))
-    held += [lax.ppermute(piece, "c", swap) for piece in held]
+        moves = [(i, (i + hop) % ring) for i in range(ring)]
+        held[back, False] = lax.ppermute(block, ("zh", "zl"), moves)
 
     near = lax.all_to_all(chip_sum(got, keep), ("x", "yl"), split_axis=0, concat_axis=0, tiled=True)
     near = near_sum(near)
+    _, held = lax.optimization_barrier((near, held))
     far = lax.all_to_all(near, ("zh", "yh", "zl"), split_axis=0, concat_axis=0, tiled=True)
     weight_grad, bias_grad = last_sum(far, 1.0 / count)
 
-    ctx_grad = ctx_product(chips, grad_out, held)
+    part = ctx_product(chips, jnp.float32, grad_out, held)
+    part, held = lax.optimization_barrier((part, held))
+    late = {(back, True): lax.ppermute(held[back, False], "c", swap) for back in range(1, chips)}
+    ctx_grad = ctx_product(chips, jnp.bfloat16, grad_out, late, part)
     return ctx_grad, weight_grad, bias_grad
 
 

time: 80.3 us -> 77.1 us (0.960)
  the two profiles are of different devices: /device:TPU:2 before, /device:TPU:10 now
where the time goes in v7:
time: 77.1 us; the launch traced here: 76.6 us
  starting transfers between devices  43.3 us (56%)
  waiting for transfers between devices  18.1 us (23%)
  Pallas kernels  10.7 us (14%)
  local copies, waits for them, and re-layouts  2.55 us (3%)
  other arithmetic  1.2 us (2%)
    all_to_all x1, starting transfers between devices, body(): lax.all_to_all(chip_sum(got, keep), ('x', 'yl'), split_axis=0, concat_axi...  13 us
    all_to_all x1, starting transfers between devices, body(): lax.all_to_all(near, ('zh', 'yh', 'zl'), split_axis=0, concat_axis=0, til...  12.7 us
    all_to_all x1, waiting for transfers between devices, body(): lax.all_to_all(near, ('zh', 'yh', 'zl'), split_axis=0, concat_axis=0, til...  9.41 us
    ppermute x2, starting transfers between devices, body(): held[back, False] = lax.ppermute(block, ('zh', 'zl'), moves)  9.32 us
    ppermute x2, starting transfers between devices, body(): lax.ppermute(held[back, False], 'c', swap)  4.33 us
    all_to_all x1, waiting for transfers between devices, body(): lax.all_to_all(chip_sum(got, keep), ('x', 'yl'), split_axis=0, concat_axi...  4.21 us
    pallas_call x2, Pallas kernels, ctx_product(): pl.pallas_call(functools.partial(ctx_kernel, chips, tuple(held)), out_sha...  3.93 us
    pallas_call x1, Pallas kernels, local_terms(): pl.pallas_call(functools.partial(term_kernel, sizes), out_shape=(piece, p...  3.37 us
  transfers between devices with their start and end apart: 8, of which 4 were waited for; matrix products, arithmetic and copies ran while one was open for 2% of the time, Pallas kernels for 7%

profile of v7, /device:TPU:10, one launch (start us, length us, event | category | flops | bytes accessed | tf_op | source)
XLA Modules:
  0.0 76.6 jit_solution(16829072541439916517)
XLA Ops:
  0.6 0.0 copy-start
  0.6 1.4 %copy-done = bf16[512,1536]{1,0:T(8,128)(2,1)S(1)} copy-done((bf16[512,1536]{1,0:T(8,128)(2,1)S(1)}, bf16[512,1536]{1,0:T(8,128)(2,1)}, u32[]{:S(2)}) %copy-start) | copy-done | bytes 1572888
  2.0 1.1 %copy-done.2 = bf16[512,768]{1,0:T(8,128)(2,1)S(1)} copy-done((bf16[512,768]{1,0:T(8,128)(2,1)S(1)}, bf16[512,768]{1,0:T(8,128)(2,1)}, u32[]{:S(2)}) %copy-start.2) | copy-done | bytes 786456
  3.2 3.4 %shard_map.67 = (bf16[8,48,1664]{2,1,0:T(8,128)(2,1)S(1)}, bf16[8,48,1664]{2,1,0:T(8,128)(2,1)S(1)}) custom-call(bf16[512,1536]{1,0:T(8,128)(2,1)S(1)} %copy-done, bf16[512,768]{1,0:T(8,128)(2,1)S(1)} %copy-done.2), custom_call_target="tpu_custom_call" | custom-call | flops 4000000000 | bytes 5000000 | tf_op jit(solution)/shard_map/pallas_call | solution.py:91
  6.5 1.9 %collective-permute-start = (bf16[8,48,1664]{2,1,0:T(8,128)(2,1)S(1)}, bf16[8,48,1664]{2,1,0:T(8,128)(2,1)S(1)}, u32[]{:S(2)}, u32[]{:S(2)}) collective-permute-start(bf16[8,48,1664]{2,1,0:T(8,128)(2,1)S(1)} %get-tuple-element.14), channel_id=1, source_target_pairs={{0,1},{1,0},{2,3},{3,2},{4,5},{5,4},{6,7},{7,6},{8,9},{9,8},{10,11... | collective-permute-start | bytes 3833864 | tf_op jit(solution)/shard_map/ppermute | solution.py:216
  8.5 3.0 %collective-permute-done.got_ref = bf16[8,48,1664]{2,1,0:T(8,128)(2,1)S(1)} collective-permute-done((bf16[8,48,1664]{2,1,0:T(8,128)(2,1)S(1)}, bf16[8,48,1664]{2,1,0:T(8,128)(2,1)S(1)}, u32[]{:S(2)}, u32[]{:S(2)}) %collective-permute-start) | collective-permute-done | bytes 1277984 | tf_op jit(solution)/shard_map/ppermute | solution.py:216
  11.4 1.6 %shard_map.68 = bf16[8,48,1664]{2,1,0:T(8,128)(2,1)} custom-call(bf16[8,48,1664]{2,1,0:T(8,128)(2,1)S(1)} %collective-permute-done.got_ref, bf16[8,48,1664]{2,1,0:T(8,128)(2,1)S(1)} %get-tuple-element.15.keep_ref), custom_call_target="tpu_custom_call" | custom-call | flops 1000000 | bytes 4000000 | tf_op jit(solution)/shard_map/pallas_call | solution.py:111
  13.1 13.0 %all-to-all-start = ((bf16[8,48,1664]{2,1,0:T(8,128)(2,1)}), bf16[8,48,1664]{2,1,0:T(8,128)(2,1)S(1)}, u32[]{:S(2)}, u32[]{:S(2)}) async-start(bf16[8,48,1664]{2,1,0:T(8,128)(2,1)} %shard_map.68), calls=%async_computation | async-start | bytes 2555904 | tf_op jit(solution)/shard_map/all_to_all | solution.py:224
  26.1 0.0 copy-start.1
  26.1 1.2 %fusion.refs_0_ = bf16[256,768]{1,0:T(8,128)(2,1)S(1)} fusion(bf16[1,256,768]{2,1,0:T(8,128)(2,1)} %param.6, f32[768]{0:T(1024)S(1)} %convert_reduce_fusion), kind=kLoop, calls=%fused_computation.1 | loop fusion | flops 589824 | bytes 789504 | tf_op jit(solution)/shard_map/convert_element_type | solution.py:217
  27.3 1.9 %collective-permute-start.1 = (bf16[256,768]{1,0:T(8,128)(2,1)S(1)}, bf16[256,768]{1,0:T(8,128)(2,1)}, u32[]{:S(2)}, u32[]{:S(2)}) collective-permute-start(bf16[256,768]{1,0:T(8,128)(2,1)S(1)} %fusion.refs_0_), channel_id=1, source_target_pairs={{0,1},{1,0},{2,3},{3,2},{4,5},{5,4},{6,7},{7,6},{8,9},{9,8},{10,11... | collective-permute-start | bytes 1179656 | tf_op jit(solution)/shard_map/ppermute | solution.py:218
  29.3 1.9 %collective-permute-start.2 = (bf16[256,768]{1,0:T(8,128)(2,1)S(1)}, bf16[256,768]{1,0:T(8,128)(2,1)}, u32[]{:S(2)}, u32[]{:S(2)}) collective-permute-start(bf16[256,768]{1,0:T(8,128)(2,1)S(1)} %fusion.refs_0_), channel_id=1, source_target_pairs={{0,2},{2,4},{4,192},{192,194},{194,196},{196,384},{384,386},{386,3... | collective-permute-start | bytes 1179656 | tf_op jit(solution)/shard_map/ppermute | solution.py:222
  31.2 7.4 %collective-permute-start.3 = (bf16[256,768]{1,0:T(8,128)(2,1)S(1)}, bf16[256,768]{1,0:T(8,128)(2,1)}, u32[]{:S(2)}, u32[]{:S(2)}) collective-permute-start(bf16[256,768]{1,0:T(8,128)(2,1)S(1)} %fusion.refs_0_), channel_id=1, source_target_pairs={{0,580},{2,0},{4,2},{192,4},{194,192},{196,194},{384,196},{386,384... | collective-permute-start | bytes 1179656 | tf_op jit(solution)/shard_map/ppermute | solution.py:222
  38.6 4.2 %all-to-all-done.got_ref = bf16[8,48,1664]{2,1,0:T(8,128)(2,1)S(1)} async-done(((bf16[8,48,1664]{2,1,0:T(8,128)(2,1)}), bf16[8,48,1664]{2,1,0:T(8,128)(2,1)S(1)}, u32[]{:S(2)}, u32[]{:S(2)}) %all-to-all-start) | async-done | bytes 1277984 | tf_op jit(solution)/shard_map/all_to_all | solution.py:224
  42.8 1.1 %shard_map.69 = bf16[48,13,128]{2,1,0:T(8,128)(2,1)} custom-call(bf16[8,48,1664]{2,1,0:T(8,128)(2,1)S(1)} %all-to-all-done.got_ref), custom_call_target="tpu_custom_call" | custom-call | flops 1000000 | bytes 2000000 | tf_op jit(solution)/shard_map/pallas_call | solution.py:136
  43.9 12.7 %all-to-all-start.1 = ((bf16[48,13,128]{2,1,0:T(8,128)(2,1)}), bf16[48,13,128]{2,1,0:T(8,128)(2,1)S(1)}, u32[]{:S(2)}, u32[]{:S(2)}) async-start(bf16[48,13,128]{2,1,0:T(8,128)(2,1)} %shard_map.69), calls=%async_computation.1 | async-start | bytes 393216 | tf_op jit(solution)/shard_map/all_to_all | solution.py:227
  56.6 0.0 collective-permute-done.2.refs_2_
  56.7 2.4 %shard_map.70.refs_2_ = f32[512,768]{1,0:T(8,128)S(1)} custom-call(bf16[512,1536]{1,0:T(8,128)(2,1)S(1)} %copy-done.1, bf16[256,768]{1,0:T(8,128)(2,1)S(1)} %fusion.refs_0_, bf16[256,768]{1,0:T(8,128)(2,1)} %collective-permute-done.1.refs_1_, bf16[256,768]{1,0:T(8,128)(2,1)} %collective-permute-done.2.refs_2_, bf16[256,768]{1,0:T(8,128)(2,1)} %collective-permute-done.3.refs_3_), custom_call_target="tpu_custom_call" | custom-call | flops 800000000 | bytes 4000000 | tf_op jit(solution)/shard_map/pallas_call | solution.py:198
  59.1 1.9 %collective-permute-start.4 = (bf16[256,768]{1,0:T(8,128)(2,1)}, bf16[256,768]{1,0:T(8,128)(2,1)S(1)}, u32[]{:S(2)}, u32[]{:S(2)}) collective-permute-start(bf16[256,768]{1,0:T(8,128)(2,1)} %collective-permute-done.2.refs_2_), channel_id=1, source_target_pairs={{0,1},{1,0},{2,3},{3,2},{4,5},{5,4},{6,7},{7,6},{8,9},{9,8},{10,11... | collective-permute-start | bytes 1179656 | tf_op jit(solution)/shard_map/ppermute | solution.py:232
  61.0 2.4 %collective-permute-start.5 = (bf16[256,768]{1,0:T(8,128)(2,1)}, bf16[256,768]{1,0:T(8,128)(2,1)S(1)}, u32[]{:S(2)}, u32[]{:S(2)}) collective-permute-start(bf16[256,768]{1,0:T(8,128)(2,1)} %collective-permute-done.3.refs_3_), channel_id=1, source_target_pairs={{0,1},{1,0},{2,3},{3,2},{4,5},{5,4},{6,7},{7,6},{8,9},{9,8},{10,11... | collective-permute-start | bytes 1179656 | tf_op jit(solution)/shard_map/ppermute | solution.py:232
  63.4 1.5 %collective-permute-done.5.refs_1_ = bf16[256,768]{1,0:T(8,128)(2,1)S(1)} collective-permute-done((bf16[256,768]{1,0:T(8,128)(2,1)}, bf16[256,768]{1,0:T(8,128)(2,1)S(1)}, u32[]{:S(2)}, u32[]{:S(2)}) %collective-permute-start.5) | collective-permute-done | bytes 393248 | tf_op jit(solution)/shard_map/ppermute | solution.py:232
  65.0 1.5 %shard_map.71 = bf16[512,768]{1,0:T(8,128)(2,1)} custom-call(bf16[512,1536]{1,0:T(8,128)(2,1)S(1)} %copy-done.1, bf16[256,768]{1,0:T(8,128)(2,1)S(1)} %collective-permute-done.4.refs_0_, bf16[256,768]{1,0:T(8,128)(2,1)S(1)} %collective-permute-done.5.refs_1_, f32[512,768]{1,0:T(8,128)S(1)} %shard_map.70.refs_2_), custom_call_target="tpu_custom_call" | custom-call | flops 400000000 | bytes 4000000 | tf_op jit(solution)/shard_map/pallas_call | solution.py:198
  66.5 9.4 %all-to-all-done.1.far_ref = bf16[48,13,128]{2,1,0:T(8,128)(2,1)S(1)} async-done(((bf16[48,13,128]{2,1,0:T(8,128)(2,1)}), bf16[48,13,128]{2,1,0:T(8,128)(2,1)S(1)}, u32[]{:S(2)}, u32[]{:S(2)}) %all-to-all-start.1) | async-done | bytes 159776 | tf_op jit(solution)/shard_map/all_to_all | solution.py:227
  75.9 0.7 shard_map.72
  (8 shorter events, 0.0 us)
Async XLA Ops:
  0.6 1.4 %copy-start = (bf16[512,1536]{1,0:T(8,128)(2,1)S(1)}, bf16[512,1536]{1,0:T(8,128)(2,1)}, u32[]{:S(2)}) copy-start(bf16[512,1536]{1,0:T(8,128)(2,1)} %grad_ref.5) | copy-start | bytes 4718596
  2.0 1.1 %copy-start.2 = (bf16[512,768]{1,0:T(8,128)(2,1)S(1)}, bf16[512,768]{1,0:T(8,128)(2,1)}, u32[]{:S(2)}) copy-start(bf16[512,768]{1,0:T(8,128)(2,1)} %ctx_ref.1) | copy-start | bytes 2359300
  6.5 4.9 %collective-permute-start = (bf16[8,48,1664]{2,1,0:T(8,128)(2,1)S(1)}, bf16[8,48,1664]{2,1,0:T(8,128)(2,1)S(1)}, u32[]{:S(2)}, u32[]{:S(2)}) collective-permute-start(bf16[8,48,1664]{2,1,0:T(8,128)(2,1)S(1)} %get-tuple-element.14), channel_id=1, source_target_pairs={{0,1},{1,0},{2,3},{3,2},{4,5},{5,4},{6,7},{7,6},{8,9},{9,8},{10,11... | collective-permute-start | bytes 3833864 | tf_op jit(solution)/shard_map/ppermute | solution.py:216
  13.1 13.1 %copy-start.3 = (bf16[1,768]{1,0:T(2,128)(2,1)S(1)}, bf16[1,768]{1,0:T(2,128)(2,1)}, u32[]{:S(2)}) copy-start(bf16[1,768]{1,0:T(2,128)(2,1)} %param.7) | copy-start | bytes 4612
  13.1 29.7 %all-to-all-start = ((bf16[8,48,1664]{2,1,0:T(8,128)(2,1)}), bf16[8,48,1664]{2,1,0:T(8,128)(2,1)S(1)}, u32[]{:S(2)}, u32[]{:S(2)}) async-start(bf16[8,48,1664]{2,1,0:T(8,128)(2,1)} %shard_map.68), calls=%async_computation | async-start | bytes 2555904 | tf_op jit(solution)/shard_map/all_to_all | solution.py:224
  26.1 30.5 %copy-start.1 = (bf16[512,1536]{1,0:T(8,128)(2,1)S(1)}, bf16[512,1536]{1,0:T(8,128)(2,1)}, u32[]{:S(2)}) copy-start(bf16[512,1536]{1,0:T(8,128)(2,1)} %grad_ref.5) | copy-start | bytes 4718596
  27.3 29.3 %collective-permute-start.1 = (bf16[256,768]{1,0:T(8,128)(2,1)S(1)}, bf16[256,768]{1,0:T(8,128)(2,1)}, u32[]{:S(2)}, u32[]{:S(2)}) collective-permute-start(bf16[256,768]{1,0:T(8,128)(2,1)S(1)} %fusion.refs_0_), channel_id=1, source_target_pairs={{0,1},{1,0},{2,3},{3,2},{4,5},{5,4},{6,7},{7,6},{8,9},{9,8},{10,11... | collective-permute-start | bytes 1179656 | tf_op jit(solution)/shard_map/ppermute | solution.py:218
  29.3 27.4 %collective-permute-start.2 = (bf16[256,768]{1,0:T(8,128)(2,1)S(1)}, bf16[256,768]{1,0:T(8,128)(2,1)}, u32[]{:S(2)}, u32[]{:S(2)}) collective-permute-start(bf16[256,768]{1,0:T(8,128)(2,1)S(1)} %fusion.refs_0_), channel_id=1, source_target_pairs={{0,2},{2,4},{4,192},{192,194},{194,196},{196,384},{384,386},{386,3... | collective-permute-start | bytes 1179656 | tf_op jit(solution)/shard_map/ppermute | solution.py:222
  31.2 25.4 %collective-permute-start.3 = (bf16[256,768]{1,0:T(8,128)(2,1)S(1)}, bf16[256,768]{1,0:T(8,128)(2,1)}, u32[]{:S(2)}, u32[]{:S(2)}) collective-permute-start(bf16[256,768]{1,0:T(8,128)(2,1)S(1)} %fusion.refs_0_), channel_id=1, source_target_pairs={{0,580},{2,0},{4,2},{192,4},{194,192},{196,194},{384,196},{386,384... | collective-permute-start | bytes 1179656 | tf_op jit(solution)/shard_map/ppermute | solution.py:222
  43.9 32.0 %all-to-all-start.1 = ((bf16[48,13,128]{2,1,0:T(8,128)(2,1)}), bf16[48,13,128]{2,1,0:T(8,128)(2,1)S(1)}, u32[]{:S(2)}, u32[]{:S(2)}) async-start(bf16[48,13,128]{2,1,0:T(8,128)(2,1)} %shard_map.69), calls=%async_computation.1 | async-start | bytes 393216 | tf_op jit(solution)/shard_map/all_to_all | solution.py:227
  59.1 4.3 %collective-permute-start.4 = (bf16[256,768]{1,0:T(8,128)(2,1)}, bf16[256,768]{1,0:T(8,128)(2,1)S(1)}, u32[]{:S(2)}, u32[]{:S(2)}) collective-permute-start(bf16[256,768]{1,0:T(8,128)(2,1)} %collective-permute-done.2.refs_2_), channel_id=1, source_target_pairs={{0,1},{1,0},{2,3},{3,2},{4,5},{5,4},{6,7},{7,6},{8,9},{9,8},{10,11... | collective-permute-start | bytes 1179656 | tf_op jit(solution)/shard_map/ppermute | solution.py:232
  61.0 4.0 %collective-permute-start.5 = (bf16[256,768]{1,0:T(8,128)(2,1)}, bf16[256,768]{1,0:T(8,128)(2,1)S(1)}, u32[]{:S(2)}, u32[]{:S(2)}) collective-permute-start(bf16[256,768]{1,0:T(8,128)(2,1)} %collective-permute-done.3.refs_3_), channel_id=1, source_target_pairs={{0,1},{1,0},{2,3},{3,2},{4,5},{5,4},{6,7},{7,6},{8,9},{9,8},{10,11... | collective-permute-start | bytes 1179656 | tf_op jit(solution)/shard_map/ppermute | solution.py:232

commit v8 on v7

--- a/solution.py
+++ b/solution.py
@@ -119,12 +119,14 @@
 
 
 def near_kernel(got_ref, sum_ref, wide):
-    for chunk in range(sum_ref.shape[1]):
+    chunks = got_ref.shape[2] // PAD
+    wide[:, chunks:, :] = jnp.zeros((wide.shape[0], wide.shape[1] - chunks, PAD), jnp.float32)
+    for chunk in range(chunks):
         lanes = slice(chunk * PAD, (chunk + 1) * PAD)
         total = got_ref[0, :, lanes].astype(jnp.float32)
         for index in range(1, got_ref.shape[0]):
             total = total + got_ref[index, :, lanes].astype(jnp.float32)
-        if chunk == sum_ref.shape[1] - 1:
+        if chunk == chunks - 1:
             total = split_pairs(join_pairs(total))
         wide[:, chunk, :] = total
     sum_ref[...] = wide[...].astype(sum_ref.dtype)
@@ -132,7 +134,7 @@
 
 def near_sum(got):
     _, rows, lanes = got.shape
-    shape = (rows, lanes // PAD, PAD)
+    shape = (rows, (lanes // PAD + 15) // 16 * 16, PAD)
     return pl.pallas_call(
         near_kernel,
         out_shape=jax.ShapeDtypeStruct(shape, jnp.bfloat16),
@@ -149,7 +151,7 @@
     for index in range(1, far_ref.shape[0]):
         total = total + far_ref[index].astype(jnp.float32)
     total = total * scale
-    chunks = (total.shape[0] - 1) // 2
+    chunks = weight_ref.shape[1] // PAD
     for s in range(2):
         for chunk in range(chunks):
             at = s * chunks + chunk
@@ -160,8 +162,7 @@
         bias_ref[s] = jnp.sum(jnp.where((lane == 2 * s) | (lane == 2 * s + 1), tail, 0.0))
 
 
-def last_sum(far, scale):
-    width = (far.shape[1] - 1) // 2 * PAD
+def last_sum(far, width, scale):
     return pl.pallas_call(
         functools.partial(last_kernel, scale),
         out_shape=(jax.ShapeDtypeStruct((2, width), jnp.float32), jax.ShapeDtypeStruct((2,), jnp.float32)),
@@ -225,7 +226,7 @@
     near = near_sum(near)
     _, held = lax.optimization_barrier((near, held))
     far = lax.all_to_all(near, ("zh", "yh", "zl"), split_axis=0, concat_axis=0, tiled=True)
-    weight_grad, bias_grad = last_sum(far, 1.0 / count)
+    weight_grad, bias_grad = last_sum(far, context.shape[1], 1.0 / count)
 
     part = ctx_product(chips, jnp.float32, grad_out, held)
     part, held = lax.optimization_barrier((part, held))

time: 77.1 us -> 77.1 us (level)
  no operation moved by 1% of the time
where the time goes in v8:
time: 77.1 us; the launch traced here: 76.5 us
  starting transfers between devices  43.3 us (56%)
  waiting for transfers between devices  18.1 us (23%)
  Pallas kernels  10.7 us (14%)
  local copies, waits for them, and re-layouts  2.55 us (3%)
  other arithmetic  1.2 us (2%)
    all_to_all x1, starting transfers between devices, body(): lax.all_to_all(chip_sum(got, keep), ('x', 'yl'), split_axis=0, concat_axi...  13 us
    all_to_all x1, starting transfers between devices, body(): lax.all_to_all(near, ('zh', 'yh', 'zl'), split_axis=0, concat_axis=0, til...  12.7 us
    all_to_all x1, waiting for transfers between devices, body(): lax.all_to_all(near, ('zh', 'yh', 'zl'), split_axis=0, concat_axis=0, til...  9.41 us
    ppermute x2, starting transfers between devices, body(): held[back, False] = lax.ppermute(block, ('zh', 'zl'), moves)  9.32 us
    ppermute x2, starting transfers between devices, body(): lax.ppermute(held[back, False], 'c', swap)  4.33 us
    all_to_all x1, waiting for transfers between devices, body(): lax.all_to_all(chip_sum(got, keep), ('x', 'yl'), split_axis=0, concat_axi...  4.21 us
    pallas_call x2, Pallas kernels, ctx_product(): pl.pallas_call(functools.partial(ctx_kernel, chips, tuple(held)), out_sha...  3.93 us
    pallas_call x1, Pallas kernels, local_terms(): pl.pallas_call(functools.partial(term_kernel, sizes), out_shape=(piece, p...  3.37 us
  transfers between devices with their start and end apart: 8, of which 4 were waited for; matrix products, arithmetic and copies ran while one was open for 2% of the time, Pallas kernels for 7%

profile of v8, /device:TPU:10, one launch (start us, length us, event | category | flops | bytes accessed | tf_op | source)
XLA Modules:
  0.0 76.5 jit_solution(7887883756550828790)
XLA Ops:
  0.6 0.0 copy-start
  0.6 1.4 %copy-done = bf16[512,1536]{1,0:T(8,128)(2,1)S(1)} copy-done((bf16[512,1536]{1,0:T(8,128)(2,1)S(1)}, bf16[512,1536]{1,0:T(8,128)(2,1)}, u32[]{:S(2)}) %copy-start) | copy-done | bytes 1572888
  2.0 1.1 %copy-done.2 = bf16[512,768]{1,0:T(8,128)(2,1)S(1)} copy-done((bf16[512,768]{1,0:T(8,128)(2,1)S(1)}, bf16[512,768]{1,0:T(8,128)(2,1)}, u32[]{:S(2)}) %copy-start.2) | copy-done | bytes 786456
  3.2 3.4 %shard_map.67 = (bf16[8,48,1664]{2,1,0:T(8,128)(2,1)S(1)}, bf16[8,48,1664]{2,1,0:T(8,128)(2,1)S(1)}) custom-call(bf16[512,1536]{1,0:T(8,128)(2,1)S(1)} %copy-done, bf16[512,768]{1,0:T(8,128)(2,1)S(1)} %copy-done.2), custom_call_target="tpu_custom_call" | custom-call | flops 4000000000 | bytes 5000000 | tf_op jit(solution)/shard_map/pallas_call | solution.py:91
  6.5 1.9 %collective-permute-start = (bf16[8,48,1664]{2,1,0:T(8,128)(2,1)S(1)}, bf16[8,48,1664]{2,1,0:T(8,128)(2,1)S(1)}, u32[]{:S(2)}, u32[]{:S(2)}) collective-permute-start(bf16[8,48,1664]{2,1,0:T(8,128)(2,1)S(1)} %get-tuple-element.14), channel_id=1, source_target_pairs={{0,1},{1,0},{2,3},{3,2},{4,5},{5,4},{6,7},{7,6},{8,9},{9,8},{10,11... | collective-permute-start | bytes 3833864 | tf_op jit(solution)/shard_map/ppermute | solution.py:217
  8.5 3.0 %collective-permute-done.got_ref = bf16[8,48,1664]{2,1,0:T(8,128)(2,1)S(1)} collective-permute-done((bf16[8,48,1664]{2,1,0:T(8,128)(2,1)S(1)}, bf16[8,48,1664]{2,1,0:T(8,128)(2,1)S(1)}, u32[]{:S(2)}, u32[]{:S(2)}) %collective-permute-start) | collective-permute-done | bytes 1277984 | tf_op jit(solution)/shard_map/ppermute | solution.py:217
  11.4 1.6 %shard_map.68 = bf16[8,48,1664]{2,1,0:T(8,128)(2,1)} custom-call(bf16[8,48,1664]{2,1,0:T(8,128)(2,1)S(1)} %collective-permute-done.got_ref, bf16[8,48,1664]{2,1,0:T(8,128)(2,1)S(1)} %get-tuple-element.15.keep_ref), custom_call_target="tpu_custom_call" | custom-call | flops 1000000 | bytes 4000000 | tf_op jit(solution)/shard_map/pallas_call | solution.py:111
  13.1 13.0 %all-to-all-start = ((bf16[8,48,1664]{2,1,0:T(8,128)(2,1)}), bf16[8,48,1664]{2,1,0:T(8,128)(2,1)S(1)}, u32[]{:S(2)}, u32[]{:S(2)}) async-start(bf16[8,48,1664]{2,1,0:T(8,128)(2,1)} %shard_map.68), calls=%async_computation | async-start | bytes 2555904 | tf_op jit(solution)/shard_map/all_to_all | solution.py:225
  26.1 0.0 copy-start.1
  26.1 1.2 %fusion.refs_0_ = bf16[256,768]{1,0:T(8,128)(2,1)S(1)} fusion(bf16[1,256,768]{2,1,0:T(8,128)(2,1)} %param.6, f32[768]{0:T(1024)S(1)} %convert_reduce_fusion), kind=kLoop, calls=%fused_computation.1 | loop fusion | flops 589824 | bytes 789504 | tf_op jit(solution)/shard_map/convert_element_type | solution.py:218
  27.3 1.9 %collective-permute-start.1 = (bf16[256,768]{1,0:T(8,128)(2,1)S(1)}, bf16[256,768]{1,0:T(8,128)(2,1)}, u32[]{:S(2)}, u32[]{:S(2)}) collective-permute-start(bf16[256,768]{1,0:T(8,128)(2,1)S(1)} %fusion.refs_0_), channel_id=1, source_target_pairs={{0,1},{1,0},{2,3},{3,2},{4,5},{5,4},{6,7},{7,6},{8,9},{9,8},{10,11... | collective-permute-start | bytes 1179656 | tf_op jit(solution)/shard_map/ppermute | solution.py:219
  29.3 1.9 %collective-permute-start.2 = (bf16[256,768]{1,0:T(8,128)(2,1)S(1)}, bf16[256,768]{1,0:T(8,128)(2,1)}, u32[]{:S(2)}, u32[]{:S(2)}) collective-permute-start(bf16[256,768]{1,0:T(8,128)(2,1)S(1)} %fusion.refs_0_), channel_id=1, source_target_pairs={{0,2},{2,4},{4,192},{192,194},{194,196},{196,384},{384,386},{386,3... | collective-permute-start | bytes 1179656 | tf_op jit(solution)/shard_map/ppermute | solution.py:223
  31.2 7.4 %collective-permute-start.3 = (bf16[256,768]{1,0:T(8,128)(2,1)S(1)}, bf16[256,768]{1,0:T(8,128)(2,1)}, u32[]{:S(2)}, u32[]{:S(2)}) collective-permute-start(bf16[256,768]{1,0:T(8,128)(2,1)S(1)} %fusion.refs_0_), channel_id=1, source_target_pairs={{0,580},{2,0},{4,2},{192,4},{194,192},{196,194},{384,196},{386,384... | collective-permute-start | bytes 1179656 | tf_op jit(solution)/shard_map/ppermute | solution.py:223
  38.6 4.2 %all-to-all-done.got_ref = bf16[8,48,1664]{2,1,0:T(8,128)(2,1)S(1)} async-done(((bf16[8,48,1664]{2,1,0:T(8,128)(2,1)}), bf16[8,48,1664]{2,1,0:T(8,128)(2,1)S(1)}, u32[]{:S(2)}, u32[]{:S(2)}) %all-to-all-start) | async-done | bytes 1277984 | tf_op jit(solution)/shard_map/all_to_all | solution.py:225
  42.8 1.1 %shard_map.69 = bf16[48,16,128]{2,1,0:T(8,128)(2,1)} custom-call(bf16[8,48,1664]{2,1,0:T(8,128)(2,1)S(1)} %all-to-all-done.got_ref), custom_call_target="tpu_custom_call" | custom-call | flops 1000000 | bytes 2000000 | tf_op jit(solution)/shard_map/pallas_call | solution.py:138
  43.9 12.7 %all-to-all-start.1 = ((bf16[48,16,128]{2,1,0:T(8,128)(2,1)}), bf16[48,16,128]{2,1,0:T(8,128)(2,1)S(1)}, u32[]{:S(2)}, u32[]{:S(2)}) async-start(bf16[48,16,128]{2,1,0:T(8,128)(2,1)} %shard_map.69), calls=%async_computation.1 | async-start | bytes 393216 | tf_op jit(solution)/shard_map/all_to_all | solution.py:228
  56.6 0.0 collective-permute-done.1.refs_1_
  56.6 2.4 %shard_map.70.refs_2_ = f32[512,768]{1,0:T(8,128)S(1)} custom-call(bf16[512,1536]{1,0:T(8,128)(2,1)S(1)} %copy-done.1, bf16[256,768]{1,0:T(8,128)(2,1)S(1)} %fusion.refs_0_, bf16[256,768]{1,0:T(8,128)(2,1)} %collective-permute-done.1.refs_1_, bf16[256,768]{1,0:T(8,128)(2,1)} %collective-permute-done.2.refs_2_, bf16[256,768]{1,0:T(8,128)(2,1)} %collective-permute-done.3.refs_3_), custom_call_target="tpu_custom_call" | custom-call | flops 800000000 | bytes 4000000 | tf_op jit(solution)/shard_map/pallas_call | solution.py:199
  59.1 1.9 %collective-permute-start.4 = (bf16[256,768]{1,0:T(8,128)(2,1)}, bf16[256,768]{1,0:T(8,128)(2,1)S(1)}, u32[]{:S(2)}, u32[]{:S(2)}) collective-permute-start(bf16[256,768]{1,0:T(8,128)(2,1)} %collective-permute-done.2.refs_2_), channel_id=1, source_target_pairs={{0,1},{1,0},{2,3},{3,2},{4,5},{5,4},{6,7},{7,6},{8,9},{9,8},{10,11... | collective-permute-start | bytes 1179656 | tf_op jit(solution)/shard_map/ppermute | solution.py:233
  61.0 2.4 %collective-permute-start.5 = (bf16[256,768]{1,0:T(8,128)(2,1)}, bf16[256,768]{1,0:T(8,128)(2,1)S(1)}, u32[]{:S(2)}, u32[]{:S(2)}) collective-permute-start(bf16[256,768]{1,0:T(8,128)(2,1)} %collective-permute-done.3.refs_3_), channel_id=1, source_target_pairs={{0,1},{1,0},{2,3},{3,2},{4,5},{5,4},{6,7},{7,6},{8,9},{9,8},{10,11... | collective-permute-start | bytes 1179656 | tf_op jit(solution)/shard_map/ppermute | solution.py:233
  63.4 1.5 %collective-permute-done.5.refs_1_ = bf16[256,768]{1,0:T(8,128)(2,1)S(1)} collective-permute-done((bf16[256,768]{1,0:T(8,128)(2,1)}, bf16[256,768]{1,0:T(8,128)(2,1)S(1)}, u32[]{:S(2)}, u32[]{:S(2)}) %collective-permute-start.5) | collective-permute-done | bytes 393248 | tf_op jit(solution)/shard_map/ppermute | solution.py:233
  64.9 1.5 %shard_map.71 = bf16[512,768]{1,0:T(8,128)(2,1)} custom-call(bf16[512,1536]{1,0:T(8,128)(2,1)S(1)} %copy-done.1, bf16[256,768]{1,0:T(8,128)(2,1)S(1)} %collective-permute-done.4.refs_0_, bf16[256,768]{1,0:T(8,128)(2,1)S(1)} %collective-permute-done.5.refs_1_, f32[512,768]{1,0:T(8,128)S(1)} %shard_map.70.refs_2_), custom_call_target="tpu_custom_call" | custom-call | flops 400000000 | bytes 4000000 | tf_op jit(solution)/shard_map/pallas_call | solution.py:199
  66.4 9.4 %all-to-all-done.1.far_ref = bf16[48,16,128]{2,1,0:T(8,128)(2,1)S(1)} async-done(((bf16[48,16,128]{2,1,0:T(8,128)(2,1)}), bf16[48,16,128]{2,1,0:T(8,128)(2,1)S(1)}, u32[]{:S(2)}, u32[]{:S(2)}) %all-to-all-start.1) | async-done | bytes 196640 | tf_op jit(solution)/shard_map/all_to_all | solution.py:228
  75.9 0.7 shard_map.72
  (8 shorter events, 0.0 us)
Async XLA Ops:
  0.6 1.4 %copy-start = (bf16[512,1536]{1,0:T(8,128)(2,1)S(1)}, bf16[512,1536]{1,0:T(8,128)(2,1)}, u32[]{:S(2)}) copy-start(bf16[512,1536]{1,0:T(8,128)(2,1)} %grad_ref.5) | copy-start | bytes 4718596
  2.0 1.1 %copy-start.2 = (bf16[512,768]{1,0:T(8,128)(2,1)S(1)}, bf16[512,768]{1,0:T(8,128)(2,1)}, u32[]{:S(2)}) copy-start(bf16[512,768]{1,0:T(8,128)(2,1)} %ctx_ref.1) | copy-start | bytes 2359300
  6.5 4.9 %collective-permute-start = (bf16[8,48,1664]{2,1,0:T(8,128)(2,1)S(1)}, bf16[8,48,1664]{2,1,0:T(8,128)(2,1)S(1)}, u32[]{:S(2)}, u32[]{:S(2)}) collective-permute-start(bf16[8,48,1664]{2,1,0:T(8,128)(2,1)S(1)} %get-tuple-element.14), channel_id=1, source_target_pairs={{0,1},{1,0},{2,3},{3,2},{4,5},{5,4},{6,7},{7,6},{8,9},{9,8},{10,11... | collective-permute-start | bytes 3833864 | tf_op jit(solution)/shard_map/ppermute | solution.py:217
  13.1 13.1 %copy-start.3 = (bf16[1,768]{1,0:T(2,128)(2,1)S(1)}, bf16[1,768]{1,0:T(2,128)(2,1)}, u32[]{:S(2)}) copy-start(bf16[1,768]{1,0:T(2,128)(2,1)} %param.7) | copy-start | bytes 4612
  13.1 29.7 %all-to-all-start = ((bf16[8,48,1664]{2,1,0:T(8,128)(2,1)}), bf16[8,48,1664]{2,1,0:T(8,128)(2,1)S(1)}, u32[]{:S(2)}, u32[]{:S(2)}) async-start(bf16[8,48,1664]{2,1,0:T(8,128)(2,1)} %shard_map.68), calls=%async_computation | async-start | bytes 2555904 | tf_op jit(solution)/shard_map/all_to_all | solution.py:225
  26.1 30.5 %copy-start.1 = (bf16[512,1536]{1,0:T(8,128)(2,1)S(1)}, bf16[512,1536]{1,0:T(8,128)(2,1)}, u32[]{:S(2)}) copy-start(bf16[512,1536]{1,0:T(8,128)(2,1)} %grad_ref.5) | copy-start | bytes 4718596
  27.3 29.3 %collective-permute-start.1 = (bf16[256,768]{1,0:T(8,128)(2,1)S(1)}, bf16[256,768]{1,0:T(8,128)(2,1)}, u32[]{:S(2)}, u32[]{:S(2)}) collective-permute-start(bf16[256,768]{1,0:T(8,128)(2,1)S(1)} %fusion.refs_0_), channel_id=1, source_target_pairs={{0,1},{1,0},{2,3},{3,2},{4,5},{5,4},{6,7},{7,6},{8,9},{9,8},{10,11... | collective-permute-start | bytes 1179656 | tf_op jit(solution)/shard_map/ppermute | solution.py:219
  29.3 27.3 %collective-permute-start.2 = (bf16[256,768]{1,0:T(8,128)(2,1)S(1)}, bf16[256,768]{1,0:T(8,128)(2,1)}, u32[]{:S(2)}, u32[]{:S(2)}) collective-permute-start(bf16[256,768]{1,0:T(8,128)(2,1)S(1)} %fusion.refs_0_), channel_id=1, source_target_pairs={{0,2},{2,4},{4,192},{192,194},{194,196},{196,384},{384,386},{386,3... | collective-permute-start | bytes 1179656 | tf_op jit(solution)/shard_map/ppermute | solution.py:223
  31.2 25.4 %collective-permute-start.3 = (bf16[256,768]{1,0:T(8,128)(2,1)S(1)}, bf16[256,768]{1,0:T(8,128)(2,1)}, u32[]{:S(2)}, u32[]{:S(2)}) collective-permute-start(bf16[256,768]{1,0:T(8,128)(2,1)S(1)} %fusion.refs_0_), channel_id=1, source_target_pairs={{0,580},{2,0},{4,2},{192,4},{194,192},{196,194},{384,196},{386,384... | collective-permute-start | bytes 1179656 | tf_op jit(solution)/shard_map/ppermute | solution.py:223
  43.9 32.0 %all-to-all-start.1 = ((bf16[48,16,128]{2,1,0:T(8,128)(2,1)}), bf16[48,16,128]{2,1,0:T(8,128)(2,1)S(1)}, u32[]{:S(2)}, u32[]{:S(2)}) async-start(bf16[48,16,128]{2,1,0:T(8,128)(2,1)} %shard_map.69), calls=%async_computation.1 | async-start | bytes 393216 | tf_op jit(solution)/shard_map/all_to_all | solution.py:228
  59.1 4.3 %collective-permute-start.4 = (bf16[256,768]{1,0:T(8,128)(2,1)}, bf16[256,768]{1,0:T(8,128)(2,1)S(1)}, u32[]{:S(2)}, u32[]{:S(2)}) collective-permute-start(bf16[256,768]{1,0:T(8,128)(2,1)} %collective-permute-done.2.refs_2_), channel_id=1, source_target_pairs={{0,1},{1,0},{2,3},{3,2},{4,5},{5,4},{6,7},{7,6},{8,9},{9,8},{10,11... | collective-permute-start | bytes 1179656 | tf_op jit(solution)/shard_map/ppermute | solution.py:233
  61.0 4.0 %collective-permute-start.5 = (bf16[256,768]{1,0:T(8,128)(2,1)}, bf16[256,768]{1,0:T(8,128)(2,1)S(1)}, u32[]{:S(2)}, u32[]{:S(2)}) collective-permute-start(bf16[256,768]{1,0:T(8,128)(2,1)} %collective-permute-done.3.refs_3_), channel_id=1, source_target_pairs={{0,1},{1,0},{2,3},{3,2},{4,5},{5,4},{6,7},{7,6},{8,9},{9,8},{10,11... | collective-permute-start | bytes 1179656 | tf_op jit(solution)/shard_map/ppermute | solution.py:233
